TPU v7x, 128 devices: a whole 4x4x4 slice. The times are simulated.
128 devices in a mesh: dp: 8 (over y_hi, z), fsdp: 16 (over y_lo, x, core).
Axes of the slice: x: 4, y: 4 (y_hi: 2, y_lo: 2; y = y_hi * 2 + y_lo), z: 4, core: 2. Of those that a mesh axis runs over, the one named last changes fastest.
Arguments:
- rollout_rows: bfloat16 [1024, 32, 8192], P(('dp', 'fsdp')), may hold values from -6 to 6
- rewards: float32 [1024], P(('dp', 'fsdp')), may hold values from -5 to 5
- group_ids: int32 [1024], P(('dp', 'fsdp')), may hold values from 0 to 63
- lengths: int32 [1024], P(('dp', 'fsdp')), may hold values from 1 to 32, 28672 in all
- packing: int32 [1024], P(('dp', 'fsdp')), may hold values from 0 to 1023, as said below
- queries: bfloat16 [32768, 4096], P(('dp', 'fsdp'))
- keys: bfloat16 [32768, 512], P(('dp', 'fsdp')), may hold values from -6 to 6
- out_grad: bfloat16 [32768, 4096], P(('dp', 'fsdp')), may hold values from -6 to 6
- value_weight: bfloat16 [8192, 512], P('fsdp'), may hold values from -0.0625 to 0.0625
Outputs:
- attn_out: bfloat16 [32768, 4096], P(('dp', 'fsdp'))
- grad_rows: bfloat16 [32768, 8192], P(('dp', 'fsdp'))
- grad_weight: bfloat16 [8, 8192, 512], P('dp', 'fsdp')
Inputs may be any that keep to these rules, and one draw needn't show every extreme that they name: packing is a bijection onto 0 to 1023. Rollout row b * 8 + s (b = device block in dp+fsdp order) goes to a trainer slot of a block b' with the same fsdp index. From one device at most 2 rollouts go to any one device, and exactly 2 to some device; among devices of one fsdp index, the number of rollouts sent from dp index p to dp index (p + o) mod 8 depends on o only; each device receives exactly 8. `group_ids`: some groups may be empty.
All inputs are finite; a program needn't handle non-finite values. No bound on the sum of `lengths` on one device may be relied on, other than what follows from the above.
Results may differ from a plain program's by a relative error of at most 0.023.
Values may be sent and summed in bfloat16 or wider, within the bound.
No kernel may reach another device: no remote copies, remote signals or barrier semaphores. Data moves between devices by JAX's collectives and lax.ppermute only.
A program may use at most 128 MiB of HBM per device.

v0:
```python
import jax
import jax.numpy as jnp
from jax import lax
from jax.sharding import PartitionSpec as P

HD = 128
GSIZE = 16


def shards(
    rollout_rows, rewards, group_ids, lengths, packing, queries, keys, out_grad, value_weight
):
    slots, seq, width = rollout_rows.shape
    count_dp = lax.axis_size("dp")
    count_fsdp = lax.axis_size("fsdp")
    capacity = 2 * slots // count_dp
    groups = slots * count_dp * count_fsdp // GSIZE
    group_hit = (group_ids[:, None] == jnp.arange(groups, dtype=jnp.int32)[None, :]).astype(
        jnp.float32
    )
    totals = jnp.sum(group_hit * rewards[:, None], axis=0)
    counts = jnp.sum(group_hit, axis=0)
    totals, counts = lax.psum((totals, counts), ("dp", "fsdp"))
    means = totals / jnp.maximum(counts, 1.0)
    advantage = (rewards - jnp.sum(group_hit * means[None, :], axis=1)).astype(jnp.bfloat16)
    dest_dp = packing // slots // count_fsdp
    dest_slot = packing % slots
    index = jnp.arange(slots, dtype=jnp.int32)
    same_dest = (dest_dp[:, None] == dest_dp[None, :]) & (index[:, None] > index[None, :])
    rank = jnp.sum(same_dest.astype(jnp.int32), axis=1)
    position = dest_dp * capacity + rank
    pick = jnp.arange(count_dp * capacity, dtype=jnp.int32)[:, None] == position[None, :]
    pick_int = pick.astype(jnp.int32)
    send_rows = jnp.dot(
        pick.astype(jnp.bfloat16),
        rollout_rows.reshape(slots, seq * width),
        preferred_element_type=jnp.float32,
    )
    send_rows = send_rows.astype(jnp.bfloat16).reshape(count_dp, capacity, seq, width)
    send_slot = jnp.sum(pick_int * (dest_slot + 1)[None, :], axis=1) - 1
    send_len = jnp.sum(pick_int * lengths[None, :], axis=1)
    send_meta = jnp.stack([send_slot, send_len], axis=-1).reshape(count_dp, capacity, 2)
    send_adv = jnp.sum(pick.astype(jnp.float32) * advantage.astype(jnp.float32)[None, :], axis=1)
    send_adv = send_adv.astype(jnp.bfloat16).reshape(count_dp, capacity)
    recv_rows, recv_meta, recv_adv = (
        lax.all_to_all(send_rows, "dp", split_axis=0, concat_axis=0, tiled=True),
        lax.all_to_all(send_meta, "dp", split_axis=0, concat_axis=0, tiled=True),
        lax.all_to_all(send_adv, "dp", split_axis=0, concat_axis=0, tiled=True),
    )
    recv_meta = recv_meta.reshape(count_dp * capacity, 2)
    place = index[:, None] == recv_meta[:, 0][None, :]
    packed_rows = jnp.dot(
        place.astype(jnp.bfloat16),
        recv_rows.reshape(count_dp * capacity, seq * width),
        preferred_element_type=jnp.float32,
    )
    packed_rows = packed_rows.astype(jnp.bfloat16).reshape(slots * seq, width)
    packed_len = jnp.sum(place.astype(jnp.int32) * recv_meta[:, 1][None, :], axis=1)
    packed_adv = jnp.sum(
        place.astype(jnp.float32) * recv_adv.reshape(-1).astype(jnp.float32)[None, :], axis=1
    )
    value_width = value_weight.shape[1]
    full_weight = lax.all_gather(value_weight, "fsdp", axis=0, tiled=True)
    values = jnp.dot(packed_rows, full_weight, preferred_element_type=jnp.float32)
    values = values.astype(jnp.bfloat16)
    kv_heads = value_width // HD
    group_q = queries.shape[1] // value_width
    query_heads = queries.reshape(slots, seq, kv_heads, group_q, HD)
    key_heads = keys.reshape(slots, seq, kv_heads, HD)
    value_heads = values.reshape(slots, seq, kv_heads, HD)
    scores = jnp.einsum(
        "sikgd,sjkd->skgij", query_heads, key_heads, preferred_element_type=jnp.float32
    )
    scores = scores / jnp.sqrt(jnp.float32(HD))
    steps = jnp.arange(seq, dtype=jnp.int32)
    live = steps[None, :] < packed_len[:, None]
    causal = steps[:, None] >= steps[None, :]
    allowed = causal[None, None, None, :, :] & live[:, None, None, None, :]
    masked = jnp.where(allowed, scores, -jnp.inf)
    top = jnp.max(masked, axis=-1, keepdims=True)
    weights = jnp.where(allowed, jnp.exp(masked - top), 0.0)
    probs = (weights / jnp.sum(weights, axis=-1, keepdims=True)).astype(jnp.bfloat16)
    outputs = jnp.einsum(
        "skgij,sjkd->sikgd", probs, value_heads, preferred_element_type=jnp.float32
    )
    query_live = live.astype(jnp.float32)[:, :, None, None, None]
    attn_out = (outputs * query_live).astype(jnp.bfloat16).reshape(slots * seq, queries.shape[1])
    factor = -packed_adv * seq / packed_len.astype(jnp.float32)
    cot = (
        factor[:, None, None, None, None]
        * query_live
        * out_grad.reshape(slots, seq, kv_heads, group_q, HD).astype(jnp.float32)
    )
    cot = cot.astype(jnp.bfloat16)
    dvalues = jnp.einsum("skgij,sikgd->sjkd", probs, cot, preferred_element_type=jnp.float32)
    dvalues = dvalues.astype(jnp.bfloat16).reshape(slots * seq, value_width)
    grad_rows = lax.dot_general(
        dvalues, full_weight, (((1,), (1,)), ((), ())), preferred_element_type=jnp.float32
    )
    grad_rows = grad_rows.astype(jnp.bfloat16)
    grad_shard = lax.psum_scatter(
        lax.dot_general(
            packed_rows, dvalues, (((0,), (0,)), ((), ())), preferred_element_type=jnp.float32
        ).astype(jnp.bfloat16),
        "fsdp",
        scatter_dimension=0,
        tiled=True,
    ).astype(jnp.float32)
    grad_weight = (grad_shard / count_fsdp).astype(jnp.bfloat16)[None, :, :]
    return (attn_out, grad_rows, grad_weight)


def solution(mesh):
    in_specs = (
        P(("dp", "fsdp"), None, None),
        P(("dp", "fsdp")),
        P(("dp", "fsdp")),
        P(("dp", "fsdp")),
        P(("dp", "fsdp")),
        P(("dp", "fsdp"), None),
        P(("dp", "fsdp"), None),
        P(("dp", "fsdp"), None),
        P("fsdp", None),
    )
    out_specs = (P(("dp", "fsdp"), None), P(("dp", "fsdp"), None), P("dp", "fsdp", None))
    return jax.shard_map(shards, mesh=mesh, in_specs=in_specs, out_specs=out_specs, check_vma=False)
```

profile of v0, /device:TPU:2, one launch (start us, length us, event | category | flops | bytes accessed | tf_op | source)
XLA Modules:
  0.0 321.7 jit_solution(8275586059980819324)
XLA Ops:
  7.2 0.7 all-gather.2.cloned.1.call-update
  7.9 0.8 convert_reduce_fusion.1
  8.7 67.2 %all-reduce = (f32[64]{0:T(128)S(1)}, f32[64]{0:T(128)S(1)}) all-reduce(f32[64]{0:T(128)S(1)} %get-tuple-element.4, f32[64]{0:T(128)S(1)} %get-tuple-element.3), channel_id=1, replica_groups=mesh['dp'=8,'fsdp'=16] {'dp','fsdp'}, use_global_device_ids=true, to_apply=%region_7.8 | all-reduce | flops 128 | bytes 1024 | tf_op jit(solution)/shard_map/psum | solution.py:23
  75.9 0.7 and_select_fusion.1
  76.7 0.8 select_reduce_fusion.2
  77.6 0.7 convert_convert_fusion
  78.3 0.7 convert_element_type.129
  79.0 3.7 %all-to-all-start.2 = ((bf16[8,1,2]{2,1,0:T(2,128)(2,1)}), bf16[8,1,2]{2,1,0:T(2,128)(2,1)S(1)}, u32[]{:S(2)}, u32[]{:S(2)}) async-start(bf16[8,1,2]{2,1,0:T(2,128)(2,1)} %convert_element_type.129), calls=%async_computation.2 | async-start | bytes 8192 | tf_op jit(solution)/shard_map/all_to_all | solution.py:48
  82.7 0.7 select_reduce_fusion.6
  84.3 4.5 %copy.54 = bf16[1,8,32,8192]{3,1,2,0:T(8,128)(2,1)S(1)} copy(bf16[1,8,32,8192]{3,2,1,0:T(8,128)(2,1)} %bitcast.67) | data formatting | bytes 8388608
  88.8 5.1 %convolution_convert_fusion = bf16[16,262144]{1,0:T(8,128)(2,1)} fusion(bf16[8,262144]{1,0:T(8,128)(2,1)S(1)} %bitcast.65, s32[8]{0:T(128)S(1)} %multiply_add_fusion), kind=kOutput, calls=%fused_computation.1 | convolution fusion | flops 71303296 | bytes 12582944 | tf_op jit(solution)/shard_map/dot_general | solution.py:34
  93.9 7.2 %all-to-all-start = ((s32[8,2,2]{1,2,0:T(2,128)}), s32[8,2,2]{1,2,0:T(2,128)S(1)}, u32[]{:S(2)}, u32[]{:S(2)}) async-start(s32[8,2,2]{1,2,0:T(2,128)} %copy.36), calls=%async_computation | async-start | bytes 16384 | tf_op jit(solution)/shard_map/all_to_all | solution.py:47
  101.1 11.2 %copy.55 = bf16[2,8,32,8192]{3,2,1,0:T(8,128)(2,1)} copy(bf16[2,8,32,8192]{3,1,2,0:T(8,128)(2,1)} %bitcast.62) | data formatting | bytes 16777216
  112.3 7.2 %all-to-all-start.1 = ((bf16[8,2,32,8192]{3,2,1,0:T(8,128)(2,1)}), bf16[8,2,32,8192]{3,2,1,0:T(8,128)(2,1)}, u32[]{:S(2)}, u32[]{:S(2)}) async-start(bf16[8,2,32,8192]{3,2,1,0:T(8,128)(2,1)} %bitcast.64), calls=%async_computation.1 | async-start | bytes 16777216 | tf_op jit(solution)/shard_map/all_to_all | solution.py:46
  119.8 2.1 copy.57
  121.9 2.1 convert_bitcast_fusion
  124.0 2.7 copy.58
  126.7 5.5 %fusion.5 = f32[8,4,32,32,8]{3,2,4,1,0:T(8,128)} fusion(bf16[8,32,4,8,128]{4,3,2,1,0:T(8,128)(2,1)S(1)} %bitcast.66, bf16[8,32,4,128,1]{3,2,1,0,4:T(4,128)(2,1)S(1)} %bitcast.72), kind=kOutput, calls=%fused_computation.14 | convolution fusion | flops 67108864 | bytes 3407872 | tf_op jit(solution)/shard_map/sikgd,sjkd->skgij/dot_general | solution.py:71
  132.9 5.6 %fusion.36 = (f32[8,4,8,32]{3,2,1,0:T(8,128)S(1)}, f32[8,4,8,32,32]{3,4,2,1,0:T(8,128)S(1)}) fusion(f32[8,4,32,32,8]{3,2,4,1,0:T(8,128)} %fusion.5, pred[8,32,32]{1,2,0:T(8,128)(4,1)S(1)} %broadcast_and_fusion), kind=kOutput, calls=%fused_computation.75 | output fusion | flops 1835039 | bytes 2138112 | tf_op jit(solution)/shard_map/sub | solution.py:81
  138.5 2.8 fusion.18
  141.4 70.8 %all-to-all-done.1 = bf16[8,2,32,8192]{3,2,1,0:T(8,128)(2,1)} async-done(((bf16[8,2,32,8192]{3,2,1,0:T(8,128)(2,1)}), bf16[8,2,32,8192]{3,2,1,0:T(8,128)(2,1)}, u32[]{:S(2)}, u32[]{:S(2)}) %all-to-all-start.1) | async-done | bytes 8388640 | tf_op jit(solution)/shard_map/all_to_all | solution.py:46
  212.2 11.4 %copy.56 = bf16[2,8,32,8192]{3,1,2,0:T(8,128)(2,1)} copy(bf16[2,8,32,8192]{3,2,1,0:T(8,128)(2,1)} %bitcast.17) | data formatting | bytes 16777216
  223.6 6.6 %convolution_convert_fusion.1 = bf16[8,262144]{1,0:T(8,128)(2,1)} fusion(bf16[16,262144]{1,0:T(8,128)(2,1)} %bitcast.63, s32[16]{0:T(128)S(1)} %get-tuple-element.9), kind=kOutput, calls=%fused_computation.2 | convolution fusion | flops 69206144 | bytes 12582976 | tf_op jit(solution)/shard_map/dot_general | solution.py:52
  230.3 6.0 %reshape.195 = bf16[256,8192]{1,0:T(8,128)(2,1)} reshape(bf16[8,262144]{1,0:T(8,128)(2,1)} %convolution_convert_fusion.1) | data formatting | bytes 8388608 | tf_op jit(solution)/shard_map/reshape | solution.py:57
  236.3 7.8 %convolution_convert_fusion.2 = bf16[8192,512]{1,0:T(8,128)(2,1)} fusion(bf16[256,8192]{1,0:T(8,128)(2,1)} %reshape.195, bf16[32,8,4,128]{3,2,1,0:T(4,128)(2,1)S(1)} %bitcast.69), kind=kOutput, calls=%fused_computation.3 | convolution fusion | flops 2151677952 | bytes 12845056 | tf_op jit(solution)/shard_map/dot_general | solution.py:102
  244.1 7.0 %convolution_convert_fusion.4 = bf16[256,512]{1,0:T(8,128)(2,1)S(1)} fusion(bf16[256,8192]{1,0:T(8,128)(2,1)} %reshape.195, bf16[8192,512]{1,0:T(8,128)(2,1)} %all-gather.2.cloned.1.call-done), kind=kOutput, calls=%fused_computation.23 | convolution fusion | flops 2147614720 | bytes 12845056 | tf_op jit(solution)/shard_map/dot_general | solution.py:64
  251.2 3.4 %fusion.11 = bf16[8,32,4,8,128]{4,1,3,2,0:T(8,128)(2,1)S(1)} fusion(f32[8,32]{1,0:T(8,128)S(1)} %get-tuple-element.12, bf16[8,32,4,128,1]{3,2,1,0,4:T(4,128)(2,1)S(1)} %bitcast.73, f32[8,4,8,32,32]{3,4,2,1,0:T(8,128)} %copy-done.2, f32[8,4,8,32]{3,2,1,0:T(8,128)S(1)} %get-tuple-element.15), kind=kOutput, calls=%fused_computation.20 | convolution fusion | flops 69730304 | bytes 3441664 | tf_op jit(solution)/shard_map/skgij,sjkd->sikgd/dot_general | solution.py:83
  254.6 0.8 copy.42
  255.4 2.3 reshape.199
  257.7 7.9 %convolution_convert_fusion.3 = bf16[256,8192]{1,0:T(8,128)(2,1)} fusion(bf16[8192,512]{1,0:T(8,128)(2,1)} %all-gather.2.cloned.1.call-done, bf16[32,8,4,128]{3,2,1,0:T(4,128)(2,1)S(1)} %bitcast.70), kind=kOutput, calls=%fused_computation.4 | convolution fusion | flops 2149580800 | bytes 12845056 | tf_op jit(solution)/shard_map/dot_general | solution.py:97
  265.6 47.3 %reduce-scatter.2.cloned.1.call-done = bf16[512,512]{1,0:T(8,128)(2,1)} async-done(((bf16[8192,512]{1,0:T(8,128)(2,1)}), bf16[512,512]{1,0:T(8,128)(2,1)}) %reduce-scatter.2.cloned.1.call-update) | async-done | bytes 524304 | tf_op jit(solution)/shard_map/reduce_scatter | solution.py:101
  313.0 1.9 fusion.21
  (36 shorter events, 2.3 us)
Async XLA Ops:
  7.2 236.9 %all-gather.2.cloned.1.call-start = ((), (), s32[]{:S(2)}) async-start(), calls=%async_computation.4 | async-start | bytes 8912896 | tf_op jit(solution)/shard_map/all_gather | solution.py:63
  79.0 14.9 %all-to-all-start.2 = ((bf16[8,1,2]{2,1,0:T(2,128)(2,1)}), bf16[8,1,2]{2,1,0:T(2,128)(2,1)S(1)}, u32[]{:S(2)}, u32[]{:S(2)}) async-start(bf16[8,1,2]{2,1,0:T(2,128)(2,1)} %convert_element_type.129), calls=%async_computation.2 | async-start | bytes 8192 | tf_op jit(solution)/shard_map/all_to_all | solution.py:48
  93.9 18.4 %all-to-all-start = ((s32[8,2,2]{1,2,0:T(2,128)}), s32[8,2,2]{1,2,0:T(2,128)S(1)}, u32[]{:S(2)}, u32[]{:S(2)}) async-start(s32[8,2,2]{1,2,0:T(2,128)} %copy.36), calls=%async_computation | async-start | bytes 16384 | tf_op jit(solution)/shard_map/all_to_all | solution.py:47
  112.3 99.9 %all-to-all-start.1 = ((bf16[8,2,32,8192]{3,2,1,0:T(8,128)(2,1)}), bf16[8,2,32,8192]{3,2,1,0:T(8,128)(2,1)}, u32[]{:S(2)}, u32[]{:S(2)}) async-start(bf16[8,2,32,8192]{3,2,1,0:T(8,128)(2,1)} %bitcast.64), calls=%async_computation.1 | async-start | bytes 16777216 | tf_op jit(solution)/shard_map/all_to_all | solution.py:46
  119.5 2.3 copy-start.1
  119.5 193.4 %reduce-scatter.2.cloned.1.call-start = ((), (), s32[]{:S(2)}) async-start(), calls=%async_computation.5 | async-start | bytes 8912896 | tf_op jit(solution)/shard_map/reduce_scatter | solution.py:101
  132.9 5.6 %copy-start = (f32[32,8,32,128]{3,2,1,0:T(8,128)S(1)}, f32[32,8,32,128]{3,2,1,0:T(8,128)}, u32[]{:S(2)}) copy-start(f32[32,8,32,128]{3,2,1,0:T(8,128)} %copy.58) | copy-start | bytes 12582916
  138.4 2.8 copy-start.2
Sparse Core Ops, SparseCore 0:
  9.7 54.8 all-gather.1
  244.2 68.7 reduce-scatter.1
where the time goes:
time: 327 us; the launch traced here: 322 us
  waiting for transfers between devices  119 us (36%)
  blocking collectives  67.2 us (21%)
  matrix products  46.1 us (14%)
  local copies, waits for them, and re-layouts  42.9 us (13%)
  starting transfers between devices  18.4 us (6%)
  between operations  14.2 us (4%)
  other arithmetic  14.1 us (4%)
    all_to_all x1, waiting for transfers between devices, shards(): lax.all_to_all(send_rows, 'dp', split_axis=0, concat_axis=0, tiled=True)  70.8 us
    psum x1, blocking collectives, shards(): totals, counts = lax.psum((totals, counts), ('dp', 'fsdp'))  67.2 us
    reduce_scatter x1, waiting for transfers between devices, shards(): lax.psum_scatter(lax.dot_general(packed_rows, dvalues, (((0,), (0,)), (()...  47.3 us
    unnamed x11, local copies, waits for them, and re-layouts  31.9 us
    dot_general x1, matrix products, shards(): lax.dot_general(dvalues, full_weight, (((1,), (1,)), ((), ())), preferred...  7.94 us
    dot_general x1, matrix products, shards(): lax.dot_general(packed_rows, dvalues, (((0,), (0,)), ((), ())), preferred...  7.78 us
    all_to_all x1, starting transfers between devices, shards(): lax.all_to_all(send_meta, 'dp', split_axis=0, concat_axis=0, tiled=True)  7.21 us
    all_to_all x1, starting transfers between devices, shards(): lax.all_to_all(send_rows, 'dp', split_axis=0, concat_axis=0, tiled=True)  7.21 us
  transfers between devices with their start and end apart: 5, of which 2 were waited for; matrix products, arithmetic and copies ran while one was open for 31% of the time, Pallas kernels for 0%

commit v1 on v0

v1 whole, which is shorter than its diff:
```python
import functools

import jax
import jax.numpy as jnp
from jax import lax
from jax.experimental import pallas as pl
from jax.experimental.pallas import tpu as pltpu
from jax.sharding import PartitionSpec as P

HD = 128
VMEM = 56 * 1024 * 1024


def params(**kw):
    return pltpu.CompilerParams(vmem_limit_bytes=VMEM, **kw)


def prepare_body(slots, dp, fsdp, where, packing, lengths, rewards, groups, info, order):
    lane = lax.broadcasted_iota(jnp.int32, info.shape, 1)
    told = jnp.zeros(info.shape, jnp.float32)
    for r in range(slots):
        told = jnp.where(lane == r, packing[r].astype(jnp.float32), told)
        told = jnp.where(lane == slots + r, lengths[r].astype(jnp.float32), told)
        told = jnp.where(lane == 2 * slots + r, rewards[r], told)
        told = jnp.where(lane == 3 * slots + r, groups[r].astype(jnp.float32), told)
    info[...] = told
    home = where[1]
    offsets = [lax.rem(lax.div(packing[r], slots * fsdp) - home + dp, dp) for r in range(slots)]
    mine = jnp.int32(0)
    for r in range(slots):
        colour = jnp.int32(0)
        for k in range(slots):
            if k != r:
                first = offsets[k] <= offsets[r] if k < r else offsets[k] < offsets[r]
                colour = colour + jnp.where(first, 1, 0)
        order[r] = colour
        mine = mine + jnp.where(colour == home, offsets[r], 0)
    order[slots] = mine


def prepare(where, packing, lengths, rewards, groups, dp, fsdp):
    slots = packing.shape[0]
    smem = pl.BlockSpec(memory_space=pltpu.SMEM)
    return pl.pallas_call(
        functools.partial(prepare_body, slots, dp, fsdp),
        in_specs=[smem] * 5,
        out_specs=[pl.BlockSpec(memory_space=pltpu.VMEM), smem],
        out_shape=[
            jax.ShapeDtypeStruct((dp * fsdp, 4 * slots), jnp.float32),
            jax.ShapeDtypeStruct((slots + 1,), jnp.int32),
        ],
        name="prepare",
    )(where, packing, lengths, rewards, groups)


def pack_body(fsdp, order, rows, out, held, cut, arrive, leave):
    slots, _, width = rows.shape
    part = width // fsdp
    ins = [pltpu.make_async_copy(rows.at[r], held.at[r], arrive.at[r]) for r in range(slots)]
    outs = [pltpu.make_async_copy(cut.at[r], out.at[order[r]], leave.at[r]) for r in range(slots)]
    for copy in ins:
        copy.start()
    for r in range(slots):
        ins[r].wait()
        for f in range(fsdp):
            cut[r, f] = held[r, :, f * part : (f + 1) * part]
        outs[r].start()
    for copy in outs:
        copy.wait()


def pack(order, rows, fsdp):
    slots, seq, width = rows.shape
    part = width // fsdp
    return pl.pallas_call(
        functools.partial(pack_body, fsdp),
        in_specs=[pl.BlockSpec(memory_space=pltpu.SMEM), pl.BlockSpec(memory_space=pl.ANY)],
        out_specs=pl.BlockSpec(memory_space=pl.ANY),
        out_shape=jax.ShapeDtypeStruct((slots, fsdp, seq, part), rows.dtype),
        scratch_shapes=[
            pltpu.VMEM((slots, seq, width), rows.dtype),
            pltpu.VMEM((slots, fsdp, seq, part), rows.dtype),
            pltpu.SemaphoreType.DMA((slots,)),
            pltpu.SemaphoreType.DMA((slots,)),
        ],
        compiler_params=params(),
        cost_estimate=pl.CostEstimate(
            flops=0, bytes_accessed=2 * rows.size * 2, transcendentals=0
        ),
        name="pack_rows",
    )(order, rows)


def turn_body(dp, slots, order, rows, out, held, arrive, leave):
    ins = [pltpu.make_async_copy(rows.at[p], held.at[p], arrive.at[p]) for p in range(dp)]
    outs = []
    for p in range(dp):
        dest = lax.rem(order[slots] + p, dp)
        outs.append(pltpu.make_async_copy(held.at[p], out.at[dest], leave.at[p]))
    for copy in ins:
        copy.start()
    for p in range(dp):
        ins[p].wait()
        outs[p].start()
    for copy in outs:
        copy.wait()


def turn(order, rows):
    dp = rows.shape[0]
    return pl.pallas_call(
        functools.partial(turn_body, dp, order.shape[0] - 1),
        in_specs=[pl.BlockSpec(memory_space=pltpu.SMEM), pl.BlockSpec(memory_space=pl.ANY)],
        out_specs=pl.BlockSpec(memory_space=pl.ANY),
        out_shape=jax.ShapeDtypeStruct(rows.shape, rows.dtype),
        scratch_shapes=[
            pltpu.VMEM(rows.shape, rows.dtype),
            pltpu.SemaphoreType.DMA((dp,)),
            pltpu.SemaphoreType.DMA((dp,)),
        ],
        compiler_params=params(),
        cost_estimate=pl.CostEstimate(
            flops=0, bytes_accessed=2 * rows.size * 2, transcendentals=0
        ),
        name="turn_rows",
    )(order, rows)


def plan_body(slots, dp, fsdp, seq, me, info, length, colours, factor):
    packing = info[0:slots, :]
    lengths = info[slots : 2 * slots, :]
    rewards = info[2 * slots : 3 * slots, :]
    groups = info[3 * slots : 4 * slots, :]
    lane = lax.broadcasted_iota(jnp.int32, packing.shape, 1)
    row = lax.broadcasted_iota(jnp.int32, packing.shape, 0)
    target = lax.div(packing.astype(jnp.int32), slots * fsdp)

    offset = lax.rem(target - lax.div(lane, fsdp) + dp, dp)
    colour = jnp.zeros(packing.shape, jnp.int32)
    for k in range(1, slots):
        other = pltpu.roll(offset, k, 0)
        first = (other < offset) | ((other == offset) & (row >= k))
        colour = colour + jnp.where(first, 1, 0)
    colour = colour.astype(jnp.float32)

    def total(x):
        return jnp.sum(jnp.sum(x, axis=0, keepdims=True), axis=1, keepdims=True)

    for s in range(slots):
        hit = jnp.where(packing == (me[0] * slots + s).astype(jnp.float32), 1.0, 0.0)
        size = total(hit * lengths)
        reward = total(hit * rewards)
        same = jnp.where(groups == total(hit * groups), 1.0, 0.0)
        mean = total(same * rewards) / jnp.maximum(total(same), 1.0)
        advantage = (reward - mean).astype(jnp.bfloat16).astype(jnp.float32)
        factor[s : s + 1, :] = jnp.broadcast_to(-advantage * seq / size, (1, 128))
        colours[s] = total(hit * colour)[0, 0].astype(jnp.int32)
        length[s] = size[0, 0].astype(jnp.int32)


def plan(me, info, slots, dp, fsdp, seq):
    smem = pl.BlockSpec(memory_space=pltpu.SMEM)
    vmem = pl.BlockSpec(memory_space=pltpu.VMEM)
    return pl.pallas_call(
        functools.partial(plan_body, slots, dp, fsdp, seq),
        in_specs=[smem, vmem],
        out_specs=[smem, smem, vmem],
        out_shape=[
            jax.ShapeDtypeStruct((slots,), jnp.int32),
            jax.ShapeDtypeStruct((slots,), jnp.int32),
            jax.ShapeDtypeStruct((slots, 128), jnp.float32),
        ],
        cost_estimate=pl.CostEstimate(flops=1, bytes_accessed=1, transcendentals=0),
        name="plan_slots",
    )(me, info)


def stack_heads(ref, kh, group):
    cols = [ref[:, (kh * group + g) * HD : (kh * group + g + 1) * HD] for g in range(group)]
    return jnp.concatenate(cols, axis=0)


def probs_body(kv, group, slots, length, colours, factor, q, k, og, dv, turned, probs, held):
    s = pl.program_id(0)
    seq = q.shape[0]
    size = length[s]
    scale = factor[pl.ds(s, 1), :]
    key_pos = lax.broadcasted_iota(jnp.int32, (seq, group * seq), 0)
    query_pos = lax.rem(lax.broadcasted_iota(jnp.int32, (seq, group * seq), 1), seq)
    allowed = (key_pos <= query_pos) & (key_pos < size)
    live = query_pos < size
    shares = []
    for kh in range(kv):
        queries = stack_heads(q, kh, group)
        keys = k[:, kh * HD : (kh + 1) * HD]
        scores = lax.dot_general(
            keys, queries, (((1,), (1,)), ((), ())), preferred_element_type=jnp.float32
        ) / jnp.sqrt(jnp.float32(HD))
        masked = jnp.where(allowed, scores, -jnp.inf)
        top = jnp.max(masked, axis=0, keepdims=True)
        weights = jnp.where(allowed, jnp.exp(masked - top), 0.0)
        share = weights / jnp.sum(weights, axis=0, keepdims=True)
        share = jnp.where(live, share, 0.0)
        shares.append(share)
        share = share.astype(jnp.bfloat16)
        grads = stack_heads(og, kh, group)
        part = jnp.dot(share, grads, preferred_element_type=jnp.float32)
        part = (part * scale).astype(jnp.bfloat16)
        dv[:, kh * HD : (kh + 1) * HD] = part
        held[colours[s], :, kh * HD : (kh + 1) * HD] = part
    probs[0] = jnp.concatenate(shares, axis=0).T.astype(jnp.bfloat16)

    @pl.when(s == slots - 1)
    def _():
        turned[...] = held[...].reshape(slots * seq, kv * HD).T


def probs_and_dvalues(length, colours, factor, queries, keys, out_grad, slots):
    tokens, width = queries.shape
    seq = tokens // slots
    kv = keys.shape[1] // HD
    group = width // HD // kv
    return pl.pallas_call(
        functools.partial(probs_body, kv, group, slots),
        grid_spec=pltpu.PrefetchScalarGridSpec(
            num_scalar_prefetch=2,
            grid=(slots,),
            in_specs=[
                pl.BlockSpec((slots, 128), lambda s, n, c: (0, 0)),
                pl.BlockSpec((seq, width), lambda s, n, c: (s, 0)),
                pl.BlockSpec((seq, keys.shape[1]), lambda s, n, c: (s, 0)),
                pl.BlockSpec((seq, width), lambda s, n, c: (s, 0)),
            ],
            out_specs=[
                pl.BlockSpec((seq, keys.shape[1]), lambda s, n, c: (s, 0)),
                pl.BlockSpec((keys.shape[1], tokens), lambda s, n, c: (0, 0)),
                pl.BlockSpec((1, group * seq, kv * seq), lambda s, n, c: (s, 0, 0)),
            ],
            scratch_shapes=[pltpu.VMEM((slots, seq, keys.shape[1]), jnp.bfloat16)],
        ),
        out_shape=[
            jax.ShapeDtypeStruct((tokens, keys.shape[1]), jnp.bfloat16),
            jax.ShapeDtypeStruct((keys.shape[1], tokens), jnp.bfloat16),
            jax.ShapeDtypeStruct((slots, group * seq, kv * seq), jnp.bfloat16),
        ],
        compiler_params=params(),
        cost_estimate=pl.CostEstimate(flops=1, bytes_accessed=1, transcendentals=0),
        name="probs_dvalues",
    )(length, colours, factor, queries, keys, out_grad)


def values_body(steps, where, rows, near, far, out, acc):
    step = pl.program_id(0)
    dp, _, low, seq, part = rows.shape
    total = jnp.zeros(acc.shape, jnp.float32)
    for c in range(low):
        for w, h in ((near, where[2]), (far, 1 - where[2])):
            x = rows[:, h, c].reshape(dp * seq, part)
            total += jnp.dot(x, w[c], preferred_element_type=jnp.float32)

    @pl.when(step == 0)
    def _():
        acc[...] = total

    @pl.when(step > 0)
    def _():
        acc[...] += total

    @pl.when(step == steps - 1)
    def _():
        out[...] = acc[...].astype(out.dtype).reshape(out.shape)


def values_of(where, rows, near, far):
    dp, high, low, seq, part = rows.shape
    cols = near.shape[2]
    each = 2
    steps = low // each
    return pl.pallas_call(
        functools.partial(values_body, steps),
        grid_spec=pltpu.PrefetchScalarGridSpec(
            num_scalar_prefetch=1,
            grid=(steps,),
            in_specs=[pl.BlockSpec((dp, high, each, seq, part), lambda i, n: (0, 0, i, 0, 0))]
            + [pl.BlockSpec((each, part, cols), lambda i, n: (i, 0, 0))] * 2,
            out_specs=pl.BlockSpec((dp, seq, cols), lambda i, n: (0, 0, 0)),
            scratch_shapes=[pltpu.VMEM((dp * seq, cols), jnp.float32)],
        ),
        out_shape=jax.ShapeDtypeStruct((dp, seq, cols), jnp.bfloat16),
        compiler_params=params(),
        cost_estimate=pl.CostEstimate(flops=1, bytes_accessed=1, transcendentals=0),
        name="values",
    )(where, rows, near, far)


def grad_rows_body(where, dv, near, far, out):
    each, part, _ = near.shape
    half = pl.program_id(0)

    def write(w):
        for c in range(each):
            out[:, c * part : (c + 1) * part] = lax.dot_general(
                dv[...], w[c], (((1,), (1,)), ((), ())), preferred_element_type=jnp.float32
            ).astype(out.dtype)

    @pl.when(half == 0)
    def _():
        write(near)

    @pl.when(half == 1)
    def _():
        write(far)


def grad_rows_of(where, dv, near, far):
    tokens, cols = dv.shape
    low, part, _ = near.shape
    each = 4
    steps = low // each
    return pl.pallas_call(
        grad_rows_body,
        grid_spec=pltpu.PrefetchScalarGridSpec(
            num_scalar_prefetch=1,
            grid=(2, steps),
            in_specs=[
                pl.BlockSpec((tokens, cols), lambda h, i, n: (0, 0)),
                pl.BlockSpec((each, part, cols), lambda h, i, n: (i * (1 - h) + (steps - 1) * h, 0, 0)),
                pl.BlockSpec((each, part, cols), lambda h, i, n: (i * h, 0, 0)),
            ],
            out_specs=pl.BlockSpec(
                (tokens, each * part), lambda h, i, n: (0, lax.rem(n[2] + h, 2) * steps + i)
            ),
        ),
        out_shape=jax.ShapeDtypeStruct((tokens, 2 * low * part), jnp.bfloat16),
        compiler_params=params(),
        cost_estimate=pl.CostEstimate(flops=1, bytes_accessed=1, transcendentals=0),
        name="grad_rows",
    )(where, dv, near, far)


def attend_body(kv, group, dp, each, colours, where, probs, *rest):
    values, out, held = rest[:dp], rest[dp], rest[dp + 1]
    step = pl.program_id(0)
    seq, cols = values[0].shape

    @pl.when(step == 0)
    def _():
        for k in range(dp):
            held[k] = values[k][...]

    for e in range(each):
        away = lax.rem(where[1] - colours[step * each + e] + dp, dp)
        mine = held[away]
        zero = jnp.zeros((seq, HD), mine.dtype)
        blocks = []
        for kh in range(kv):
            row = [zero] * kv
            row[kh] = mine[:, kh * HD : (kh + 1) * HD]
            blocks.append(jnp.concatenate(row, axis=1))
        heads = jnp.dot(
            probs[e], jnp.concatenate(blocks, axis=0), preferred_element_type=jnp.float32
        ).astype(out.dtype)
        for kh in range(kv):
            for g in range(group):
                h = kh * group + g
                out[e * seq : (e + 1) * seq, h * HD : (h + 1) * HD] = heads[
                    g * seq : (g + 1) * seq, kh * HD : (kh + 1) * HD
                ]


def attend(colours, where, probs, values):
    slots, span, keys = probs.shape
    seq, cols = values[0].shape
    kv = cols // HD
    group = span // seq
    width = kv * group * HD
    dp = len(values)
    each = 2
    return pl.pallas_call(
        functools.partial(attend_body, kv, group, dp, each),
        grid_spec=pltpu.PrefetchScalarGridSpec(
            num_scalar_prefetch=2,
            grid=(slots // each,),
            in_specs=[pl.BlockSpec((each, span, keys), lambda s, c, w: (s, 0, 0))]
            + [pl.BlockSpec((seq, cols), lambda s, c, w: (0, 0))] * dp,
            out_specs=pl.BlockSpec((each * seq, width), lambda s, c, w: (s, 0)),
            scratch_shapes=[pltpu.VMEM((dp, seq, cols), jnp.bfloat16)],
        ),
        out_shape=jax.ShapeDtypeStruct((slots * seq, width), jnp.bfloat16),
        compiler_params=params(),
        cost_estimate=pl.CostEstimate(flops=1, bytes_accessed=1, transcendentals=0),
        name="attend",
    )(colours, where, probs, *values)


def product_body(steps, scale, where, near_rows, far_rows, near, far, out, acc):
    step = pl.program_id(0)
    colours, _, each, seq, width = near_rows.shape
    part = jnp.zeros(acc.shape, jnp.float32)
    for rows, dv in ((near_rows, near), (far_rows, far)):
        for b in range(each):
            x = rows[:, 0, b].reshape(colours * seq, width)
            part += jnp.dot(dv[b], x, preferred_element_type=jnp.float32)

    @pl.when(step == 0)
    def _():
        acc[...] = part

    @pl.when(step > 0)
    def _():
        acc[...] += part

    @pl.when(step == steps - 1)
    def _():
        out[...] = (acc[...] * scale).T.astype(out.dtype)


def product(where, rows, near, far, scale):
    colours, _, low, seq, width = rows.shape
    cols = near.shape[1]
    each = 2
    steps = low // each
    return pl.pallas_call(
        functools.partial(product_body, steps, scale),
        grid_spec=pltpu.PrefetchScalarGridSpec(
            num_scalar_prefetch=1,
            grid=(steps,),
            in_specs=[
                pl.BlockSpec((colours, 1, each, seq, width), lambda i, n: (0, n[2], i, 0, 0)),
                pl.BlockSpec((colours, 1, each, seq, width), lambda i, n: (0, 1 - n[2], i, 0, 0)),
                pl.BlockSpec((each, cols, colours * seq), lambda i, n: (i, 0, 0)),
                pl.BlockSpec((each, cols, colours * seq), lambda i, n: (i, 0, 0)),
            ],
            out_specs=pl.BlockSpec((width, cols), lambda i, n: (0, 0)),
            scratch_shapes=[pltpu.VMEM((cols, width), jnp.float32)],
        ),
        out_shape=jax.ShapeDtypeStruct((width, cols), jnp.bfloat16),
        compiler_params=params(),
        cost_estimate=pl.CostEstimate(
            flops=2 * rows.size * cols,
            bytes_accessed=2 * (2 * rows.size + width * cols),
            transcendentals=0,
        ),
        name="weight_product",
    )(where, rows, rows, near, far)


def shards(
    rollout_rows, rewards, group_ids, lengths, packing, queries, keys, out_grad, value_weight
):
    slots, seq, width = rollout_rows.shape
    dp = lax.axis_size("dp")
    fsdp = lax.axis_size("fsdp")
    part = width // fsdp
    home = lax.axis_index("dp")
    place = lax.axis_index("fsdp")
    where = jnp.stack([home * fsdp + place, home, lax.div(place, fsdp // 2)]).astype(jnp.int32)
    info, order = prepare(where, packing, lengths, rewards, group_ids, dp, fsdp)
    info = lax.all_to_all(info, ("dp", "fsdp"), split_axis=0, concat_axis=0, tiled=True)
    rows = pack(order, rollout_rows, fsdp)
    low = fsdp // 2
    halves = [list(range(low)), list(range(low, fsdp))]
    swap = [(i, (i + low) % fsdp) for i in range(fsdp)]
    far_weight = lax.ppermute(value_weight, "fsdp", swap)
    rows, info, far_weight = lax.optimization_barrier((rows, info, far_weight))
    rows = lax.all_to_all(
        rows.reshape(dp, fsdp * seq, part), "dp", split_axis=0, concat_axis=0, tiled=True
    )
    near = lax.all_gather(value_weight, "fsdp", axis_index_groups=halves)
    far = lax.all_gather(far_weight, "fsdp", axis_index_groups=halves)
    length, colours, factor = plan(where, info.T, slots, dp, fsdp, seq)
    dvalues, coloured, probs = probs_and_dvalues(
        length, colours, factor, queries, keys, out_grad, slots
    )
    rows, dvalues, probs = lax.optimization_barrier((rows, dvalues, probs))
    far_dv = lax.ppermute(coloured, "fsdp", swap)
    rows = turn(order, rows)
    rows, far_dv = lax.optimization_barrier((rows, far_dv))
    coloured, near, far = lax.optimization_barrier((coloured, near, far))
    near_dv = lax.all_gather(coloured, "fsdp", axis_index_groups=halves)
    far_dv = lax.all_gather(far_dv, "fsdp", axis_index_groups=halves)
    values = values_of(where, rows.reshape(dp, 2, low, seq, part), near, far)
    grad_rows = grad_rows_of(where, dvalues, near, far)
    held = [
        lax.dynamic_index_in_dim(values, lax.rem(home + k, dp), 0, keepdims=False)
        for k in range(dp)
    ]
    held = [held[0]] + [
        lax.ppermute(held[k], "dp", [(i, (i + k) % dp) for i in range(dp)])
        for k in range(1, dp)
    ]
    rows = lax.all_to_all(
        rows.reshape(dp * fsdp, seq, part),
        ("dp", "fsdp"),
        split_axis=0,
        concat_axis=0,
        tiled=True,
    )
    rows, grad_rows = lax.optimization_barrier((rows, grad_rows))
    grad_weight = product(
        where, rows.reshape(dp, 2, low, seq, part), near_dv, far_dv, 1.0 / fsdp
    )[None]
    attn_out = attend(colours, where, probs, held)
    return (attn_out, grad_rows, grad_weight)


def solution(mesh):
    in_specs = (
        P(("dp", "fsdp"), None, None),
        P(("dp", "fsdp")),
        P(("dp", "fsdp")),
        P(("dp", "fsdp")),
        P(("dp", "fsdp")),
        P(("dp", "fsdp"), None),
        P(("dp", "fsdp"), None),
        P(("dp", "fsdp"), None),
        P("fsdp", None),
    )
    out_specs = (P(("dp", "fsdp"), None), P(("dp", "fsdp"), None), P("dp", "fsdp", None))
    return jax.shard_map(shards, mesh=mesh, in_specs=in_specs, out_specs=out_specs, check_vma=False)
```

time: 327 us -> 184 us (0.56); the launches traced: 322 us -> 182 us
  blocking collectives: 67.2 us -> 0 us
  waiting for transfers between devices: 119 us -> 63.9 us
  Pallas kernels: 0 us -> 50.6 us
  matrix products: 46.1 us -> 0 us
  local copies, waits for them, and re-layouts: 42.9 us -> 4.27 us
  starting transfers between devices: 18.4 us -> 48.7 us
  other arithmetic: 14.1 us -> 0.62 us
    psum x1 -> x0, blocking collectives: 67.2 us -> none  [shards(): totals, counts = lax.psum((totals, counts), ('dp', 'fsdp'))]
    pallas_call x0 -> x9, Pallas kernels: none -> 50.6 us  [the longest x1 10.4 us: probs_and_dvalues(): pl.pallas_call(functools.partial(probs_body, kv, group, slots), grid_spec...]
    reduce_scatter x1 -> x0, waiting for transfers between devices: 47.3 us -> none  [shards(): lax.psum_scatter(lax.dot_general(packed_rows, dvalues, (((0,), (0,)), (()...]
    dot_general x8 -> x0, matrix products: 46.1 us -> none  [the longest x1 7.94 us: shards(): lax.dot_general(dvalues, full_weight, (((1,), (1,)), ((), ())), preferred...]
    unnamed x11 -> x18, local copies, waits for them, and re-layouts: 31.9 us -> 2.09 us
    ppermute x0 -> x9, starting transfers between devices: none -> 26.6 us  [the longest x7 24.2 us: shards(): lax.ppermute(held[k], 'dp', [(i, (i + k) % dp) for i in range(dp)])]
    all_to_all x3, waiting for transfers between devices: 70.8 us -> 54.2 us  [the longest x1 37.5 us: shards(): lax.all_to_all(rows.reshape(dp, fsdp * seq, part), 'dp', split_axis=0, co...]
    reshape x5 -> x0, local copies, waits for them, and re-layouts: 8.51 us -> none  [the longest x1 6 us: shards(): packed_rows = packed_rows.astype(jnp.bfloat16).reshape(slots * seq, width)]
  transfers between devices with their start and end apart: 5 -> 16, of which waited for: 2 -> 4; matrix products, arithmetic and copies ran while one was open for 31% -> 2% of each run, Pallas kernels for 0% -> 24%
where the time goes in v1:
time: 184 us; the launch traced here: 182 us
  waiting for transfers between devices  63.9 us (35%)
  Pallas kernels  50.6 us (28%)
  starting transfers between devices  48.7 us (26%)
  between operations  14 us (8%)
  local copies, waits for them, and re-layouts  4.27 us (2%)
    all_to_all x1, waiting for transfers between devices, shards(): lax.all_to_all(rows.reshape(dp, fsdp * seq, part), 'dp', split_axis=0, co...  37.5 us
    ppermute x7, starting transfers between devices, shards(): lax.ppermute(held[k], 'dp', [(i, (i + k) % dp) for i in range(dp)])  24.2 us
    all_to_all x1, waiting for transfers between devices, shards(): lax.all_to_all(rows.reshape(dp * fsdp, seq, part), ('dp', 'fsdp'), split_...  12.2 us
    pallas_call x1, Pallas kernels, probs_and_dvalues(): pl.pallas_call(functools.partial(probs_body, kv, group, slots), grid_spec...  10.4 us
    all_to_all x1, starting transfers between devices, shards(): lax.all_to_all(info, ('dp', 'fsdp'), split_axis=0, concat_axis=0, tiled=T...  10.2 us
    pallas_call x1, Pallas kernels, grad_rows_of(): pl.pallas_call(grad_rows_body, grid_spec=pltpu.PrefetchScalarGridSpec(num...  8.54 us
    ppermute x7, waiting for transfers between devices, shards(): lax.ppermute(held[k], 'dp', [(i, (i + k) % dp) for i in range(dp)])  8.5 us
    pallas_call x1, Pallas kernels, values_of(): pl.pallas_call(functools.partial(values_body, steps), grid_spec=pltpu.Pre...  7.96 us
  transfers between devices with their start and end apart: 16, of which 4 were waited for; matrix products, arithmetic and copies ran while one was open for 2% of the time, Pallas kernels for 24%

profile of v1, /device:TPU:2, one launch (start us, length us, event | category | flops | bytes accessed | tf_op | source)
XLA Modules:
  0.0 182.1 jit_solution(11042182930306134729)
XLA Ops:
  7.2 0.7 all-gather.9.cloned.1.call-update
  7.9 1.7 collective-permute-start
  9.6 0.6 pad_add_fusion.where.me
  10.2 1.4 prepare.1
  11.5 10.2 %all-to-all-start = ((f32[128,1,32]{2,1,0:T(1,128)}), f32[128,1,32]{2,1,0:T(1,128)S(1)}, u32[]{:S(2)}, u32[]{:S(2)}) async-start(f32[128,1,32]{2,1,0:T(1,128)} %bitcast.44), calls=%async_computation | async-start | bytes 131072 | tf_op jit(solution)/shard_map/all_to_all | solution.py:459
  21.8 4.5 %pack_rows.1 = bf16[8,16,32,512]{3,2,1,0:T(8,128)(2,1)} custom-call(s32[9]{0:T(128)} %get-tuple-element.24.order, bf16[8,32,8192]{2,1,0:T(8,128)(2,1)} %rows.1), custom_call_target="tpu_custom_call" | custom-call | bytes 8388608 | tf_op jit(solution)/shard_map/pack_rows/pallas_call | solution.py:75
  26.3 4.5 %all-to-all-done = f32[128,1,32]{2,1,0:T(1,128)S(1)} async-done(((f32[128,1,32]{2,1,0:T(1,128)}), f32[128,1,32]{2,1,0:T(1,128)S(1)}, u32[]{:S(2)}, u32[]{:S(2)}) %all-to-all-start) | async-done | bytes 16416 | tf_op jit(solution)/shard_map/all_to_all | solution.py:459
  30.8 0.7 copy.14
  31.5 0.8 copy-done
  32.3 4.6 %all-to-all-start.1 = ((bf16[8,512,512]{2,1,0:T(8,128)(2,1)}), bf16[8,512,512]{2,1,0:T(8,128)(2,1)}, u32[]{:S(2)}, u32[]{:S(2)}) async-start(bf16[8,512,512]{2,1,0:T(8,128)(2,1)} %bitcast.39), calls=%async_computation.1 | async-start | bytes 8388608 | tf_op jit(solution)/shard_map/all_to_all | solution.py:466
  36.9 1.5 plan_slots.1
  38.5 10.4 %probs_dvalues.1 = (bf16[256,512]{1,0:T(8,128)(2,1)}, bf16[512,256]{1,0:T(8,128)(2,1)}, bf16[8,256,128]{2,1,0:T(8,128)(2,1)}) custom-call(s32[8]{0:T(128)} %get-tuple-element.29.length, s32[8]{0:T(128)} %get-tuple-element.27.colours, f32[8,128]{1,0:T(8,128)} %get-tuple-element.30.factor, bf16[256,4096]{1,0:T(8,128)(2,1)} %q.1, bf16[256,512]{1,0:T(8,128)(2,1)} %k.1, ...), custom_call_target="tpu_custom_call" | custom-call | flops 1 | bytes 1 | tf_op jit(solution)/shard_map/probs_dvalues/pallas_call | solution.py:223
  48.9 0.7 collective-permute-start.1
  49.6 37.5 %all-to-all-done.1.rows = bf16[8,512,512]{2,1,0:T(8,128)(2,1)} async-done(((bf16[8,512,512]{2,1,0:T(8,128)(2,1)}), bf16[8,512,512]{2,1,0:T(8,128)(2,1)}, u32[]{:S(2)}, u32[]{:S(2)}) %all-to-all-start.1) | async-done | bytes 4194336 | tf_op jit(solution)/shard_map/all_to_all | solution.py:466
  87.1 4.2 %turn_rows.1 = bf16[8,512,512]{2,1,0:T(8,128)(2,1)} custom-call(s32[9]{0:T(128)} %get-tuple-element.24.order, bf16[8,512,512]{2,1,0:T(8,128)(2,1)} %all-to-all-done.1.rows), custom_call_target="tpu_custom_call" | custom-call | bytes 8388608 | tf_op jit(solution)/shard_map/turn_rows/pallas_call | solution.py:111
  91.4 0.7 copy-done.1
  92.1 7.1 %all-to-all-start.2 = ((bf16[128,32,512]{2,1,0:T(8,128)(2,1)}), bf16[128,32,512]{2,1,0:T(8,128)(2,1)}, u32[]{:S(2)}, u32[]{:S(2)}) async-start(bf16[128,32,512]{2,1,0:T(8,128)(2,1)} %bitcast.33), calls=%async_computation.2 | async-start | bytes 8388608 | tf_op jit(solution)/shard_map/all_to_all | solution.py:492
  99.3 0.5 all-gather.13.cloned.1.call-update
  99.9 8.0 %values.1 = bf16[8,32,512]{2,1,0:T(8,128)(2,1)} custom-call(s32[3]{0:T(128)} %pad_add_fusion.where.me, bf16[8,2,8,32,512]{4,3,2,1,0:T(8,128)(2,1)} %bitcast.34, bf16[8,512,512]{2,1,0:T(8,128)(2,1)} %bitcast.35, bf16[8,512,512]{2,1,0:T(8,128)(2,1)} %bitcast.37), custom_call_target="tpu_custom_call" | custom-call | flops 1 | bytes 1 | tf_op jit(solution)/shard_map/values/pallas_call | solution.py:279
  107.8 1.5 dynamic-slice_bitcast_fusion
  109.3 1.6 collective-permute-start.2
  110.9 3.1 %collective-permute-start.3 = (bf16[32,512]{1,0:T(8,128)(2,1)S(1)}, bf16[32,512]{1,0:T(8,128)(2,1)S(1)}, u32[]{:S(2)}, u32[]{:S(2)}) collective-permute-start(bf16[32,512]{1,0:T(8,128)(2,1)S(1)} %get-tuple-element.50), channel_id=1, source_target_pairs={{0,32},{16,48},{32,64},{48,80},{64,96},{80,112},{96,0},{112,16},{1... | collective-permute-start | bytes 98312 | tf_op jit(solution)/shard_map/ppermute | solution.py:489
  114.0 3.7 %collective-permute-start.4 = (bf16[32,512]{1,0:T(8,128)(2,1)S(1)}, bf16[32,512]{1,0:T(8,128)(2,1)S(1)}, u32[]{:S(2)}, u32[]{:S(2)}) collective-permute-start(bf16[32,512]{1,0:T(8,128)(2,1)S(1)} %get-tuple-element.49), channel_id=1, source_target_pairs={{0,48},{16,64},{32,80},{48,96},{64,112},{80,0},{96,16},{112,32},{1... | collective-permute-start | bytes 98312 | tf_op jit(solution)/shard_map/ppermute | solution.py:489
  118.2 3.4 %collective-permute-start.6 = (bf16[32,512]{1,0:T(8,128)(2,1)S(1)}, bf16[32,512]{1,0:T(8,128)(2,1)S(1)}, u32[]{:S(2)}, u32[]{:S(2)}) collective-permute-start(bf16[32,512]{1,0:T(8,128)(2,1)S(1)} %get-tuple-element.47), channel_id=1, source_target_pairs={{0,80},{16,96},{32,112},{48,0},{64,16},{80,32},{96,48},{112,64},{1... | collective-permute-start | bytes 98312 | tf_op jit(solution)/shard_map/ppermute | solution.py:489
  121.5 8.5 %collective-permute-done.2.rest_1_ = bf16[32,512]{1,0:T(8,128)(2,1)S(1)} collective-permute-done((bf16[32,512]{1,0:T(8,128)(2,1)S(1)}, bf16[32,512]{1,0:T(8,128)(2,1)S(1)}, u32[]{:S(2)}, u32[]{:S(2)}) %collective-permute-start.2) | collective-permute-done | bytes 32800 | tf_op jit(solution)/shard_map/ppermute | solution.py:489
  130.0 10.4 %collective-permute-start.7 = (bf16[32,512]{1,0:T(8,128)(2,1)S(1)}, bf16[32,512]{1,0:T(8,128)(2,1)S(1)}, u32[]{:S(2)}, u32[]{:S(2)}) collective-permute-start(bf16[32,512]{1,0:T(8,128)(2,1)S(1)} %get-tuple-element.46), channel_id=1, source_target_pairs={{0,96},{16,112},{32,0},{48,16},{64,32},{80,48},{96,64},{112,80},{1... | collective-permute-start | bytes 98312 | tf_op jit(solution)/shard_map/ppermute | solution.py:489
  140.4 1.6 collective-permute-start.8
  142.0 8.5 %grad_rows.1 = bf16[256,8192]{1,0:T(8,128)(2,1)} custom-call(s32[3]{0:T(128)} %pad_add_fusion.where.me, bf16[256,512]{1,0:T(8,128)(2,1)} %get-tuple-element.40.dv, bf16[8,512,512]{2,1,0:T(8,128)(2,1)} %bitcast.36, bf16[8,512,512]{2,1,0:T(8,128)(2,1)} %bitcast.38), custom_call_target="tpu_custom_call" | custom-call | flops 1 | bytes 1 | tf_op jit(solution)/shard_map/grad_rows/pallas_call | solution.py:320
  150.7 0.5 copy-done.4
  151.3 4.8 %attend.1 = bf16[256,4096]{1,0:T(8,128)(2,1)} custom-call(s32[8]{0:T(128)} %get-tuple-element.27.colours, s32[3]{0:T(128)} %pad_add_fusion.where.me, bf16[8,256,128]{2,1,0:T(8,128)(2,1)} %get-tuple-element.33.probs, bf16[32,512]{1,0:T(8,128)(2,1)} %get-tuple-element.52.rest_0_, bf16[32,512]{1,0:T(8,128)(2,1)} %copy-done.2, bf16[32,512]{1,0:T(8,128)(2,1)} %copy-done.3, ...), custom_call_target="tpu_custom_call" | custom-call | flops 1 | bytes 1 | tf_op jit(solution)/shard_map/attend/pallas_call | solution.py:379
  156.0 12.2 %all-to-all-done.2 = bf16[128,32,512]{2,1,0:T(8,128)(2,1)} async-done(((bf16[128,32,512]{2,1,0:T(8,128)(2,1)}), bf16[128,32,512]{2,1,0:T(8,128)(2,1)}, u32[]{:S(2)}, u32[]{:S(2)}) %all-to-all-start.2) | async-done | bytes 4194336 | tf_op jit(solution)/shard_map/all_to_all | solution.py:492
  168.3 7.3 %weight_product.1 = bf16[512,512]{1,0:T(8,128)(2,1)} custom-call(s32[3]{0:T(128)} %pad_add_fusion.where.me, bf16[8,2,8,32,512]{4,3,2,1,0:T(8,128)(2,1)} %bitcast.20.near_rows.far_rows, bf16[8,2,8,32,512]{4,3,2,1,0:T(8,128)(2,1)} %bitcast.20.near_rows.far_rows, bf16[8,512,256]{2,1,0:T(8,128)(2,1)} %bitcast.41, bf16[8,512,256]{2,1,0:T(8,128)(2,1)} %bitcast.40), custom_call_target="tpu_custom_call" | custom-call | flops 2147483648 | bytes 8912896 | tf_op jit(solution)/shard_map/weight_product/pallas_call | solution.py:423
  (34 shorter events, 0.8 us)
Async XLA Ops:
  7.2 92.1 %all-gather.9.cloned.1.call-start = ((), (), s32[]{:S(2)}) async-start(), calls=%async_computation.3 | async-start | bytes 4718592 | tf_op jit(solution)/shard_map/all_gather | solution.py:469
  7.9 23.6 %collective-permute-start = (bf16[512,512]{1,0:T(8,128)(2,1)}, bf16[512,512]{1,0:T(8,128)(2,1)S(1)}, u32[]{:S(2)}, u32[]{:S(2)}) collective-permute-start(bf16[512,512]{1,0:T(8,128)(2,1)} %param.17), channel_id=1, source_target_pairs={{0,8},{1,9},{2,10},{3,11},{4,12},{5,13},{6,14},{7,15},{8,0},{9,1},... | collective-permute-start | bytes 1572872 | tf_op jit(solution)/shard_map/ppermute | solution.py:464
  11.5 19.2 %all-to-all-start = ((f32[128,1,32]{2,1,0:T(1,128)}), f32[128,1,32]{2,1,0:T(1,128)S(1)}, u32[]{:S(2)}, u32[]{:S(2)}) async-start(f32[128,1,32]{2,1,0:T(1,128)} %bitcast.44), calls=%async_computation | async-start | bytes 131072 | tf_op jit(solution)/shard_map/all_to_all | solution.py:459
  21.8 77.5 %all-gather.11.cloned.1.call-start = ((), (), s32[]{:S(2)}) async-start(), calls=%async_computation.4 | async-start | bytes 4718592 | tf_op jit(solution)/shard_map/all_gather | solution.py:470
  31.5 0.8 copy-start
  32.3 54.8 %all-to-all-start.1 = ((bf16[8,512,512]{2,1,0:T(8,128)(2,1)}), bf16[8,512,512]{2,1,0:T(8,128)(2,1)}, u32[]{:S(2)}, u32[]{:S(2)}) async-start(bf16[8,512,512]{2,1,0:T(8,128)(2,1)} %bitcast.39), calls=%async_computation.1 | async-start | bytes 8388608 | tf_op jit(solution)/shard_map/all_to_all | solution.py:466
  36.9 131.4 %all-gather.15.cloned.1.call-start = ((), (), s32[]{:S(2)}) async-start(), calls=%async_computation.6 | async-start | bytes 2359296 | tf_op jit(solution)/shard_map/all_gather | solution.py:481
  48.9 42.5 %collective-permute-start.1 = (bf16[512,256]{1,0:T(8,128)(2,1)}, bf16[512,256]{1,0:T(8,128)(2,1)S(1)}, u32[]{:S(2)}, u32[]{:S(2)}) collective-permute-start(bf16[512,256]{1,0:T(8,128)(2,1)} %get-tuple-element.43), channel_id=1, source_target_pairs={{0,8},{1,9},{2,10},{3,11},{4,12},{5,13},{6,14},{7,15},{8,0},{9,1},... | collective-permute-start | bytes 786440 | tf_op jit(solution)/shard_map/ppermute | solution.py:476
  91.4 0.7 copy-start.1
  92.1 76.2 %all-to-all-start.2 = ((bf16[128,32,512]{2,1,0:T(8,128)(2,1)}), bf16[128,32,512]{2,1,0:T(8,128)(2,1)}, u32[]{:S(2)}, u32[]{:S(2)}) async-start(bf16[128,32,512]{2,1,0:T(8,128)(2,1)} %bitcast.33), calls=%async_computation.2 | async-start | bytes 8388608 | tf_op jit(solution)/shard_map/all_to_all | solution.py:492
  99.2 69.0 %all-gather.13.cloned.1.call-start = ((), (), s32[]{:S(2)}) async-start(), calls=%async_computation.5 | async-start | bytes 2359296 | tf_op jit(solution)/shard_map/all_gather | solution.py:480
  109.3 20.7 %collective-permute-start.2 = (bf16[32,512]{1,0:T(8,128)(2,1)S(1)}, bf16[32,512]{1,0:T(8,128)(2,1)S(1)}, u32[]{:S(2)}, u32[]{:S(2)}) collective-permute-start(bf16[32,512]{1,0:T(8,128)(2,1)S(1)} %get-tuple-element.51), channel_id=1, source_target_pairs={{0,16},{16,32},{32,48},{48,64},{64,80},{80,96},{96,112},{112,0},{1... | collective-permute-start | bytes 98312 | tf_op jit(solution)/shard_map/ppermute | solution.py:489
  110.9 29.5 %collective-permute-start.3 = (bf16[32,512]{1,0:T(8,128)(2,1)S(1)}, bf16[32,512]{1,0:T(8,128)(2,1)S(1)}, u32[]{:S(2)}, u32[]{:S(2)}) collective-permute-start(bf16[32,512]{1,0:T(8,128)(2,1)S(1)} %get-tuple-element.50), channel_id=1, source_target_pairs={{0,32},{16,48},{32,64},{48,80},{64,96},{80,112},{96,0},{112,16},{1... | collective-permute-start | bytes 98312 | tf_op jit(solution)/shard_map/ppermute | solution.py:489
  114.0 36.6 %collective-permute-start.4 = (bf16[32,512]{1,0:T(8,128)(2,1)S(1)}, bf16[32,512]{1,0:T(8,128)(2,1)S(1)}, u32[]{:S(2)}, u32[]{:S(2)}) collective-permute-start(bf16[32,512]{1,0:T(8,128)(2,1)S(1)} %get-tuple-element.49), channel_id=1, source_target_pairs={{0,48},{16,64},{32,80},{48,96},{64,112},{80,0},{96,16},{112,32},{1... | collective-permute-start | bytes 98312 | tf_op jit(solution)/shard_map/ppermute | solution.py:489
  117.7 32.9 %collective-permute-start.5 = (bf16[32,512]{1,0:T(8,128)(2,1)S(1)}, bf16[32,512]{1,0:T(8,128)(2,1)S(1)}, u32[]{:S(2)}, u32[]{:S(2)}) collective-permute-start(bf16[32,512]{1,0:T(8,128)(2,1)S(1)} %get-tuple-element.48), channel_id=1, source_target_pairs={{0,64},{16,80},{32,96},{48,112},{64,0},{80,16},{96,32},{112,48},{1... | collective-permute-start | bytes 98312 | tf_op jit(solution)/shard_map/ppermute | solution.py:489
  118.2 32.4 %collective-permute-start.6 = (bf16[32,512]{1,0:T(8,128)(2,1)S(1)}, bf16[32,512]{1,0:T(8,128)(2,1)S(1)}, u32[]{:S(2)}, u32[]{:S(2)}) collective-permute-start(bf16[32,512]{1,0:T(8,128)(2,1)S(1)} %get-tuple-element.47), channel_id=1, source_target_pairs={{0,80},{16,96},{32,112},{48,0},{64,16},{80,32},{96,48},{112,64},{1... | collective-permute-start | bytes 98312 | tf_op jit(solution)/shard_map/ppermute | solution.py:489
  130.0 20.6 %copy-start.2 = (bf16[32,512]{1,0:T(8,128)(2,1)}, bf16[32,512]{1,0:T(8,128)(2,1)S(1)}, u32[]{:S(2)}) copy-start(bf16[32,512]{1,0:T(8,128)(2,1)S(1)} %collective-permute-done.2.rest_1_) | copy-start | bytes 98308
  130.0 20.6 %collective-permute-start.7 = (bf16[32,512]{1,0:T(8,128)(2,1)S(1)}, bf16[32,512]{1,0:T(8,128)(2,1)S(1)}, u32[]{:S(2)}, u32[]{:S(2)}) collective-permute-start(bf16[32,512]{1,0:T(8,128)(2,1)S(1)} %get-tuple-element.46), channel_id=1, source_target_pairs={{0,96},{16,112},{32,0},{48,16},{64,32},{80,48},{96,64},{112,80},{1... | collective-permute-start | bytes 98312 | tf_op jit(solution)/shard_map/ppermute | solution.py:489
  140.4 10.1 %copy-start.3 = (bf16[32,512]{1,0:T(8,128)(2,1)}, bf16[32,512]{1,0:T(8,128)(2,1)S(1)}, u32[]{:S(2)}) copy-start(bf16[32,512]{1,0:T(8,128)(2,1)S(1)} %collective-permute-done.3.rest_2_) | copy-start | bytes 98308
  140.4 10.2 %collective-permute-start.8 = (bf16[32,512]{1,0:T(8,128)(2,1)S(1)}, bf16[32,512]{1,0:T(8,128)(2,1)S(1)}, u32[]{:S(2)}, u32[]{:S(2)}) collective-permute-start(bf16[32,512]{1,0:T(8,128)(2,1)S(1)} %get-tuple-element.45), channel_id=1, source_target_pairs={{0,112},{16,0},{32,16},{48,32},{64,48},{80,64},{96,80},{112,96},{1... | collective-permute-start | bytes 98312 | tf_op jit(solution)/shard_map/ppermute | solution.py:489
  150.6 0.6 copy-start.4
  150.6 0.6 copy-start.5
  150.6 0.6 copy-start.6
  150.7 0.6 copy-start.7
  150.7 0.6 copy-start.8
Sparse Core Ops, SparseCore 0:
  9.7 33.7 all-gather.8
  45.8 31.9 all-gather.10
  92.2 37.6 all-gather.14
  131.4 32.4 all-gather.12

commit v2 on v1

--- a/solution.py
+++ b/solution.py
@@ -15,7 +15,7 @@
     return pltpu.CompilerParams(vmem_limit_bytes=VMEM, **kw)
 
 
-def prepare_body(slots, dp, fsdp, where, packing, lengths, rewards, groups, info, order):
+def prepare_body(slots, dp, fsdp, packing, lengths, rewards, groups, info, order):
     lane = lax.broadcasted_iota(jnp.int32, info.shape, 1)
     told = jnp.zeros(info.shape, jnp.float32)
     for r in range(slots):
@@ -24,7 +24,7 @@
         told = jnp.where(lane == 2 * slots + r, rewards[r], told)
         told = jnp.where(lane == 3 * slots + r, groups[r].astype(jnp.float32), told)
     info[...] = told
-    home = where[1]
+    home = lax.axis_index("dp")
     offsets = [lax.rem(lax.div(packing[r], slots * fsdp) - home + dp, dp) for r in range(slots)]
     mine = jnp.int32(0)
     for r in range(slots):
@@ -38,19 +38,19 @@
     order[slots] = mine
 
 
-def prepare(where, packing, lengths, rewards, groups, dp, fsdp):
+def prepare(packing, lengths, rewards, groups, dp, fsdp):
     slots = packing.shape[0]
     smem = pl.BlockSpec(memory_space=pltpu.SMEM)
     return pl.pallas_call(
         functools.partial(prepare_body, slots, dp, fsdp),
-        in_specs=[smem] * 5,
+        in_specs=[smem] * 4,
         out_specs=[pl.BlockSpec(memory_space=pltpu.VMEM), smem],
         out_shape=[
             jax.ShapeDtypeStruct((dp * fsdp, 4 * slots), jnp.float32),
             jax.ShapeDtypeStruct((slots + 1,), jnp.int32),
         ],
         name="prepare",
-    )(where, packing, lengths, rewards, groups)
+    )(packing, lengths, rewards, groups)
 
 
 def pack_body(fsdp, order, rows, out, held, cut, arrive, leave):
@@ -58,12 +58,13 @@
     part = width // fsdp
     ins = [pltpu.make_async_copy(rows.at[r], held.at[r], arrive.at[r]) for r in range(slots)]
     outs = [pltpu.make_async_copy(cut.at[r], out.at[order[r]], leave.at[r]) for r in range(slots)]
+    half = fsdp // 2
     for copy in ins:
         copy.start()
     for r in range(slots):
         ins[r].wait()
         for f in range(fsdp):
-            cut[r, f] = held[r, :, f * part : (f + 1) * part]
+            cut[r, f % half * 2 + f // half] = held[r, :, f * part : (f + 1) * part]
         outs[r].start()
     for copy in outs:
         copy.wait()
@@ -127,10 +128,11 @@
 
 
 def plan_body(slots, dp, fsdp, seq, me, info, length, colours, factor):
-    packing = info[0:slots, :]
-    lengths = info[slots : 2 * slots, :]
-    rewards = info[2 * slots : 3 * slots, :]
-    groups = info[3 * slots : 4 * slots, :]
+    told = info[...].T
+    packing = told[0:slots, :]
+    lengths = told[slots : 2 * slots, :]
+    rewards = told[2 * slots : 3 * slots, :]
+    groups = told[3 * slots : 4 * slots, :]
     lane = lax.broadcasted_iota(jnp.int32, packing.shape, 1)
     row = lax.broadcasted_iota(jnp.int32, packing.shape, 0)
     target = lax.div(packing.astype(jnp.int32), slots * fsdp)
@@ -249,14 +251,20 @@
     )(length, colours, factor, queries, keys, out_grad)
 
 
-def values_body(steps, where, rows, near, far, out, acc):
+def values_body(steps, where, rows, *rest):
+    weights, out, acc = rest[:4], rest[4], rest[5]
     step = pl.program_id(0)
-    dp, _, low, seq, part = rows.shape
-    total = jnp.zeros(acc.shape, jnp.float32)
-    for c in range(low):
-        for w, h in ((near, where[2]), (far, 1 - where[2])):
-            x = rows[:, h, c].reshape(dp * seq, part)
-            total += jnp.dot(x, w[c], preferred_element_type=jnp.float32)
+    dp, _, _, _, seq, part = rows.shape
+    lhs, rhs = [], []
+    for n, w in enumerate(weights):
+        x = rows[:, 0, lax.rem(where[4] + n // 2, 2), lax.rem(where[2] + n % 2, 2)]
+        lhs.append(x.reshape(dp * seq, part))
+        rhs.append(w[0])
+    total = jnp.dot(
+        jnp.concatenate(lhs, axis=1),
+        jnp.concatenate(rhs, axis=0),
+        preferred_element_type=jnp.float32,
+    )
 
     @pl.when(step == 0)
     def _():
@@ -271,18 +279,21 @@
         out[...] = acc[...].astype(out.dtype).reshape(out.shape)
 
 
-def values_of(where, rows, near, far):
-    dp, high, low, seq, part = rows.shape
-    cols = near.shape[2]
-    each = 2
-    steps = low // each
-    return pl.pallas_call(
-        functools.partial(values_body, steps),
+def values_of(where, rows, weights):
+    dp, around, cores, high, seq, part = rows.shape
+    cols = weights[0].shape[2]
+    return pl.pallas_call(
+        functools.partial(values_body, around),
         grid_spec=pltpu.PrefetchScalarGridSpec(
             num_scalar_prefetch=1,
-            grid=(steps,),
-            in_specs=[pl.BlockSpec((dp, high, each, seq, part), lambda i, n: (0, 0, i, 0, 0))]
-            + [pl.BlockSpec((each, part, cols), lambda i, n: (i, 0, 0))] * 2,
+            grid=(around,),
+            in_specs=[
+                pl.BlockSpec(
+                    (dp, 1, cores, high, seq, part),
+                    lambda i, n: (0, lax.rem(n[3] - i + around, around), 0, 0, 0, 0),
+                )
+            ]
+            + [pl.BlockSpec((1, part, cols), lambda i, n: (i, 0, 0))] * 4,
             out_specs=pl.BlockSpec((dp, seq, cols), lambda i, n: (0, 0, 0)),
             scratch_shapes=[pltpu.VMEM((dp * seq, cols), jnp.float32)],
         ),
@@ -290,67 +301,70 @@
         compiler_params=params(),
         cost_estimate=pl.CostEstimate(flops=1, bytes_accessed=1, transcendentals=0),
         name="values",
-    )(where, rows, near, far)
-
-
-def grad_rows_body(where, dv, near, far, out):
-    each, part, _ = near.shape
+    )(where, rows, *weights)
+
+
+def grad_rows_body(where, dv, *rest):
+    weights, outs = rest[:4], rest[4]
+    part = weights[0].shape[1]
     half = pl.program_id(0)
 
-    def write(w):
-        for c in range(each):
-            out[:, c * part : (c + 1) * part] = lax.dot_general(
-                dv[...], w[c], (((1,), (1,)), ((), ())), preferred_element_type=jnp.float32
-            ).astype(out.dtype)
-
-    @pl.when(half == 0)
-    def _():
-        write(near)
-
-    @pl.when(half == 1)
-    def _():
-        write(far)
-
-
-def grad_rows_of(where, dv, near, far):
+    def write(first, second):
+        for c, w in enumerate((first, second)):
+            outs[:, c * part : (c + 1) * part] = lax.dot_general(
+                dv[...], w[0], (((1,), (1,)), ((), ())), preferred_element_type=jnp.float32
+            ).astype(outs.dtype)
+
+    for h in range(2):
+        for c in range(2):
+
+            @pl.when((half == h) & (where[4] == c))
+            def _(h=h, c=c):
+                write(weights[2 * c + h], weights[2 * (1 - c) + h])
+
+
+def grad_rows_of(where, dv, weights):
     tokens, cols = dv.shape
-    low, part, _ = near.shape
-    each = 4
-    steps = low // each
+    around, part, _ = weights[0].shape
+    last = around - 1
+    near = pl.BlockSpec((1, part, cols), lambda h, i, n: (i * (1 - h) + last * h, 0, 0))
+    far = pl.BlockSpec((1, part, cols), lambda h, i, n: (i * h, 0, 0))
     return pl.pallas_call(
         grad_rows_body,
         grid_spec=pltpu.PrefetchScalarGridSpec(
             num_scalar_prefetch=1,
-            grid=(2, steps),
-            in_specs=[
-                pl.BlockSpec((tokens, cols), lambda h, i, n: (0, 0)),
-                pl.BlockSpec((each, part, cols), lambda h, i, n: (i * (1 - h) + (steps - 1) * h, 0, 0)),
-                pl.BlockSpec((each, part, cols), lambda h, i, n: (i * h, 0, 0)),
-            ],
+            grid=(2, around),
+            in_specs=[pl.BlockSpec((tokens, cols), lambda h, i, n: (0, 0)), near, far, near, far],
             out_specs=pl.BlockSpec(
-                (tokens, each * part), lambda h, i, n: (0, lax.rem(n[2] + h, 2) * steps + i)
+                (tokens, 2 * part),
+                lambda h, i, n: (
+                    0,
+                    lax.rem(n[2] + h, 2) * around + lax.rem(n[3] - i + around, around),
+                ),
             ),
         ),
-        out_shape=jax.ShapeDtypeStruct((tokens, 2 * low * part), jnp.bfloat16),
+        out_shape=jax.ShapeDtypeStruct((tokens, 4 * around * part), jnp.bfloat16),
         compiler_params=params(),
         cost_estimate=pl.CostEstimate(flops=1, bytes_accessed=1, transcendentals=0),
         name="grad_rows",
-    )(where, dv, near, far)
-
-
-def attend_body(kv, group, dp, each, colours, where, probs, *rest):
-    values, out, held = rest[:dp], rest[dp], rest[dp + 1]
+    )(where, dv, *weights)
+
+
+def attend_body(kv, group, levels, each, colours, where, probs, *rest):
+    values, out, held = rest[:levels], rest[levels], rest[levels + 1]
     step = pl.program_id(0)
-    seq, cols = values[0].shape
+    _, seq, cols = values[0].shape
 
     @pl.when(step == 0)
     def _():
-        for k in range(dp):
-            held[k] = values[k][...]
+        for k in range(levels):
+            held[2 * k : 2 * k + 2] = values[k][...]
 
     for e in range(each):
-        away = lax.rem(where[1] - colours[step * each + e] + dp, dp)
-        mine = held[away]
+        colour = colours[step * each + e]
+        away = lax.rem(where[1] - colour + 2 * levels, levels)
+        other = lax.rem(lax.div(where[1], levels) + lax.div(colour, levels), 2)
+        mine = held[2 * away + other]
         zero = jnp.zeros((seq, HD), mine.dtype)
         blocks = []
         for kh in range(kv):
@@ -370,21 +384,21 @@
 
 def attend(colours, where, probs, values):
     slots, span, keys = probs.shape
-    seq, cols = values[0].shape
+    _, seq, cols = values[0].shape
     kv = cols // HD
     group = span // seq
     width = kv * group * HD
-    dp = len(values)
+    levels = len(values)
     each = 2
     return pl.pallas_call(
-        functools.partial(attend_body, kv, group, dp, each),
+        functools.partial(attend_body, kv, group, levels, each),
         grid_spec=pltpu.PrefetchScalarGridSpec(
             num_scalar_prefetch=2,
             grid=(slots // each,),
             in_specs=[pl.BlockSpec((each, span, keys), lambda s, c, w: (s, 0, 0))]
-            + [pl.BlockSpec((seq, cols), lambda s, c, w: (0, 0))] * dp,
+            + [pl.BlockSpec((2, seq, cols), lambda s, c, w: (0, 0, 0))] * levels,
             out_specs=pl.BlockSpec((each * seq, width), lambda s, c, w: (s, 0)),
-            scratch_shapes=[pltpu.VMEM((dp, seq, cols), jnp.bfloat16)],
+            scratch_shapes=[pltpu.VMEM((2 * levels, seq, cols), jnp.bfloat16)],
         ),
         out_shape=jax.ShapeDtypeStruct((slots * seq, width), jnp.bfloat16),
         compiler_params=params(),
@@ -393,56 +407,69 @@
     )(colours, where, probs, *values)
 
 
-def product_body(steps, scale, where, near_rows, far_rows, near, far, out, acc):
-    step = pl.program_id(0)
-    colours, _, each, seq, width = near_rows.shape
-    part = jnp.zeros(acc.shape, jnp.float32)
-    for rows, dv in ((near_rows, near), (far_rows, far)):
-        for b in range(each):
-            x = rows[:, 0, b].reshape(colours * seq, width)
-            part += jnp.dot(dv[b], x, preferred_element_type=jnp.float32)
-
-    @pl.when(step == 0)
-    def _():
-        acc[...] = part
-
-    @pl.when(step > 0)
-    def _():
-        acc[...] += part
-
-    @pl.when(step == steps - 1)
-    def _():
-        out[...] = (acc[...] * scale).T.astype(out.dtype)
-
-
-def product(where, rows, near, far, scale):
-    colours, _, low, seq, width = rows.shape
-    cols = near.shape[1]
-    each = 2
-    steps = low // each
-    return pl.pallas_call(
-        functools.partial(product_body, steps, scale),
+def product_body(scale, where, rows, near, far, out):
+    colours, around, _, _, seq, width = rows.shape
+    lhs, rhs = [], []
+    for k in range(around):
+        for other, dv in enumerate((near, far)):
+            x = rows[:, lax.rem(where[3] - k + around, around), lax.rem(where[4] + other, 2), 0]
+            rhs.append(x.reshape(colours * seq, width))
+            lhs.append(dv[k])
+    part = jnp.dot(
+        jnp.concatenate(lhs, axis=1),
+        jnp.concatenate(rhs, axis=0),
+        preferred_element_type=jnp.float32,
+    )
+    out[...] = (part * scale).T.astype(out.dtype)
+
+
+def product(where, rows, near, far, scale, apart, dtype):
+    colours, around, cores, high, seq, width = rows.shape
+    _, cols, tokens = near.shape
+    return pl.pallas_call(
+        functools.partial(product_body, scale),
         grid_spec=pltpu.PrefetchScalarGridSpec(
             num_scalar_prefetch=1,
-            grid=(steps,),
+            grid=(1,),
             in_specs=[
-                pl.BlockSpec((colours, 1, each, seq, width), lambda i, n: (0, n[2], i, 0, 0)),
-                pl.BlockSpec((colours, 1, each, seq, width), lambda i, n: (0, 1 - n[2], i, 0, 0)),
-                pl.BlockSpec((each, cols, colours * seq), lambda i, n: (i, 0, 0)),
-                pl.BlockSpec((each, cols, colours * seq), lambda i, n: (i, 0, 0)),
-            ],
+                pl.BlockSpec(
+                    (colours, around, cores, 1, seq, width),
+                    lambda i, n: (0, 0, 0, lax.rem(n[2] + apart, high), 0, 0),
+                )
+            ]
+            + [pl.BlockSpec((around, cols, tokens), lambda i, n: (0, 0, 0))] * 2,
             out_specs=pl.BlockSpec((width, cols), lambda i, n: (0, 0)),
-            scratch_shapes=[pltpu.VMEM((cols, width), jnp.float32)],
-        ),
-        out_shape=jax.ShapeDtypeStruct((width, cols), jnp.bfloat16),
-        compiler_params=params(),
-        cost_estimate=pl.CostEstimate(
-            flops=2 * rows.size * cols,
-            bytes_accessed=2 * (2 * rows.size + width * cols),
-            transcendentals=0,
-        ),
+        ),
+        out_shape=jax.ShapeDtypeStruct((width, cols), dtype),
+        compiler_params=params(),
+        cost_estimate=pl.CostEstimate(flops=1, bytes_accessed=1, transcendentals=0),
         name="weight_product",
-    )(where, rows, rows, near, far)
+    )(where, rows, near, far)
+
+
+def swap_rows(x, fsdp):
+    return lax.ppermute(x, "fsdp", [(i, (i + fsdp // 2) % fsdp) for i in range(fsdp)])
+
+
+def step_along(x, fsdp, step):
+    half = fsdp // 2
+    to = [(i, i // half * half + (i + 2 * step) % half) for i in range(fsdp)]
+    return lax.ppermute(x, "fsdp", to)
+
+
+def neighbours(x, fsdp):
+    return step_along(x, fsdp, 1), step_along(x, fsdp, -1)
+
+
+def opposite(back, front, fsdp):
+    middle = back.shape[0] // 2
+    return jnp.concatenate(
+        [step_along(back[:middle], fsdp, 1), step_along(front[middle:], fsdp, -1)], axis=0
+    )
+
+
+def swap_cores(x, fsdp):
+    return lax.ppermute(x, "fsdp", [(i, i ^ 1) for i in range(fsdp)])
 
 
 def shards(
@@ -454,53 +481,78 @@
     part = width // fsdp
     home = lax.axis_index("dp")
     place = lax.axis_index("fsdp")
-    where = jnp.stack([home * fsdp + place, home, lax.div(place, fsdp // 2)]).astype(jnp.int32)
-    info, order = prepare(where, packing, lengths, rewards, group_ids, dp, fsdp)
+    around = fsdp // 4
+    where = jnp.stack(
+        [home * fsdp + place, home, place // (2 * around), place // 2 % around, place % 2]
+    ).astype(jnp.int32)
+    info, order = prepare(packing, lengths, rewards, group_ids, dp, fsdp)
     info = lax.all_to_all(info, ("dp", "fsdp"), split_axis=0, concat_axis=0, tiled=True)
     rows = pack(order, rollout_rows, fsdp)
-    low = fsdp // 2
-    halves = [list(range(low)), list(range(low, fsdp))]
-    swap = [(i, (i + low) % fsdp) for i in range(fsdp)]
-    far_weight = lax.ppermute(value_weight, "fsdp", swap)
-    rows, info, far_weight = lax.optimization_barrier((rows, info, far_weight))
+    across = swap_rows(value_weight, fsdp)
+    back, front = neighbours(value_weight, fsdp)
+    rows, info, across, back, front = lax.optimization_barrier(
+        (rows, info, across, back, front)
+    )
     rows = lax.all_to_all(
         rows.reshape(dp, fsdp * seq, part), "dp", split_axis=0, concat_axis=0, tiled=True
     )
-    near = lax.all_gather(value_weight, "fsdp", axis_index_groups=halves)
-    far = lax.all_gather(far_weight, "fsdp", axis_index_groups=halves)
-    length, colours, factor = plan(where, info.T, slots, dp, fsdp, seq)
-    dvalues, coloured, probs = probs_and_dvalues(
+    own = [value_weight, back, opposite(back, front, fsdp), front]
+    across_back, across_front = neighbours(across, fsdp)
+    length, colours, factor = plan(where, info, slots, dp, fsdp, seq)
+    dvalues, turned, probs = probs_and_dvalues(
         length, colours, factor, queries, keys, out_grad, slots
     )
-    rows, dvalues, probs = lax.optimization_barrier((rows, dvalues, probs))
-    far_dv = lax.ppermute(coloured, "fsdp", swap)
+    dv_back, dv_front = neighbours(turned, fsdp)
+    across_way = opposite(across_back, across_front, fsdp)
+    across = [across, across_back, across_way, across_front]
+    own, dvalues = lax.optimization_barrier((own, dvalues))
+    own = jnp.stack(own)
+    own_far = swap_cores(own, fsdp)
+    across = jnp.stack(across)
+    across_far = swap_cores(across, fsdp)
+    weights = (own, across, own_far, across_far)
+    near_dv = jnp.stack([turned, dv_back, opposite(dv_back, dv_front, fsdp), dv_front])
+    far_dv = swap_cores(near_dv, fsdp)
+    rows, dvalues, probs, weights, near_dv, far_dv = lax.optimization_barrier(
+        (rows, dvalues, probs, weights, near_dv, far_dv)
+    )
     rows = turn(order, rows)
-    rows, far_dv = lax.optimization_barrier((rows, far_dv))
-    coloured, near, far = lax.optimization_barrier((coloured, near, far))
-    near_dv = lax.all_gather(coloured, "fsdp", axis_index_groups=halves)
-    far_dv = lax.all_gather(far_dv, "fsdp", axis_index_groups=halves)
-    values = values_of(where, rows.reshape(dp, 2, low, seq, part), near, far)
-    grad_rows = grad_rows_of(where, dvalues, near, far)
-    held = [
-        lax.dynamic_index_in_dim(values, lax.rem(home + k, dp), 0, keepdims=False)
-        for k in range(dp)
+    half = fsdp // 2
+    groups = [
+        [d * fsdp + h * half + i for d in range(dp) for i in range(half)] for h in range(2)
     ]
-    held = [held[0]] + [
-        lax.ppermute(held[k], "dp", [(i, (i + k) % dp) for i in range(dp)])
-        for k in range(1, dp)
-    ]
+    sent = rows
     rows = lax.all_to_all(
-        rows.reshape(dp * fsdp, seq, part),
+        rows.reshape(dp * half, 2 * seq, part),
         ("dp", "fsdp"),
         split_axis=0,
         concat_axis=0,
+        axis_index_groups=groups,
         tiled=True,
-    )
-    rows, grad_rows = lax.optimization_barrier((rows, grad_rows))
-    grad_weight = product(
-        where, rows.reshape(dp, 2, low, seq, part), near_dv, far_dv, 1.0 / fsdp
-    )[None]
+    ).reshape(dp, around, 2, 2, seq, part)
+    grad_rows = grad_rows_of(where, dvalues, weights)
+    sent, grad_rows = lax.optimization_barrier((sent, grad_rows))
+    values = values_of(where, sent.reshape(dp, around, 2, 2, seq, part), weights)
+    side, level = home // 4, home % 4
+    keep = lax.dynamic_slice_in_dim(values, side * 4, 4, 0)
+    give = lax.dynamic_slice_in_dim(values, (1 - side) * 4, 4, 0)
+    got = lax.ppermute(give, "dp", [(i, (i + 4) % dp) for i in range(dp)])
+    rows, got = lax.optimization_barrier((rows, got))
+    both = [
+        jnp.stack([lax.dynamic_index_in_dim(v, (level + k) % 4, 0, False) for v in (keep, got)])
+        for k in range(4)
+    ]
+    held = [both[0]] + [
+        lax.ppermute(both[k], "dp", [(i, i // 4 * 4 + (i + k) % 4) for i in range(dp)])
+        for k in range(1, 4)
+    ]
+    given = product(where, rows, near_dv, far_dv, 1.0 / fsdp, 1, jnp.bfloat16)
+    rows, given = lax.optimization_barrier((rows, given))
+    given = swap_rows(given, fsdp)
+    own = product(where, rows, near_dv, far_dv, 1.0 / fsdp, 0, jnp.float32)
     attn_out = attend(colours, where, probs, held)
+    given, own, attn_out = lax.optimization_barrier((given, own, attn_out))
+    grad_weight = (own + given.astype(jnp.float32)).astype(jnp.bfloat16)[None]
     return (attn_out, grad_rows, grad_weight)
 
 

time: 184 us -> 178 us (0.967)
  between operations: 14 us -> 0.99 us
  waiting for transfers between devices: 63.9 us -> 54.6 us
  starting transfers between devices: 48.7 us -> 56.1 us
  Pallas kernels: 50.6 us -> 54.8 us
  other arithmetic: 0.62 us -> 3.38 us
  local copies, waits for them, and re-layouts: 4.27 us -> 6.61 us
    ppermute x9 -> x21, waiting for transfers between devices: 8.51 us -> 49.2 us  [the longest x1 32 us: shards(): got = lax.ppermute(give, 'dp', [(i, (i + 4) % dp) for i in range(dp)])]
    all_to_all x1, waiting for transfers between devices: 37.5 us -> 0.65 us  [shards(): lax.all_to_all(rows.reshape(dp, fsdp * seq, part), 'dp', split_axis=0, co...]
    all_to_all x1, waiting for transfers between devices: 12.2 us -> 0.01 us  [shards(): lax.all_to_all(rows.reshape(dp * half, 2 * seq, part), ('dp', 'fsdp'), sp...]
    all_to_all x1, starting transfers between devices: 7.15 us -> 11.6 us  [shards(): lax.all_to_all(rows.reshape(dp * half, 2 * seq, part), ('dp', 'fsdp'), sp...]
    ppermute x9 -> x21, starting transfers between devices: 26.6 us -> 29.7 us  [the longest x12 16 us: step_along(): return lax.ppermute(x, 'fsdp', to)]
    pallas_call x3 -> x4, Pallas kernels: 20 us -> 22.8 us  [the longest x2 10.3 us: product(): pl.pallas_call(functools.partial(product_body, scale), grid_spec=pltpu.Pr...]
  transfers between devices with their start and end apart: 16 -> 24, of which waited for: 4 -> 9; matrix products, arithmetic and copies ran while one was open for 2% -> 3% of each run, Pallas kernels for 24% -> 26%
where the time goes in v2:
time: 178 us; the launch traced here: 177 us
  starting transfers between devices  56.1 us (32%)
  Pallas kernels  54.8 us (31%)
  waiting for transfers between devices  54.6 us (31%)
  local copies, waits for them, and re-layouts  6.61 us (4%)
  other arithmetic  3.38 us (2%)
    ppermute x1, waiting for transfers between devices, shards(): got = lax.ppermute(give, 'dp', [(i, (i + 4) % dp) for i in range(dp)])  32 us
    ppermute x12, starting transfers between devices, step_along(): return lax.ppermute(x, 'fsdp', to)  16 us
    ppermute x12, waiting for transfers between devices, step_along(): return lax.ppermute(x, 'fsdp', to)  14.5 us
    all_to_all x1, starting transfers between devices, shards(): lax.all_to_all(rows.reshape(dp * half, 2 * seq, part), ('dp', 'fsdp'), sp...  11.6 us
    pallas_call x1, Pallas kernels, probs_and_dvalues(): pl.pallas_call(functools.partial(probs_body, kv, group, slots), grid_spec...  10.4 us
    pallas_call x2, Pallas kernels, product(): pl.pallas_call(functools.partial(product_body, scale), grid_spec=pltpu.Pr...  10.3 us
    all_to_all x1, starting transfers between devices, shards(): lax.all_to_all(info, ('dp', 'fsdp'), split_axis=0, concat_axis=0, tiled=T...  10.2 us
    pallas_call x1, Pallas kernels, grad_rows_of(): pl.pallas_call(grad_rows_body, grid_spec=pltpu.PrefetchScalarGridSpec(num...  9.97 us
  transfers between devices with their start and end apart: 24, of which 9 were waited for; matrix products, arithmetic and copies ran while one was open for 3% of the time, Pallas kernels for 26%

profile of v2, /device:TPU:2, one launch (start us, length us, event | category | flops | bytes accessed | tf_op | source)
XLA Modules:
  0.0 176.5 jit_solution(7101139198399169466)
XLA Ops:
  0.6 1.7 collective-permute-start
  2.3 1.5 collective-permute-start.1
  4.3 1.4 prepare.1
  5.7 10.2 %all-to-all-start = ((f32[128,1,32]{2,1,0:T(1,128)}), f32[128,1,32]{2,1,0:T(1,128)S(1)}, u32[]{:S(2)}, u32[]{:S(2)}) async-start(f32[128,1,32]{2,1,0:T(1,128)} %bitcast.43), calls=%async_computation | async-start | bytes 131072 | tf_op jit(solution)/shard_map/all_to_all | solution.py:489
  15.9 4.2 %pack_rows.1 = bf16[8,16,32,512]{3,2,1,0:T(8,128)(2,1)} custom-call(s32[9]{0:T(128)} %get-tuple-element.39.order, bf16[8,32,8192]{2,1,0:T(8,128)(2,1)} %rows.1), custom_call_target="tpu_custom_call" | custom-call | bytes 8388608 | tf_op jit(solution)/shard_map/pack_rows/pallas_call | solution.py:76
  20.1 4.8 %all-to-all-done = f32[128,1,32]{2,1,0:T(1,128)S(1)} async-done(((f32[128,1,32]{2,1,0:T(1,128)}), f32[128,1,32]{2,1,0:T(1,128)S(1)}, u32[]{:S(2)}, u32[]{:S(2)}) %all-to-all-start) | async-done | bytes 16416 | tf_op jit(solution)/shard_map/all_to_all | solution.py:489
  25.5 4.5 %all-to-all-start.1 = ((bf16[8,512,512]{2,1,0:T(8,128)(2,1)}), bf16[8,512,512]{2,1,0:T(8,128)(2,1)}, u32[]{:S(2)}, u32[]{:S(2)}) async-start(bf16[8,512,512]{2,1,0:T(8,128)(2,1)} %bitcast.31), calls=%async_computation.1 | async-start | bytes 8388608 | tf_op jit(solution)/shard_map/all_to_all | solution.py:496
  30.6 1.6 collective-permute-start.7
  33.4 2.2 %collective-permute-start.4 = (bf16[256,512]{1,0:T(8,128)(2,1)}, bf16[256,512]{1,0:T(8,128)(2,1)}, u32[]{:S(2)}, u32[]{:S(2)}) collective-permute-start(bf16[256,512]{1,0:T(8,128)(2,1)} %slice.19), channel_id=1, source_target_pairs={{0,6},{1,7},{2,0},{3,1},{4,2},{5,3},{6,4},{7,5},{8,14},{9,15},{10,... | collective-permute-start | bytes 786440 | tf_op jit(solution)/shard_map/ppermute | solution.py:457
  36.3 1.7 plan_slots.1
  38.1 10.4 %probs_dvalues.1 = (bf16[256,512]{1,0:T(8,128)(2,1)}, bf16[512,256]{1,0:T(8,128)(2,1)}, bf16[8,256,128]{2,1,0:T(8,128)(2,1)}) custom-call(s32[8]{0:T(128)} %get-tuple-element.45.length, s32[8]{0:T(128)} %get-tuple-element.46.colours, f32[8,128]{1,0:T(8,128)} %get-tuple-element.47.factor, bf16[256,4096]{1,0:T(8,128)(2,1)} %q.1, bf16[256,512]{1,0:T(8,128)(2,1)} %k.1, ...), custom_call_target="tpu_custom_call" | custom-call | flops 1 | bytes 1 | tf_op jit(solution)/shard_map/probs_dvalues/pallas_call | solution.py:225
  48.7 3.3 %collective-permute-start.8 = (bf16[256,512]{1,0:T(8,128)(2,1)S(1)}, bf16[256,512]{1,0:T(8,128)(2,1)S(1)}, u32[]{:S(2)}, u32[]{:S(2)}) collective-permute-start(bf16[256,512]{1,0:T(8,128)(2,1)S(1)} %slice.25), channel_id=1, source_target_pairs={{0,6},{1,7},{2,0},{3,1},{4,2},{5,3},{6,4},{7,5},{8,14},{9,15},{10,... | collective-permute-start | bytes 786440 | tf_op jit(solution)/shard_map/ppermute | solution.py:457
  53.4 3.7 %collective-permute-done.6 = bf16[256,512]{1,0:T(8,128)(2,1)S(1)} collective-permute-done((bf16[256,512]{1,0:T(8,128)(2,1)S(1)}, bf16[256,512]{1,0:T(8,128)(2,1)S(1)}, u32[]{:S(2)}, u32[]{:S(2)}) %collective-permute-start.6) | collective-permute-done | bytes 262176 | tf_op jit(solution)/shard_map/ppermute | solution.py:457
  58.1 2.4 %collective-permute-start.11 = (bf16[512,256]{1,0:T(8,128)(2,1)S(1)}, bf16[512,256]{1,0:T(8,128)(2,1)S(1)}, u32[]{:S(2)}, u32[]{:S(2)}) collective-permute-start(bf16[512,256]{1,0:T(8,128)(2,1)S(1)} %copy-done.10), channel_id=1, source_target_pairs={{0,2},{1,3},{2,4},{3,5},{4,6},{5,7},{6,0},{7,1},{8,10},{9,11},{10,... | collective-permute-start | bytes 786440 | tf_op jit(solution)/shard_map/ppermute | solution.py:457
  61.1 6.4 %collective-permute-done.11 = bf16[512,256]{1,0:T(8,128)(2,1)S(1)} collective-permute-done((bf16[512,256]{1,0:T(8,128)(2,1)S(1)}, bf16[512,256]{1,0:T(8,128)(2,1)S(1)}, u32[]{:S(2)}, u32[]{:S(2)}) %collective-permute-start.11) | collective-permute-done | bytes 262176 | tf_op jit(solution)/shard_map/ppermute | solution.py:457
  67.5 1.8 %collective-permute-start.12 = (bf16[256,256]{1,0:T(8,128)(2,1)S(1)}, bf16[256,256]{1,0:T(8,128)(2,1)S(1)}, u32[]{:S(2)}, u32[]{:S(2)}) collective-permute-start(bf16[256,256]{1,0:T(8,128)(2,1)S(1)} %slice.26), channel_id=1, source_target_pairs={{0,2},{1,3},{2,4},{3,5},{4,6},{5,7},{6,0},{7,1},{8,10},{9,11},{10,... | collective-permute-start | bytes 393224 | tf_op jit(solution)/shard_map/ppermute | solution.py:457
  70.7 2.8 %collective-permute-done.12 = bf16[256,256]{1,0:T(8,128)(2,1)S(1)} collective-permute-done((bf16[256,256]{1,0:T(8,128)(2,1)S(1)}, bf16[256,256]{1,0:T(8,128)(2,1)S(1)}, u32[]{:S(2)}, u32[]{:S(2)}) %collective-permute-start.12) | collective-permute-done | bytes 131104 | tf_op jit(solution)/shard_map/ppermute | solution.py:457
  73.5 1.2 collective-permute-done.14
  75.0 2.6 %collective-permute-done.15.far = bf16[4,512,256]{2,1,0:T(8,128)(2,1)S(1)} collective-permute-done((bf16[4,512,256]{2,1,0:T(8,128)(2,1)S(1)}, bf16[4,512,256]{2,1,0:T(8,128)(2,1)S(1)}, u32[]{:S(2)}, u32[]{:S(2)}) %collective-permute-start.15) | collective-permute-done | bytes 1048608 | tf_op jit(solution)/shard_map/ppermute | solution.py:472
  79.3 4.3 %turn_rows.1 = bf16[8,512,512]{2,1,0:T(8,128)(2,1)} custom-call(s32[9]{0:T(128)} %get-tuple-element.39.order, bf16[8,512,512]{2,1,0:T(8,128)(2,1)} %all-to-all-done.1.rows), custom_call_target="tpu_custom_call" | custom-call | bytes 8388608 | tf_op jit(solution)/shard_map/turn_rows/pallas_call | solution.py:112
  83.6 11.6 %all-to-all-start.2 = ((bf16[64,64,512]{2,1,0:T(8,128)(2,1)}), bf16[64,64,512]{2,1,0:T(8,128)(2,1)}, u32[]{:S(2)}, u32[]{:S(2)}) async-start(bf16[64,64,512]{2,1,0:T(8,128)(2,1)} %bitcast.29), calls=%async_computation.2 | async-start | bytes 8388608 | tf_op jit(solution)/shard_map/all_to_all | solution.py:525
  95.3 10.0 %grad_rows.1 = bf16[256,8192]{1,0:T(8,128)(2,1)} custom-call(s32[5]{0:T(128)} %stack.88.me.where, bf16[256,512]{1,0:T(8,128)(2,1)} %get-tuple-element.58.dv, bf16[4,512,512]{2,1,0:T(8,128)(2,1)} %copy-done, bf16[4,512,512]{2,1,0:T(8,128)(2,1)} %copy-done.1, bf16[4,512,512]{2,1,0:T(8,128)(2,1)} %copy-done.3, bf16[4,512,512]{2,1,0:T(8,128)(2,1)} %collective-permute-done.10.rest_3_), custom_call_target="tpu_custom_call" | custom-call | flops 1 | bytes 1 | tf_op jit(solution)/shard_map/grad_rows/pallas_call | solution.py:332
  105.3 7.8 %values.1 = bf16[8,32,512]{2,1,0:T(8,128)(2,1)} custom-call(s32[5]{0:T(128)} %stack.88.me.where, bf16[8,4,2,2,32,512]{5,4,3,2,1,0:T(8,128)(2,1)} %bitcast.30, bf16[4,512,512]{2,1,0:T(8,128)(2,1)} %copy-done, bf16[4,512,512]{2,1,0:T(8,128)(2,1)} %copy-done.1, bf16[4,512,512]{2,1,0:T(8,128)(2,1)} %copy-done.3, bf16[4,512,512]{2,1,0:T(8,128)(2,1)} %collective-permute-done.10.rest_3_), custom_call_target="tpu_custom_call" | custom-call | flops 1 | bytes 1 | tf_op jit(solution)/shard_map/values/pallas_call | solution.py:285
  114.0 3.3 %collective-permute-start.16 = (bf16[4,32,512]{2,1,0:T(8,128)(2,1)S(1)}, bf16[4,32,512]{2,1,0:T(8,128)(2,1)S(1)}, u32[]{:S(2)}, u32[]{:S(2)}) collective-permute-start(bf16[4,32,512]{2,1,0:T(8,128)(2,1)S(1)} %constant_dynamic-slice_fusion.8), channel_id=1, source_target_pairs={{0,64},{16,80},{32,96},{48,112},{64,0},{80,16},{96,32},{112,48},{1... | collective-permute-start | bytes 393224 | tf_op jit(solution)/shard_map/ppermute | solution.py:539
  118.1 32.0 %collective-permute-done.16 = bf16[4,32,512]{2,1,0:T(8,128)(2,1)S(1)} collective-permute-done((bf16[4,32,512]{2,1,0:T(8,128)(2,1)S(1)}, bf16[4,32,512]{2,1,0:T(8,128)(2,1)S(1)}, u32[]{:S(2)}, u32[]{:S(2)}) %collective-permute-start.16) | collective-permute-done | bytes 131104 | tf_op jit(solution)/shard_map/ppermute | solution.py:539
  150.1 5.0 %weight_product.2 = bf16[512,512]{1,0:T(8,128)(2,1)} custom-call(s32[5]{0:T(128)} %stack.88.me.where, bf16[8,4,2,2,32,512]{5,4,3,2,1,0:T(8,128)(2,1)} %bitcast.22.rows, bf16[4,512,256]{2,1,0:T(8,128)(2,1)} %copy-done.2, bf16[4,512,256]{2,1,0:T(8,128)(2,1)} %copy-done.5), custom_call_target="tpu_custom_call" | custom-call | flops 1 | bytes 1 | tf_op jit(solution)/shard_map/weight_product/pallas_call | solution.py:429
  155.1 3.1 %collective-permute-start.17 = (bf16[512,512]{1,0:T(8,128)(2,1)}, bf16[512,512]{1,0:T(8,128)(2,1)S(1)}, u32[]{:S(2)}, u32[]{:S(2)}) collective-permute-start(bf16[512,512]{1,0:T(8,128)(2,1)} %weight_product.2), channel_id=1, source_target_pairs={{0,8},{1,9},{2,10},{3,11},{4,12},{5,13},{6,14},{7,15},{8,0},{9,1},... | collective-permute-start | bytes 1572872 | tf_op jit(solution)/shard_map/ppermute | solution.py:451
  158.3 1.5 collective-permute-start.20
  159.8 2.3 %collective-permute-start.19 = (bf16[2,32,512]{2,1,0:T(8,128)(2,1)S(1)}, bf16[2,32,512]{2,1,0:T(8,128)(2,1)S(1)}, u32[]{:S(2)}, u32[]{:S(2)}) collective-permute-start(bf16[2,32,512]{2,1,0:T(8,128)(2,1)S(1)} %pad_maximum_fusion.6), channel_id=1, source_target_pairs={{0,32},{16,48},{32,0},{48,16},{64,96},{80,112},{96,64},{112,80},{1... | collective-permute-start | bytes 196616 | tf_op jit(solution)/shard_map/ppermute | solution.py:546
  162.1 1.5 collective-permute-start.18
  163.6 5.3 %weight_product.3 = f32[512,512]{1,0:T(8,128)} custom-call(s32[5]{0:T(128)} %stack.88.me.where, bf16[8,4,2,2,32,512]{5,4,3,2,1,0:T(8,128)(2,1)} %bitcast.22.rows, bf16[4,512,256]{2,1,0:T(8,128)(2,1)} %copy-done.2, bf16[4,512,256]{2,1,0:T(8,128)(2,1)} %copy-done.5), custom_call_target="tpu_custom_call" | custom-call | flops 1 | bytes 1 | tf_op jit(solution)/shard_map/weight_product/pallas_call | solution.py:429
  170.8 4.8 %attend.1 = bf16[256,4096]{1,0:T(8,128)(2,1)} custom-call(s32[8]{0:T(128)} %get-tuple-element.46.colours, s32[5]{0:T(128)} %stack.88.me.where, bf16[8,256,128]{2,1,0:T(8,128)(2,1)} %get-tuple-element.69.probs, bf16[2,32,512]{2,1,0:T(8,128)(2,1)} %pad_maximum_fusion.4.rest_0_, bf16[2,32,512]{2,1,0:T(8,128)(2,1)} %copy-done.13, ...), custom_call_target="tpu_custom_call" | custom-call | flops 1 | bytes 1 | tf_op jit(solution)/shard_map/attend/pallas_call | solution.py:393
  (75 shorter events, 14.5 us)
Async XLA Ops:
  0.6 24.3 %collective-permute-start = (bf16[512,512]{1,0:T(8,128)(2,1)}, bf16[512,512]{1,0:T(8,128)(2,1)S(1)}, u32[]{:S(2)}, u32[]{:S(2)}) collective-permute-start(bf16[512,512]{1,0:T(8,128)(2,1)} %param.17), channel_id=1, source_target_pairs={{0,8},{1,9},{2,10},{3,11},{4,12},{5,13},{6,14},{7,15},{8,0},{9,1},... | collective-permute-start | bytes 1572872 | tf_op jit(solution)/shard_map/ppermute | solution.py:451
  2.3 22.6 %collective-permute-start.1 = (bf16[512,512]{1,0:T(8,128)(2,1)}, bf16[512,512]{1,0:T(8,128)(2,1)S(1)}, u32[]{:S(2)}, u32[]{:S(2)}) collective-permute-start(bf16[512,512]{1,0:T(8,128)(2,1)} %param.17), channel_id=1, source_target_pairs={{0,2},{1,3},{2,4},{3,5},{4,6},{5,7},{6,0},{7,1},{8,10},{9,11},{10,... | collective-permute-start | bytes 1572872 | tf_op jit(solution)/shard_map/ppermute | solution.py:457
  3.8 21.1 %collective-permute-start.2 = (bf16[512,512]{1,0:T(8,128)(2,1)}, bf16[512,512]{1,0:T(8,128)(2,1)S(1)}, u32[]{:S(2)}, u32[]{:S(2)}) collective-permute-start(bf16[512,512]{1,0:T(8,128)(2,1)} %param.17), channel_id=1, source_target_pairs={{0,6},{1,7},{2,0},{3,1},{4,2},{5,3},{6,4},{7,5},{8,14},{9,15},{10,... | collective-permute-start | bytes 1572872 | tf_op jit(solution)/shard_map/ppermute | solution.py:457
  5.7 19.2 %all-to-all-start = ((f32[128,1,32]{2,1,0:T(1,128)}), f32[128,1,32]{2,1,0:T(1,128)S(1)}, u32[]{:S(2)}, u32[]{:S(2)}) async-start(f32[128,1,32]{2,1,0:T(1,128)} %bitcast.43), calls=%async_computation | async-start | bytes 131072 | tf_op jit(solution)/shard_map/all_to_all | solution.py:489
  24.9 5.7 %copy-start.7 = (bf16[512,512]{1,0:T(8,128)(2,1)}, bf16[512,512]{1,0:T(8,128)(2,1)S(1)}, u32[]{:S(2)}) copy-start(bf16[512,512]{1,0:T(8,128)(2,1)S(1)} %collective-permute-done) | copy-start | bytes 1572868
  25.5 53.8 %all-to-all-start.1 = ((bf16[8,512,512]{2,1,0:T(8,128)(2,1)}), bf16[8,512,512]{2,1,0:T(8,128)(2,1)}, u32[]{:S(2)}, u32[]{:S(2)}) async-start(bf16[8,512,512]{2,1,0:T(8,128)(2,1)} %bitcast.31), calls=%async_computation.1 | async-start | bytes 8388608 | tf_op jit(solution)/shard_map/all_to_all | solution.py:496
  30.1 18.4 %collective-permute-start.5 = (bf16[512,512]{1,0:T(8,128)(2,1)S(1)}, bf16[512,512]{1,0:T(8,128)(2,1)S(1)}, u32[]{:S(2)}, u32[]{:S(2)}) collective-permute-start(bf16[512,512]{1,0:T(8,128)(2,1)S(1)} %collective-permute-done), channel_id=1, source_target_pairs={{0,2},{1,3},{2,4},{3,5},{4,6},{5,7},{6,0},{7,1},{8,10},{9,11},{10,... | collective-permute-start | bytes 1572872 | tf_op jit(solution)/shard_map/ppermute | solution.py:457
  30.6 18.0 %collective-permute-start.7 = (bf16[512,512]{1,0:T(8,128)(2,1)S(1)}, bf16[512,512]{1,0:T(8,128)(2,1)S(1)}, u32[]{:S(2)}, u32[]{:S(2)}) collective-permute-start(bf16[512,512]{1,0:T(8,128)(2,1)S(1)} %collective-permute-done), channel_id=1, source_target_pairs={{0,6},{1,7},{2,0},{3,1},{4,2},{5,3},{6,4},{7,5},{8,14},{9,15},{10,... | collective-permute-start | bytes 1572872 | tf_op jit(solution)/shard_map/ppermute | solution.py:457
  32.2 19.8 %collective-permute-start.3 = (bf16[256,512]{1,0:T(8,128)(2,1)S(1)}, bf16[256,512]{1,0:T(8,128)(2,1)}, u32[]{:S(2)}, u32[]{:S(2)}) collective-permute-start(bf16[256,512]{1,0:T(8,128)(2,1)S(1)} %slice.18), channel_id=1, source_target_pairs={{0,2},{1,3},{2,4},{3,5},{4,6},{5,7},{6,0},{7,1},{8,10},{9,11},{10,... | collective-permute-start | bytes 786440 | tf_op jit(solution)/shard_map/ppermute | solution.py:457
  33.4 18.5 %collective-permute-start.4 = (bf16[256,512]{1,0:T(8,128)(2,1)}, bf16[256,512]{1,0:T(8,128)(2,1)}, u32[]{:S(2)}, u32[]{:S(2)}) collective-permute-start(bf16[256,512]{1,0:T(8,128)(2,1)} %slice.19), channel_id=1, source_target_pairs={{0,6},{1,7},{2,0},{3,1},{4,2},{5,3},{6,4},{7,5},{8,14},{9,15},{10,... | collective-permute-start | bytes 786440 | tf_op jit(solution)/shard_map/ppermute | solution.py:457
  48.5 4.5 %copy-start.6 = (bf16[512,512]{1,0:T(8,128)(2,1)S(1)}, bf16[512,512]{1,0:T(8,128)(2,1)}, u32[]{:S(2)}) copy-start(bf16[512,512]{1,0:T(8,128)(2,1)} %param.17) | copy-start | bytes 1572868
  48.6 8.5 %collective-permute-start.6 = (bf16[256,512]{1,0:T(8,128)(2,1)S(1)}, bf16[256,512]{1,0:T(8,128)(2,1)S(1)}, u32[]{:S(2)}, u32[]{:S(2)}) collective-permute-start(bf16[256,512]{1,0:T(8,128)(2,1)S(1)} %slice.24), channel_id=1, source_target_pairs={{0,2},{1,3},{2,4},{3,5},{4,6},{5,7},{6,0},{7,1},{8,10},{9,11},{10,... | collective-permute-start | bytes 786440 | tf_op jit(solution)/shard_map/ppermute | solution.py:457
  48.7 8.4 %collective-permute-start.8 = (bf16[256,512]{1,0:T(8,128)(2,1)S(1)}, bf16[256,512]{1,0:T(8,128)(2,1)S(1)}, u32[]{:S(2)}, u32[]{:S(2)}) collective-permute-start(bf16[256,512]{1,0:T(8,128)(2,1)S(1)} %slice.25), channel_id=1, source_target_pairs={{0,6},{1,7},{2,0},{3,1},{4,2},{5,3},{6,4},{7,5},{8,14},{9,15},{10,... | collective-permute-start | bytes 786440 | tf_op jit(solution)/shard_map/ppermute | solution.py:457
  53.1 4.1 %copy-start.8 = (bf16[512,512]{1,0:T(8,128)(2,1)S(1)}, bf16[512,512]{1,0:T(8,128)(2,1)}, u32[]{:S(2)}) copy-start(bf16[512,512]{1,0:T(8,128)(2,1)} %copy-done.7) | copy-start | bytes 1572868
  53.3 4.1 %copy-start = (bf16[4,512,512]{2,1,0:T(8,128)(2,1)}, bf16[4,512,512]{2,1,0:T(8,128)(2,1)S(1)}, u32[]{:S(2)}) copy-start(bf16[4,512,512]{2,1,0:T(8,128)(2,1)S(1)} %pad_maximum_fusion.rest_0_) | copy-start | bytes 6291460
  53.4 24.3 %collective-permute-start.9 = (bf16[4,512,512]{2,1,0:T(8,128)(2,1)S(1)}, bf16[4,512,512]{2,1,0:T(8,128)(2,1)S(1)}, u32[]{:S(2)}, u32[]{:S(2)}) collective-permute-start(bf16[4,512,512]{2,1,0:T(8,128)(2,1)S(1)} %pad_maximum_fusion.rest_0_), channel_id=1, source_target_pairs={{0,1},{1,0},{2,3},{3,2},{4,5},{5,4},{6,7},{7,6},{8,9},{9,8},{10,11... | collective-permute-start | bytes 6291464 | tf_op jit(solution)/shard_map/ppermute | solution.py:472
  57.4 20.2 %copy-start.1 = (bf16[4,512,512]{2,1,0:T(8,128)(2,1)}, bf16[4,512,512]{2,1,0:T(8,128)(2,1)S(1)}, u32[]{:S(2)}) copy-start(bf16[4,512,512]{2,1,0:T(8,128)(2,1)S(1)} %pad_maximum_fusion.1.rest_1_) | copy-start | bytes 6291460
  57.5 21.2 %collective-permute-start.10 = (bf16[4,512,512]{2,1,0:T(8,128)(2,1)S(1)}, bf16[4,512,512]{2,1,0:T(8,128)(2,1)}, u32[]{:S(2)}, u32[]{:S(2)}) collective-permute-start(bf16[4,512,512]{2,1,0:T(8,128)(2,1)S(1)} %pad_maximum_fusion.1.rest_1_), channel_id=1, source_target_pairs={{0,1},{1,0},{2,3},{3,2},{4,5},{5,4},{6,7},{7,6},{8,9},{9,8},{10,11... | collective-permute-start | bytes 6291464 | tf_op jit(solution)/shard_map/ppermute | solution.py:472
  58.1 9.4 %collective-permute-start.11 = (bf16[512,256]{1,0:T(8,128)(2,1)S(1)}, bf16[512,256]{1,0:T(8,128)(2,1)S(1)}, u32[]{:S(2)}, u32[]{:S(2)}) collective-permute-start(bf16[512,256]{1,0:T(8,128)(2,1)S(1)} %copy-done.10), channel_id=1, source_target_pairs={{0,2},{1,3},{2,4},{3,5},{4,6},{5,7},{6,0},{7,1},{8,10},{9,11},{10,... | collective-permute-start | bytes 786440 | tf_op jit(solution)/shard_map/ppermute | solution.py:457
  60.5 9.1 %collective-permute-start.13 = (bf16[512,256]{1,0:T(8,128)(2,1)S(1)}, bf16[512,256]{1,0:T(8,128)(2,1)S(1)}, u32[]{:S(2)}, u32[]{:S(2)}) collective-permute-start(bf16[512,256]{1,0:T(8,128)(2,1)S(1)} %copy-done.10), channel_id=1, source_target_pairs={{0,6},{1,7},{2,0},{3,1},{4,2},{5,3},{6,4},{7,5},{8,14},{9,15},{10,... | collective-permute-start | bytes 786440 | tf_op jit(solution)/shard_map/ppermute | solution.py:457
  67.5 6.1 %collective-permute-start.12 = (bf16[256,256]{1,0:T(8,128)(2,1)S(1)}, bf16[256,256]{1,0:T(8,128)(2,1)S(1)}, u32[]{:S(2)}, u32[]{:S(2)}) collective-permute-start(bf16[256,256]{1,0:T(8,128)(2,1)S(1)} %slice.26), channel_id=1, source_target_pairs={{0,2},{1,3},{2,4},{3,5},{4,6},{5,7},{6,0},{7,1},{8,10},{9,11},{10,... | collective-permute-start | bytes 393224 | tf_op jit(solution)/shard_map/ppermute | solution.py:457
  69.6 5.1 %collective-permute-start.14 = (bf16[256,256]{1,0:T(8,128)(2,1)S(1)}, bf16[256,256]{1,0:T(8,128)(2,1)S(1)}, u32[]{:S(2)}, u32[]{:S(2)}) collective-permute-start(bf16[256,256]{1,0:T(8,128)(2,1)S(1)} %slice.27), channel_id=1, source_target_pairs={{0,6},{1,7},{2,0},{3,1},{4,2},{5,3},{6,4},{7,5},{8,14},{9,15},{10,... | collective-permute-start | bytes 393224 | tf_op jit(solution)/shard_map/ppermute | solution.py:457
  74.9 8.7 %copy-start.2 = (bf16[4,512,256]{2,1,0:T(8,128)(2,1)}, bf16[4,512,256]{2,1,0:T(8,128)(2,1)S(1)}, u32[]{:S(2)}) copy-start(bf16[4,512,256]{2,1,0:T(8,128)(2,1)S(1)} %pad_maximum_fusion.2.near) | copy-start | bytes 3145732
  74.9 2.7 %collective-permute-start.15 = (bf16[4,512,256]{2,1,0:T(8,128)(2,1)S(1)}, bf16[4,512,256]{2,1,0:T(8,128)(2,1)S(1)}, u32[]{:S(2)}, u32[]{:S(2)}) collective-permute-start(bf16[4,512,256]{2,1,0:T(8,128)(2,1)S(1)} %pad_maximum_fusion.2.near), channel_id=1, source_target_pairs={{0,1},{1,0},{2,3},{3,2},{4,5},{5,4},{6,7},{7,6},{8,9},{9,8},{10,11... | collective-permute-start | bytes 3145736 | tf_op jit(solution)/shard_map/ppermute | solution.py:472
  78.7 5.0 %copy-start.3 = (bf16[4,512,512]{2,1,0:T(8,128)(2,1)}, bf16[4,512,512]{2,1,0:T(8,128)(2,1)S(1)}, u32[]{:S(2)}) copy-start(bf16[4,512,512]{2,1,0:T(8,128)(2,1)S(1)} %collective-permute-done.9.rest_2_) | copy-start | bytes 6291460
  83.6 66.5 %all-to-all-start.2 = ((bf16[64,64,512]{2,1,0:T(8,128)(2,1)}), bf16[64,64,512]{2,1,0:T(8,128)(2,1)}, u32[]{:S(2)}, u32[]{:S(2)}) async-start(bf16[64,64,512]{2,1,0:T(8,128)(2,1)} %bitcast.29), calls=%async_computation.2 | async-start | bytes 8388608 | tf_op jit(solution)/shard_map/all_to_all | solution.py:525
  114.0 36.2 %collective-permute-start.16 = (bf16[4,32,512]{2,1,0:T(8,128)(2,1)S(1)}, bf16[4,32,512]{2,1,0:T(8,128)(2,1)S(1)}, u32[]{:S(2)}, u32[]{:S(2)}) collective-permute-start(bf16[4,32,512]{2,1,0:T(8,128)(2,1)S(1)} %constant_dynamic-slice_fusion.8), channel_id=1, source_target_pairs={{0,64},{16,80},{32,96},{48,112},{64,0},{80,16},{96,32},{112,48},{1... | collective-permute-start | bytes 393224 | tf_op jit(solution)/shard_map/ppermute | solution.py:539
  155.1 20.5 %collective-permute-start.17 = (bf16[512,512]{1,0:T(8,128)(2,1)}, bf16[512,512]{1,0:T(8,128)(2,1)S(1)}, u32[]{:S(2)}, u32[]{:S(2)}) collective-permute-start(bf16[512,512]{1,0:T(8,128)(2,1)} %weight_product.2), channel_id=1, source_target_pairs={{0,8},{1,9},{2,10},{3,11},{4,12},{5,13},{6,14},{7,15},{8,0},{9,1},... | collective-permute-start | bytes 1572872 | tf_op jit(solution)/shard_map/ppermute | solution.py:451
  158.3 11.2 %collective-permute-start.20 = (bf16[2,32,512]{2,1,0:T(8,128)(2,1)S(1)}, bf16[2,32,512]{2,1,0:T(8,128)(2,1)S(1)}, u32[]{:S(2)}, u32[]{:S(2)}) collective-permute-start(bf16[2,32,512]{2,1,0:T(8,128)(2,1)S(1)} %pad_maximum_fusion.7), channel_id=1, source_target_pairs={{0,48},{16,0},{32,16},{48,32},{64,112},{80,64},{96,80},{112,96},{1... | collective-permute-start | bytes 196616 | tf_op jit(solution)/shard_map/ppermute | solution.py:546
  159.8 9.7 %collective-permute-start.19 = (bf16[2,32,512]{2,1,0:T(8,128)(2,1)S(1)}, bf16[2,32,512]{2,1,0:T(8,128)(2,1)S(1)}, u32[]{:S(2)}, u32[]{:S(2)}) collective-permute-start(bf16[2,32,512]{2,1,0:T(8,128)(2,1)S(1)} %pad_maximum_fusion.6), channel_id=1, source_target_pairs={{0,32},{16,48},{32,0},{48,16},{64,96},{80,112},{96,64},{112,80},{1... | collective-permute-start | bytes 196616 | tf_op jit(solution)/shard_map/ppermute | solution.py:546
  162.1 7.4 %collective-permute-start.18 = (bf16[2,32,512]{2,1,0:T(8,128)(2,1)S(1)}, bf16[2,32,512]{2,1,0:T(8,128)(2,1)S(1)}, u32[]{:S(2)}, u32[]{:S(2)}) collective-permute-start(bf16[2,32,512]{2,1,0:T(8,128)(2,1)S(1)} %pad_maximum_fusion.5), channel_id=1, source_target_pairs={{0,16},{16,32},{32,48},{48,0},{64,80},{80,96},{96,112},{112,64},{1... | collective-permute-start | bytes 196616 | tf_op jit(solution)/shard_map/ppermute | solution.py:546
  168.9 6.7 %copy-start.4 = (f32[512,512]{1,0:T(8,128)S(1)}, f32[512,512]{1,0:T(8,128)}, u32[]{:S(2)}) copy-start(f32[512,512]{1,0:T(8,128)} %weight_product.3) | copy-start | bytes 3145732
  (6 other events, 4.4 us)

commit v3 on v2

--- a/solution.py
+++ b/solution.py
@@ -9,10 +9,11 @@
 
 HD = 128
 VMEM = 56 * 1024 * 1024
-
-
-def params(**kw):
-    return pltpu.CompilerParams(vmem_limit_bytes=VMEM, **kw)
+SMALL = 24 * 1024 * 1024
+
+
+def params(limit=VMEM):
+    return pltpu.CompilerParams(vmem_limit_bytes=limit)
 
 
 def prepare_body(slots, dp, fsdp, packing, lengths, rewards, groups, info, order):
@@ -401,7 +402,7 @@
             scratch_shapes=[pltpu.VMEM((2 * levels, seq, cols), jnp.bfloat16)],
         ),
         out_shape=jax.ShapeDtypeStruct((slots * seq, width), jnp.bfloat16),
-        compiler_params=params(),
+        compiler_params=params(SMALL),
         cost_estimate=pl.CostEstimate(flops=1, bytes_accessed=1, transcendentals=0),
         name="attend",
     )(colours, where, probs, *values)
@@ -441,7 +442,7 @@
             out_specs=pl.BlockSpec((width, cols), lambda i, n: (0, 0)),
         ),
         out_shape=jax.ShapeDtypeStruct((width, cols), dtype),
-        compiler_params=params(),
+        compiler_params=params(SMALL),
         cost_estimate=pl.CostEstimate(flops=1, bytes_accessed=1, transcendentals=0),
         name="weight_product",
     )(where, rows, near, far)

time: 178 us -> 172 us (0.966)
  Pallas kernels: 54.8 us -> 50.1 us
    pallas_call x2, Pallas kernels: 10.3 us -> 7.06 us  [product(): pl.pallas_call(functools.partial(product_body, scale), grid_spec=pltpu.Pr...]
  transfers between devices with their start and end apart: 24 -> 24, of which waited for: 9 -> 10; matrix products, arithmetic and copies ran while one was open for 3% -> 2% of each run, Pallas kernels for 26% -> 25%
where the time goes in v3:
time: 172 us; the launch traced here: 170 us
  starting transfers between devices  55.9 us (32%)
  waiting for transfers between devices  55.4 us (32%)
  Pallas kernels  50.1 us (29%)
  local copies, waits for them, and re-layouts  4.94 us (3%)
  other arithmetic  2.69 us (2%)
    ppermute x1, waiting for transfers between devices, shards(): got = lax.ppermute(give, 'dp', [(i, (i + 4) % dp) for i in range(dp)])  31.9 us
    ppermute x12, starting transfers between devices, step_along(): return lax.ppermute(x, 'fsdp', to)  16.1 us
    ppermute x12, waiting for transfers between devices, step_along(): return lax.ppermute(x, 'fsdp', to)  14.6 us
    all_to_all x1, starting transfers between devices, shards(): lax.all_to_all(rows.reshape(dp * half, 2 * seq, part), ('dp', 'fsdp'), sp...  11.2 us
    pallas_call x1, Pallas kernels, probs_and_dvalues(): pl.pallas_call(functools.partial(probs_body, kv, group, slots), grid_spec...  10.4 us
    all_to_all x1, starting transfers between devices, shards(): lax.all_to_all(info, ('dp', 'fsdp'), split_axis=0, concat_axis=0, tiled=T...  10.2 us
    pallas_call x1, Pallas kernels, grad_rows_of(): pl.pallas_call(grad_rows_body, grid_spec=pltpu.PrefetchScalarGridSpec(num...  9.97 us
    pallas_call x1, Pallas kernels, values_of(): pl.pallas_call(functools.partial(values_body, around), grid_spec=pltpu.Pr...  7.92 us
  transfers between devices with their start and end apart: 24, of which 10 were waited for; matrix products, arithmetic and copies ran while one was open for 2% of the time, Pallas kernels for 25%

profile of v3, /device:TPU:2, one launch (start us, length us, event | category | flops | bytes accessed | tf_op | source)
XLA Modules:
  0.0 169.9 jit_solution(1971498088618953839)
XLA Ops:
  0.6 1.7 collective-permute-start
  2.3 1.5 collective-permute-start.1
  4.3 1.4 prepare.1
  5.7 10.2 %all-to-all-start = ((f32[128,1,32]{2,1,0:T(1,128)}), f32[128,1,32]{2,1,0:T(1,128)S(1)}, u32[]{:S(2)}, u32[]{:S(2)}) async-start(f32[128,1,32]{2,1,0:T(1,128)} %bitcast.43), calls=%async_computation | async-start | bytes 131072 | tf_op jit(solution)/shard_map/all_to_all | solution.py:490
  15.9 4.2 %pack_rows.1 = bf16[8,16,32,512]{3,2,1,0:T(8,128)(2,1)} custom-call(s32[9]{0:T(128)} %get-tuple-element.39.order, bf16[8,32,8192]{2,1,0:T(8,128)(2,1)} %rows.1), custom_call_target="tpu_custom_call" | custom-call | bytes 8388608 | tf_op jit(solution)/shard_map/pack_rows/pallas_call | solution.py:77
  20.1 4.8 %all-to-all-done = f32[128,1,32]{2,1,0:T(1,128)S(1)} async-done(((f32[128,1,32]{2,1,0:T(1,128)}), f32[128,1,32]{2,1,0:T(1,128)S(1)}, u32[]{:S(2)}, u32[]{:S(2)}) %all-to-all-start) | async-done | bytes 16416 | tf_op jit(solution)/shard_map/all_to_all | solution.py:490
  25.5 4.6 %all-to-all-start.1 = ((bf16[8,512,512]{2,1,0:T(8,128)(2,1)}), bf16[8,512,512]{2,1,0:T(8,128)(2,1)}, u32[]{:S(2)}, u32[]{:S(2)}) async-start(bf16[8,512,512]{2,1,0:T(8,128)(2,1)} %bitcast.31), calls=%async_computation.1 | async-start | bytes 8388608 | tf_op jit(solution)/shard_map/all_to_all | solution.py:497
  30.6 1.6 collective-permute-start.7
  32.7 2.3 %collective-permute-start.4 = (bf16[256,512]{1,0:T(8,128)(2,1)S(1)}, bf16[256,512]{1,0:T(8,128)(2,1)}, u32[]{:S(2)}, u32[]{:S(2)}) collective-permute-start(bf16[256,512]{1,0:T(8,128)(2,1)S(1)} %slice.19), channel_id=1, source_target_pairs={{0,6},{1,7},{2,0},{3,1},{4,2},{5,3},{6,4},{7,5},{8,14},{9,15},{10,... | collective-permute-start | bytes 786440 | tf_op jit(solution)/shard_map/ppermute | solution.py:458
  35.7 1.7 %plan_slots.1 = (s32[8]{0:T(128)}, s32[8]{0:T(128)}, f32[8,128]{1,0:T(8,128)}) custom-call(s32[5]{0:T(128)} %stack.88.me.where, f32[128,32]{1,0:T(8,128)} %bitcast.41), custom_call_target="tpu_custom_call" | custom-call | flops 1 | bytes 1 | tf_op jit(solution)/shard_map/plan_slots/pallas_call | solution.py:167
  37.4 10.4 %probs_dvalues.1 = (bf16[256,512]{1,0:T(8,128)(2,1)}, bf16[512,256]{1,0:T(8,128)(2,1)}, bf16[8,256,128]{2,1,0:T(8,128)(2,1)}) custom-call(s32[8]{0:T(128)} %get-tuple-element.45.length, s32[8]{0:T(128)} %get-tuple-element.46.colours, f32[8,128]{1,0:T(8,128)} %get-tuple-element.47.factor, bf16[256,4096]{1,0:T(8,128)(2,1)} %q.1, bf16[256,512]{1,0:T(8,128)(2,1)} %k.1, ...), custom_call_target="tpu_custom_call" | custom-call | flops 1 | bytes 1 | tf_op jit(solution)/shard_map/probs_dvalues/pallas_call | solution.py:226
  48.0 3.3 %collective-permute-start.8 = (bf16[256,512]{1,0:T(8,128)(2,1)S(1)}, bf16[256,512]{1,0:T(8,128)(2,1)S(1)}, u32[]{:S(2)}, u32[]{:S(2)}) collective-permute-start(bf16[256,512]{1,0:T(8,128)(2,1)S(1)} %slice.25), channel_id=1, source_target_pairs={{0,6},{1,7},{2,0},{3,1},{4,2},{5,3},{6,4},{7,5},{8,14},{9,15},{10,... | collective-permute-start | bytes 786440 | tf_op jit(solution)/shard_map/ppermute | solution.py:458
  52.6 3.8 %collective-permute-done.6 = bf16[256,512]{1,0:T(8,128)(2,1)S(1)} collective-permute-done((bf16[256,512]{1,0:T(8,128)(2,1)S(1)}, bf16[256,512]{1,0:T(8,128)(2,1)S(1)}, u32[]{:S(2)}, u32[]{:S(2)}) %collective-permute-start.6) | collective-permute-done | bytes 262176 | tf_op jit(solution)/shard_map/ppermute | solution.py:458
  57.4 2.4 %collective-permute-start.11 = (bf16[512,256]{1,0:T(8,128)(2,1)S(1)}, bf16[512,256]{1,0:T(8,128)(2,1)S(1)}, u32[]{:S(2)}, u32[]{:S(2)}) collective-permute-start(bf16[512,256]{1,0:T(8,128)(2,1)S(1)} %copy-done.8), channel_id=1, source_target_pairs={{0,2},{1,3},{2,4},{3,5},{4,6},{5,7},{6,0},{7,1},{8,10},{9,11},{10,... | collective-permute-start | bytes 786440 | tf_op jit(solution)/shard_map/ppermute | solution.py:458
  60.3 6.4 %collective-permute-done.11 = bf16[512,256]{1,0:T(8,128)(2,1)S(1)} collective-permute-done((bf16[512,256]{1,0:T(8,128)(2,1)S(1)}, bf16[512,256]{1,0:T(8,128)(2,1)S(1)}, u32[]{:S(2)}, u32[]{:S(2)}) %collective-permute-start.11) | collective-permute-done | bytes 262176 | tf_op jit(solution)/shard_map/ppermute | solution.py:458
  66.8 1.8 %collective-permute-start.12 = (bf16[256,256]{1,0:T(8,128)(2,1)S(1)}, bf16[256,256]{1,0:T(8,128)(2,1)S(1)}, u32[]{:S(2)}, u32[]{:S(2)}) collective-permute-start(bf16[256,256]{1,0:T(8,128)(2,1)S(1)} %slice.26), channel_id=1, source_target_pairs={{0,2},{1,3},{2,4},{3,5},{4,6},{5,7},{6,0},{7,1},{8,10},{9,11},{10,... | collective-permute-start | bytes 393224 | tf_op jit(solution)/shard_map/ppermute | solution.py:458
  70.0 2.8 %collective-permute-done.12 = bf16[256,256]{1,0:T(8,128)(2,1)S(1)} collective-permute-done((bf16[256,256]{1,0:T(8,128)(2,1)S(1)}, bf16[256,256]{1,0:T(8,128)(2,1)S(1)}, u32[]{:S(2)}, u32[]{:S(2)}) %collective-permute-start.12) | collective-permute-done | bytes 131104 | tf_op jit(solution)/shard_map/ppermute | solution.py:458
  74.3 2.6 %collective-permute-done.15.far = bf16[4,512,256]{2,1,0:T(8,128)(2,1)S(1)} collective-permute-done((bf16[4,512,256]{2,1,0:T(8,128)(2,1)S(1)}, bf16[4,512,256]{2,1,0:T(8,128)(2,1)S(1)}, u32[]{:S(2)}, u32[]{:S(2)}) %collective-permute-start.15) | collective-permute-done | bytes 1048608 | tf_op jit(solution)/shard_map/ppermute | solution.py:473
  77.0 1.3 copy-done.5
  79.3 4.3 %turn_rows.1 = bf16[8,512,512]{2,1,0:T(8,128)(2,1)} custom-call(s32[9]{0:T(128)} %get-tuple-element.39.order, bf16[8,512,512]{2,1,0:T(8,128)(2,1)} %all-to-all-done.1.rows), custom_call_target="tpu_custom_call" | custom-call | bytes 8388608 | tf_op jit(solution)/shard_map/turn_rows/pallas_call | solution.py:113
  83.6 11.2 %all-to-all-start.2 = ((bf16[64,64,512]{2,1,0:T(8,128)(2,1)}), bf16[64,64,512]{2,1,0:T(8,128)(2,1)}, u32[]{:S(2)}, u32[]{:S(2)}) async-start(bf16[64,64,512]{2,1,0:T(8,128)(2,1)} %bitcast.29), calls=%async_computation.2 | async-start | bytes 8388608 | tf_op jit(solution)/shard_map/all_to_all | solution.py:526
  94.9 10.0 %grad_rows.1 = bf16[256,8192]{1,0:T(8,128)(2,1)} custom-call(s32[5]{0:T(128)} %stack.88.me.where, bf16[256,512]{1,0:T(8,128)(2,1)} %get-tuple-element.58.dv, bf16[4,512,512]{2,1,0:T(8,128)(2,1)} %copy-done.3, bf16[4,512,512]{2,1,0:T(8,128)(2,1)} %copy-done.4, bf16[4,512,512]{2,1,0:T(8,128)(2,1)} %copy-done.5, ...), custom_call_target="tpu_custom_call" | custom-call | flops 1 | bytes 1 | tf_op jit(solution)/shard_map/grad_rows/pallas_call | solution.py:333
  104.8 7.9 %values.1 = bf16[8,32,512]{2,1,0:T(8,128)(2,1)} custom-call(s32[5]{0:T(128)} %stack.88.me.where, bf16[8,4,2,2,32,512]{5,4,3,2,1,0:T(8,128)(2,1)} %bitcast.30, bf16[4,512,512]{2,1,0:T(8,128)(2,1)} %copy-done.3, bf16[4,512,512]{2,1,0:T(8,128)(2,1)} %copy-done.4, bf16[4,512,512]{2,1,0:T(8,128)(2,1)} %copy-done.5, ...), custom_call_target="tpu_custom_call" | custom-call | flops 1 | bytes 1 | tf_op jit(solution)/shard_map/values/pallas_call | solution.py:286
  113.7 3.3 %collective-permute-start.16 = (bf16[4,32,512]{2,1,0:T(8,128)(2,1)S(1)}, bf16[4,32,512]{2,1,0:T(8,128)(2,1)S(1)}, u32[]{:S(2)}, u32[]{:S(2)}) collective-permute-start(bf16[4,32,512]{2,1,0:T(8,128)(2,1)S(1)} %constant_dynamic-slice_fusion.8), channel_id=1, source_target_pairs={{0,64},{16,80},{32,96},{48,112},{64,0},{80,16},{96,32},{112,48},{1... | collective-permute-start | bytes 393224 | tf_op jit(solution)/shard_map/ppermute | solution.py:540
  117.8 31.9 %collective-permute-done.16 = bf16[4,32,512]{2,1,0:T(8,128)(2,1)S(1)} collective-permute-done((bf16[4,32,512]{2,1,0:T(8,128)(2,1)S(1)}, bf16[4,32,512]{2,1,0:T(8,128)(2,1)S(1)}, u32[]{:S(2)}, u32[]{:S(2)}) %collective-permute-start.16) | collective-permute-done | bytes 131104 | tf_op jit(solution)/shard_map/ppermute | solution.py:540
  149.7 3.5 %weight_product.2 = bf16[512,512]{1,0:T(8,128)(2,1)S(1)} custom-call(s32[5]{0:T(128)S(1)} %copy-done.1, bf16[8,4,2,2,32,512]{5,4,3,2,1,0:T(8,128)(2,1)} %bitcast.22.rows, bf16[4,512,256]{2,1,0:T(8,128)(2,1)S(1)} %pad_maximum_fusion.2.near, bf16[4,512,256]{2,1,0:T(8,128)(2,1)S(1)} %collective-permute-done.15.far), custom_call_target="tpu_custom_call" | custom-call | flops 1 | bytes 1 | tf_op jit(solution)/shard_map/weight_product/pallas_call | solution.py:430
  153.2 3.2 %collective-permute-start.17 = (bf16[512,512]{1,0:T(8,128)(2,1)S(1)}, bf16[512,512]{1,0:T(8,128)(2,1)S(1)}, u32[]{:S(2)}, u32[]{:S(2)}) collective-permute-start(bf16[512,512]{1,0:T(8,128)(2,1)S(1)} %weight_product.2), channel_id=1, source_target_pairs={{0,8},{1,9},{2,10},{3,11},{4,12},{5,13},{6,14},{7,15},{8,0},{9,1},... | collective-permute-start | bytes 1572872 | tf_op jit(solution)/shard_map/ppermute | solution.py:452
  156.4 1.5 collective-permute-start.20
  158.0 2.3 %collective-permute-start.19 = (bf16[2,32,512]{2,1,0:T(8,128)(2,1)S(1)}, bf16[2,32,512]{2,1,0:T(8,128)(2,1)S(1)}, u32[]{:S(2)}, u32[]{:S(2)}) collective-permute-start(bf16[2,32,512]{2,1,0:T(8,128)(2,1)S(1)} %pad_maximum_fusion.6), channel_id=1, source_target_pairs={{0,32},{16,48},{32,0},{48,16},{64,96},{80,112},{96,64},{112,80},{1... | collective-permute-start | bytes 196616 | tf_op jit(solution)/shard_map/ppermute | solution.py:547
  160.3 1.5 collective-permute-start.18
  161.8 3.6 %weight_product.3 = f32[512,512]{1,0:T(8,128)S(1)} custom-call(s32[5]{0:T(128)S(1)} %copy-done.1, bf16[8,4,2,2,32,512]{5,4,3,2,1,0:T(8,128)(2,1)} %bitcast.22.rows, bf16[4,512,256]{2,1,0:T(8,128)(2,1)S(1)} %pad_maximum_fusion.2.near, bf16[4,512,256]{2,1,0:T(8,128)(2,1)S(1)} %collective-permute-done.15.far), custom_call_target="tpu_custom_call" | custom-call | flops 1 | bytes 1 | tf_op jit(solution)/shard_map/weight_product/pallas_call | solution.py:430
  165.9 3.1 %attend.1 = bf16[256,4096]{1,0:T(8,128)(2,1)} custom-call(s32[8]{0:T(128)S(1)} %copy-done.2, s32[5]{0:T(128)S(1)} %copy-done.1, bf16[8,256,128]{2,1,0:T(8,128)(2,1)S(1)} %copy-done, bf16[2,32,512]{2,1,0:T(8,128)(2,1)S(1)} %pad_maximum_fusion.4.rest_0_, bf16[2,32,512]{2,1,0:T(8,128)(2,1)S(1)} %collective-permute-done.18.rest_1_, ...), custom_call_target="tpu_custom_call" | custom-call | flops 1 | bytes 1 | tf_op jit(solution)/shard_map/attend/pallas_call | solution.py:394
  (65 shorter events, 12.9 us)
Async XLA Ops:
  0.6 24.3 %collective-permute-start = (bf16[512,512]{1,0:T(8,128)(2,1)}, bf16[512,512]{1,0:T(8,128)(2,1)S(1)}, u32[]{:S(2)}, u32[]{:S(2)}) collective-permute-start(bf16[512,512]{1,0:T(8,128)(2,1)} %param.17), channel_id=1, source_target_pairs={{0,8},{1,9},{2,10},{3,11},{4,12},{5,13},{6,14},{7,15},{8,0},{9,1},... | collective-permute-start | bytes 1572872 | tf_op jit(solution)/shard_map/ppermute | solution.py:452
  2.3 22.6 %collective-permute-start.1 = (bf16[512,512]{1,0:T(8,128)(2,1)}, bf16[512,512]{1,0:T(8,128)(2,1)S(1)}, u32[]{:S(2)}, u32[]{:S(2)}) collective-permute-start(bf16[512,512]{1,0:T(8,128)(2,1)} %param.17), channel_id=1, source_target_pairs={{0,2},{1,3},{2,4},{3,5},{4,6},{5,7},{6,0},{7,1},{8,10},{9,11},{10,... | collective-permute-start | bytes 1572872 | tf_op jit(solution)/shard_map/ppermute | solution.py:458
  3.8 21.1 %collective-permute-start.2 = (bf16[512,512]{1,0:T(8,128)(2,1)}, bf16[512,512]{1,0:T(8,128)(2,1)S(1)}, u32[]{:S(2)}, u32[]{:S(2)}) collective-permute-start(bf16[512,512]{1,0:T(8,128)(2,1)} %param.17), channel_id=1, source_target_pairs={{0,6},{1,7},{2,0},{3,1},{4,2},{5,3},{6,4},{7,5},{8,14},{9,15},{10,... | collective-permute-start | bytes 1572872 | tf_op jit(solution)/shard_map/ppermute | solution.py:458
  5.7 19.2 %all-to-all-start = ((f32[128,1,32]{2,1,0:T(1,128)}), f32[128,1,32]{2,1,0:T(1,128)S(1)}, u32[]{:S(2)}, u32[]{:S(2)}) async-start(f32[128,1,32]{2,1,0:T(1,128)} %bitcast.43), calls=%async_computation | async-start | bytes 131072 | tf_op jit(solution)/shard_map/all_to_all | solution.py:490
  25.5 53.8 %all-to-all-start.1 = ((bf16[8,512,512]{2,1,0:T(8,128)(2,1)}), bf16[8,512,512]{2,1,0:T(8,128)(2,1)}, u32[]{:S(2)}, u32[]{:S(2)}) async-start(bf16[8,512,512]{2,1,0:T(8,128)(2,1)} %bitcast.31), calls=%async_computation.1 | async-start | bytes 8388608 | tf_op jit(solution)/shard_map/all_to_all | solution.py:497
  30.1 17.7 %collective-permute-start.5 = (bf16[512,512]{1,0:T(8,128)(2,1)S(1)}, bf16[512,512]{1,0:T(8,128)(2,1)S(1)}, u32[]{:S(2)}, u32[]{:S(2)}) collective-permute-start(bf16[512,512]{1,0:T(8,128)(2,1)S(1)} %collective-permute-done), channel_id=1, source_target_pairs={{0,2},{1,3},{2,4},{3,5},{4,6},{5,7},{6,0},{7,1},{8,10},{9,11},{10,... | collective-permute-start | bytes 1572872 | tf_op jit(solution)/shard_map/ppermute | solution.py:458
  30.6 17.3 %collective-permute-start.7 = (bf16[512,512]{1,0:T(8,128)(2,1)S(1)}, bf16[512,512]{1,0:T(8,128)(2,1)S(1)}, u32[]{:S(2)}, u32[]{:S(2)}) collective-permute-start(bf16[512,512]{1,0:T(8,128)(2,1)S(1)} %collective-permute-done), channel_id=1, source_target_pairs={{0,6},{1,7},{2,0},{3,1},{4,2},{5,3},{6,4},{7,5},{8,14},{9,15},{10,... | collective-permute-start | bytes 1572872 | tf_op jit(solution)/shard_map/ppermute | solution.py:458
  32.2 19.1 %collective-permute-start.3 = (bf16[256,512]{1,0:T(8,128)(2,1)S(1)}, bf16[256,512]{1,0:T(8,128)(2,1)S(1)}, u32[]{:S(2)}, u32[]{:S(2)}) collective-permute-start(bf16[256,512]{1,0:T(8,128)(2,1)S(1)} %slice.18), channel_id=1, source_target_pairs={{0,2},{1,3},{2,4},{3,5},{4,6},{5,7},{6,0},{7,1},{8,10},{9,11},{10,... | collective-permute-start | bytes 786440 | tf_op jit(solution)/shard_map/ppermute | solution.py:458
  32.7 18.5 %collective-permute-start.4 = (bf16[256,512]{1,0:T(8,128)(2,1)S(1)}, bf16[256,512]{1,0:T(8,128)(2,1)}, u32[]{:S(2)}, u32[]{:S(2)}) collective-permute-start(bf16[256,512]{1,0:T(8,128)(2,1)S(1)} %slice.19), channel_id=1, source_target_pairs={{0,6},{1,7},{2,0},{3,1},{4,2},{5,3},{6,4},{7,5},{8,14},{9,15},{10,... | collective-permute-start | bytes 786440 | tf_op jit(solution)/shard_map/ppermute | solution.py:458
  47.8 4.5 %copy-start.6 = (bf16[512,512]{1,0:T(8,128)(2,1)S(1)}, bf16[512,512]{1,0:T(8,128)(2,1)}, u32[]{:S(2)}) copy-start(bf16[512,512]{1,0:T(8,128)(2,1)} %param.17) | copy-start | bytes 1572868
  47.9 8.5 %collective-permute-start.6 = (bf16[256,512]{1,0:T(8,128)(2,1)S(1)}, bf16[256,512]{1,0:T(8,128)(2,1)S(1)}, u32[]{:S(2)}, u32[]{:S(2)}) collective-permute-start(bf16[256,512]{1,0:T(8,128)(2,1)S(1)} %slice.24), channel_id=1, source_target_pairs={{0,2},{1,3},{2,4},{3,5},{4,6},{5,7},{6,0},{7,1},{8,10},{9,11},{10,... | collective-permute-start | bytes 786440 | tf_op jit(solution)/shard_map/ppermute | solution.py:458
  48.0 8.4 %collective-permute-start.8 = (bf16[256,512]{1,0:T(8,128)(2,1)S(1)}, bf16[256,512]{1,0:T(8,128)(2,1)S(1)}, u32[]{:S(2)}, u32[]{:S(2)}) collective-permute-start(bf16[256,512]{1,0:T(8,128)(2,1)S(1)} %slice.25), channel_id=1, source_target_pairs={{0,6},{1,7},{2,0},{3,1},{4,2},{5,3},{6,4},{7,5},{8,14},{9,15},{10,... | collective-permute-start | bytes 786440 | tf_op jit(solution)/shard_map/ppermute | solution.py:458
  52.5 4.2 %copy-start.3 = (bf16[4,512,512]{2,1,0:T(8,128)(2,1)}, bf16[4,512,512]{2,1,0:T(8,128)(2,1)S(1)}, u32[]{:S(2)}) copy-start(bf16[4,512,512]{2,1,0:T(8,128)(2,1)S(1)} %pad_maximum_fusion.rest_0_) | copy-start | bytes 6291460
  52.6 24.4 %collective-permute-start.9 = (bf16[4,512,512]{2,1,0:T(8,128)(2,1)S(1)}, bf16[4,512,512]{2,1,0:T(8,128)(2,1)S(1)}, u32[]{:S(2)}, u32[]{:S(2)}) collective-permute-start(bf16[4,512,512]{2,1,0:T(8,128)(2,1)S(1)} %pad_maximum_fusion.rest_0_), channel_id=1, source_target_pairs={{0,1},{1,0},{2,3},{3,2},{4,5},{5,4},{6,7},{7,6},{8,9},{9,8},{10,11... | collective-permute-start | bytes 6291464 | tf_op jit(solution)/shard_map/ppermute | solution.py:473
  56.4 1.0 copy-start.8
  56.7 20.2 %copy-start.4 = (bf16[4,512,512]{2,1,0:T(8,128)(2,1)}, bf16[4,512,512]{2,1,0:T(8,128)(2,1)S(1)}, u32[]{:S(2)}) copy-start(bf16[4,512,512]{2,1,0:T(8,128)(2,1)S(1)} %pad_maximum_fusion.1.rest_1_) | copy-start | bytes 6291460
  56.7 21.5 %collective-permute-start.10 = (bf16[4,512,512]{2,1,0:T(8,128)(2,1)S(1)}, bf16[4,512,512]{2,1,0:T(8,128)(2,1)}, u32[]{:S(2)}, u32[]{:S(2)}) collective-permute-start(bf16[4,512,512]{2,1,0:T(8,128)(2,1)S(1)} %pad_maximum_fusion.1.rest_1_), channel_id=1, source_target_pairs={{0,1},{1,0},{2,3},{3,2},{4,5},{5,4},{6,7},{7,6},{8,9},{9,8},{10,11... | collective-permute-start | bytes 6291464 | tf_op jit(solution)/shard_map/ppermute | solution.py:473
  57.4 9.4 %collective-permute-start.11 = (bf16[512,256]{1,0:T(8,128)(2,1)S(1)}, bf16[512,256]{1,0:T(8,128)(2,1)S(1)}, u32[]{:S(2)}, u32[]{:S(2)}) collective-permute-start(bf16[512,256]{1,0:T(8,128)(2,1)S(1)} %copy-done.8), channel_id=1, source_target_pairs={{0,2},{1,3},{2,4},{3,5},{4,6},{5,7},{6,0},{7,1},{8,10},{9,11},{10,... | collective-permute-start | bytes 786440 | tf_op jit(solution)/shard_map/ppermute | solution.py:458
  59.8 9.1 %collective-permute-start.13 = (bf16[512,256]{1,0:T(8,128)(2,1)S(1)}, bf16[512,256]{1,0:T(8,128)(2,1)S(1)}, u32[]{:S(2)}, u32[]{:S(2)}) collective-permute-start(bf16[512,256]{1,0:T(8,128)(2,1)S(1)} %copy-done.8), channel_id=1, source_target_pairs={{0,6},{1,7},{2,0},{3,1},{4,2},{5,3},{6,4},{7,5},{8,14},{9,15},{10,... | collective-permute-start | bytes 786440 | tf_op jit(solution)/shard_map/ppermute | solution.py:458
  66.8 6.1 %collective-permute-start.12 = (bf16[256,256]{1,0:T(8,128)(2,1)S(1)}, bf16[256,256]{1,0:T(8,128)(2,1)S(1)}, u32[]{:S(2)}, u32[]{:S(2)}) collective-permute-start(bf16[256,256]{1,0:T(8,128)(2,1)S(1)} %slice.26), channel_id=1, source_target_pairs={{0,2},{1,3},{2,4},{3,5},{4,6},{5,7},{6,0},{7,1},{8,10},{9,11},{10,... | collective-permute-start | bytes 393224 | tf_op jit(solution)/shard_map/ppermute | solution.py:458
  68.9 5.1 %collective-permute-start.14 = (bf16[256,256]{1,0:T(8,128)(2,1)S(1)}, bf16[256,256]{1,0:T(8,128)(2,1)S(1)}, u32[]{:S(2)}, u32[]{:S(2)}) collective-permute-start(bf16[256,256]{1,0:T(8,128)(2,1)S(1)} %slice.27), channel_id=1, source_target_pairs={{0,6},{1,7},{2,0},{3,1},{4,2},{5,3},{6,4},{7,5},{8,14},{9,15},{10,... | collective-permute-start | bytes 393224 | tf_op jit(solution)/shard_map/ppermute | solution.py:458
  74.2 2.7 %collective-permute-start.15 = (bf16[4,512,256]{2,1,0:T(8,128)(2,1)S(1)}, bf16[4,512,256]{2,1,0:T(8,128)(2,1)S(1)}, u32[]{:S(2)}, u32[]{:S(2)}) collective-permute-start(bf16[4,512,256]{2,1,0:T(8,128)(2,1)S(1)} %pad_maximum_fusion.2.near), channel_id=1, source_target_pairs={{0,1},{1,0},{2,3},{3,2},{4,5},{5,4},{6,7},{7,6},{8,9},{9,8},{10,11... | collective-permute-start | bytes 3145736 | tf_op jit(solution)/shard_map/ppermute | solution.py:473
  77.0 1.3 copy-start.5
  83.6 66.1 %all-to-all-start.2 = ((bf16[64,64,512]{2,1,0:T(8,128)(2,1)}), bf16[64,64,512]{2,1,0:T(8,128)(2,1)}, u32[]{:S(2)}, u32[]{:S(2)}) async-start(bf16[64,64,512]{2,1,0:T(8,128)(2,1)} %bitcast.29), calls=%async_computation.2 | async-start | bytes 8388608 | tf_op jit(solution)/shard_map/all_to_all | solution.py:526
  104.8 44.9 %copy-start.1 = (s32[5]{0:T(128)S(1)}, s32[5]{0:T(128)}, u32[]{:S(2)}) copy-start(s32[5]{0:T(128)} %stack.88.me.where) | copy-start | bytes 64
  113.7 36.0 %collective-permute-start.16 = (bf16[4,32,512]{2,1,0:T(8,128)(2,1)S(1)}, bf16[4,32,512]{2,1,0:T(8,128)(2,1)S(1)}, u32[]{:S(2)}, u32[]{:S(2)}) collective-permute-start(bf16[4,32,512]{2,1,0:T(8,128)(2,1)S(1)} %constant_dynamic-slice_fusion.8), channel_id=1, source_target_pairs={{0,64},{16,80},{32,96},{48,112},{64,0},{80,16},{96,32},{112,48},{1... | collective-permute-start | bytes 393224 | tf_op jit(solution)/shard_map/ppermute | solution.py:540
  153.2 15.8 %collective-permute-start.17 = (bf16[512,512]{1,0:T(8,128)(2,1)S(1)}, bf16[512,512]{1,0:T(8,128)(2,1)S(1)}, u32[]{:S(2)}, u32[]{:S(2)}) collective-permute-start(bf16[512,512]{1,0:T(8,128)(2,1)S(1)} %weight_product.2), channel_id=1, source_target_pairs={{0,8},{1,9},{2,10},{3,11},{4,12},{5,13},{6,14},{7,15},{8,0},{9,1},... | collective-permute-start | bytes 1572872 | tf_op jit(solution)/shard_map/ppermute | solution.py:452
  156.4 9.0 %collective-permute-start.20 = (bf16[2,32,512]{2,1,0:T(8,128)(2,1)S(1)}, bf16[2,32,512]{2,1,0:T(8,128)(2,1)S(1)}, u32[]{:S(2)}, u32[]{:S(2)}) collective-permute-start(bf16[2,32,512]{2,1,0:T(8,128)(2,1)S(1)} %pad_maximum_fusion.7), channel_id=1, source_target_pairs={{0,48},{16,0},{32,16},{48,32},{64,112},{80,64},{96,80},{112,96},{1... | collective-permute-start | bytes 196616 | tf_op jit(solution)/shard_map/ppermute | solution.py:547
  158.0 7.4 %collective-permute-start.19 = (bf16[2,32,512]{2,1,0:T(8,128)(2,1)S(1)}, bf16[2,32,512]{2,1,0:T(8,128)(2,1)S(1)}, u32[]{:S(2)}, u32[]{:S(2)}) collective-permute-start(bf16[2,32,512]{2,1,0:T(8,128)(2,1)S(1)} %pad_maximum_fusion.6), channel_id=1, source_target_pairs={{0,32},{16,48},{32,0},{48,16},{64,96},{80,112},{96,64},{112,80},{1... | collective-permute-start | bytes 196616 | tf_op jit(solution)/shard_map/ppermute | solution.py:547
  160.3 5.6 %copy-start = (bf16[8,256,128]{2,1,0:T(8,128)(2,1)S(1)}, bf16[8,256,128]{2,1,0:T(8,128)(2,1)}, u32[]{:S(2)}) copy-start(bf16[8,256,128]{2,1,0:T(8,128)(2,1)} %get-tuple-element.69.probs) | copy-start | bytes 1572868
  160.3 5.6 %copy-start.2 = (s32[8]{0:T(128)S(1)}, s32[8]{0:T(128)}, u32[]{:S(2)}) copy-start(s32[8]{0:T(128)} %get-tuple-element.46.colours) | copy-start | bytes 100
  160.3 5.5 %collective-permute-start.18 = (bf16[2,32,512]{2,1,0:T(8,128)(2,1)S(1)}, bf16[2,32,512]{2,1,0:T(8,128)(2,1)S(1)}, u32[]{:S(2)}, u32[]{:S(2)}) collective-permute-start(bf16[2,32,512]{2,1,0:T(8,128)(2,1)S(1)} %pad_maximum_fusion.5), channel_id=1, source_target_pairs={{0,16},{16,32},{32,48},{48,0},{64,80},{80,96},{96,112},{112,64},{1... | collective-permute-start | bytes 196616 | tf_op jit(solution)/shard_map/ppermute | solution.py:547
  (1 other events, 0.6 us)

commit v4 on v3

--- a/solution.py
+++ b/solution.py
@@ -531,14 +531,14 @@
         axis_index_groups=groups,
         tiled=True,
     ).reshape(dp, around, 2, 2, seq, part)
-    grad_rows = grad_rows_of(where, dvalues, weights)
-    sent, grad_rows = lax.optimization_barrier((sent, grad_rows))
     values = values_of(where, sent.reshape(dp, around, 2, 2, seq, part), weights)
     side, level = home // 4, home % 4
     keep = lax.dynamic_slice_in_dim(values, side * 4, 4, 0)
     give = lax.dynamic_slice_in_dim(values, (1 - side) * 4, 4, 0)
     got = lax.ppermute(give, "dp", [(i, (i + 4) % dp) for i in range(dp)])
-    rows, got = lax.optimization_barrier((rows, got))
+    dvalues, values = lax.optimization_barrier((dvalues, values))
+    grad_rows = grad_rows_of(where, dvalues, weights)
+    rows, got, grad_rows = lax.optimization_barrier((rows, got, grad_rows))
     both = [
         jnp.stack([lax.dynamic_index_in_dim(v, (level + k) % 4, 0, False) for v in (keep, got)])
         for k in range(4)

time: 172 us -> 170 us (0.988)
  starting transfers between devices: 55.9 us -> 53 us
  waiting for transfers between devices: 55.4 us -> 57.9 us
    ppermute x12, waiting for transfers between devices: 14.6 us -> 17 us  [step_along(): return lax.ppermute(x, 'fsdp', to)]
    ppermute x12, starting transfers between devices: 16.1 us -> 14 us  [step_along(): return lax.ppermute(x, 'fsdp', to)]
    all_to_all x1, starting transfers between devices: 11.2 us -> 9.48 us  [shards(): lax.all_to_all(rows.reshape(dp * half, 2 * seq, part), ('dp', 'fsdp'), sp...]
  transfers between devices with their start and end apart: 24 -> 24, of which waited for: 10 -> 11; matrix products, arithmetic and copies ran while one was open for 2% -> 2% of each run, Pallas kernels for 25% -> 25%
where the time goes in v4:
time: 170 us; the launch traced here: 169 us
  waiting for transfers between devices  57.9 us (34%)
  starting transfers between devices  53 us (31%)
  Pallas kernels  50.1 us (29%)
  local copies, waits for them, and re-layouts  4.16 us (2%)
  other arithmetic  2.69 us (2%)
    ppermute x1, waiting for transfers between devices, shards(): got = lax.ppermute(give, 'dp', [(i, (i + 4) % dp) for i in range(dp)])  32.7 us
    ppermute x12, waiting for transfers between devices, step_along(): return lax.ppermute(x, 'fsdp', to)  17 us
    ppermute x12, starting transfers between devices, step_along(): return lax.ppermute(x, 'fsdp', to)  14 us
    pallas_call x1, Pallas kernels, probs_and_dvalues(): pl.pallas_call(functools.partial(probs_body, kv, group, slots), grid_spec...  10.4 us
    all_to_all x1, starting transfers between devices, shards(): lax.all_to_all(info, ('dp', 'fsdp'), split_axis=0, concat_axis=0, tiled=T...  10.2 us
    pallas_call x1, Pallas kernels, grad_rows_of(): pl.pallas_call(grad_rows_body, grid_spec=pltpu.PrefetchScalarGridSpec(num...  10.1 us
    all_to_all x1, starting transfers between devices, shards(): lax.all_to_all(rows.reshape(dp * half, 2 * seq, part), ('dp', 'fsdp'), sp...  9.48 us
    pallas_call x1, Pallas kernels, values_of(): pl.pallas_call(functools.partial(values_body, around), grid_spec=pltpu.Pr...  7.79 us
  transfers between devices with their start and end apart: 24, of which 11 were waited for; matrix products, arithmetic and copies ran while one was open for 2% of the time, Pallas kernels for 25%

profile of v4, /device:TPU:2, one launch (start us, length us, event | category | flops | bytes accessed | tf_op | source)
XLA Modules:
  0.0 168.8 jit_solution(3655397166277765243)
XLA Ops:
  0.6 1.6 collective-permute-start.1
  2.2 1.6 collective-permute-start
  4.3 1.4 prepare.1
  5.7 10.2 %all-to-all-start = ((f32[128,1,32]{2,1,0:T(1,128)}), f32[128,1,32]{2,1,0:T(1,128)S(1)}, u32[]{:S(2)}, u32[]{:S(2)}) async-start(f32[128,1,32]{2,1,0:T(1,128)} %bitcast.43), calls=%async_computation | async-start | bytes 131072 | tf_op jit(solution)/shard_map/all_to_all | solution.py:490
  15.9 4.2 %pack_rows.1 = bf16[8,16,32,512]{3,2,1,0:T(8,128)(2,1)} custom-call(s32[9]{0:T(128)} %get-tuple-element.39.order, bf16[8,32,8192]{2,1,0:T(8,128)(2,1)} %rows.1), custom_call_target="tpu_custom_call" | custom-call | bytes 8388608 | tf_op jit(solution)/shard_map/pack_rows/pallas_call | solution.py:77
  20.1 4.8 %all-to-all-done = f32[128,1,32]{2,1,0:T(1,128)S(1)} async-done(((f32[128,1,32]{2,1,0:T(1,128)}), f32[128,1,32]{2,1,0:T(1,128)S(1)}, u32[]{:S(2)}, u32[]{:S(2)}) %all-to-all-start) | async-done | bytes 16416 | tf_op jit(solution)/shard_map/all_to_all | solution.py:490
  25.5 4.5 %all-to-all-start.1 = ((bf16[8,512,512]{2,1,0:T(8,128)(2,1)}), bf16[8,512,512]{2,1,0:T(8,128)(2,1)}, u32[]{:S(2)}, u32[]{:S(2)}) async-start(bf16[8,512,512]{2,1,0:T(8,128)(2,1)} %bitcast.31), calls=%async_computation.1 | async-start | bytes 8388608 | tf_op jit(solution)/shard_map/all_to_all | solution.py:497
  30.1 1.5 collective-permute-start.7
  32.2 1.5 collective-permute-start.4
  34.9 1.7 %plan_slots.1 = (s32[8]{0:T(128)}, s32[8]{0:T(128)}, f32[8,128]{1,0:T(8,128)}) custom-call(s32[5]{0:T(128)} %stack.88.me.where, f32[128,32]{1,0:T(8,128)} %bitcast.41), custom_call_target="tpu_custom_call" | custom-call | flops 1 | bytes 1 | tf_op jit(solution)/shard_map/plan_slots/pallas_call | solution.py:167
  36.7 10.4 %probs_dvalues.1 = (bf16[256,512]{1,0:T(8,128)(2,1)}, bf16[512,256]{1,0:T(8,128)(2,1)}, bf16[8,256,128]{2,1,0:T(8,128)(2,1)}) custom-call(s32[8]{0:T(128)} %get-tuple-element.45.length, s32[8]{0:T(128)} %get-tuple-element.46.colours, f32[8,128]{1,0:T(8,128)} %get-tuple-element.47.factor, bf16[256,4096]{1,0:T(8,128)(2,1)} %q.1, bf16[256,512]{1,0:T(8,128)(2,1)} %k.1, ...), custom_call_target="tpu_custom_call" | custom-call | flops 1 | bytes 1 | tf_op jit(solution)/shard_map/probs_dvalues/pallas_call | solution.py:226
  47.2 1.6 collective-permute-start.8
  52.1 3.0 %collective-permute-done.8 = bf16[256,512]{1,0:T(8,128)(2,1)S(1)} collective-permute-done((bf16[256,512]{1,0:T(8,128)(2,1)S(1)}, bf16[256,512]{1,0:T(8,128)(2,1)S(1)}, u32[]{:S(2)}, u32[]{:S(2)}) %collective-permute-start.8) | collective-permute-done | bytes 262176 | tf_op jit(solution)/shard_map/ppermute | solution.py:458
  55.1 2.0 %collective-permute-done.6 = bf16[256,512]{1,0:T(8,128)(2,1)S(1)} collective-permute-done((bf16[256,512]{1,0:T(8,128)(2,1)S(1)}, bf16[256,512]{1,0:T(8,128)(2,1)S(1)}, u32[]{:S(2)}, u32[]{:S(2)}) %collective-permute-start.6) | collective-permute-done | bytes 262176 | tf_op jit(solution)/shard_map/ppermute | solution.py:458
  58.1 3.0 %collective-permute-start.13 = (bf16[512,256]{1,0:T(8,128)(2,1)S(1)}, bf16[512,256]{1,0:T(8,128)(2,1)S(1)}, u32[]{:S(2)}, u32[]{:S(2)}) collective-permute-start(bf16[512,256]{1,0:T(8,128)(2,1)S(1)} %copy-done.9), channel_id=1, source_target_pairs={{0,6},{1,7},{2,0},{3,1},{4,2},{5,3},{6,4},{7,5},{8,14},{9,15},{10,... | collective-permute-start | bytes 786440 | tf_op jit(solution)/shard_map/ppermute | solution.py:458
  61.0 5.7 %collective-permute-done.13 = bf16[512,256]{1,0:T(8,128)(2,1)S(1)} collective-permute-done((bf16[512,256]{1,0:T(8,128)(2,1)S(1)}, bf16[512,256]{1,0:T(8,128)(2,1)S(1)}, u32[]{:S(2)}, u32[]{:S(2)}) %collective-permute-start.13) | collective-permute-done | bytes 262176 | tf_op jit(solution)/shard_map/ppermute | solution.py:458
  66.7 2.6 %collective-permute-start.14 = (bf16[256,256]{1,0:T(8,128)(2,1)S(1)}, bf16[256,256]{1,0:T(8,128)(2,1)S(1)}, u32[]{:S(2)}, u32[]{:S(2)}) collective-permute-start(bf16[256,256]{1,0:T(8,128)(2,1)S(1)} %slice.27), channel_id=1, source_target_pairs={{0,6},{1,7},{2,0},{3,1},{4,2},{5,3},{6,4},{7,5},{8,14},{9,15},{10,... | collective-permute-start | bytes 393224 | tf_op jit(solution)/shard_map/ppermute | solution.py:458
  69.4 2.4 %collective-permute-done.14 = bf16[256,256]{1,0:T(8,128)(2,1)S(1)} collective-permute-done((bf16[256,256]{1,0:T(8,128)(2,1)S(1)}, bf16[256,256]{1,0:T(8,128)(2,1)S(1)}, u32[]{:S(2)}, u32[]{:S(2)}) %collective-permute-start.14) | collective-permute-done | bytes 131104 | tf_op jit(solution)/shard_map/ppermute | solution.py:458
  71.8 2.5 %collective-permute-done.12 = bf16[256,256]{1,0:T(8,128)(2,1)S(1)} collective-permute-done((bf16[256,256]{1,0:T(8,128)(2,1)S(1)}, bf16[256,256]{1,0:T(8,128)(2,1)S(1)}, u32[]{:S(2)}, u32[]{:S(2)}) %collective-permute-start.12) | collective-permute-done | bytes 131104 | tf_op jit(solution)/shard_map/ppermute | solution.py:458
  74.6 2.6 %collective-permute-done.15.far = bf16[4,512,256]{2,1,0:T(8,128)(2,1)S(1)} collective-permute-done((bf16[4,512,256]{2,1,0:T(8,128)(2,1)S(1)}, bf16[4,512,256]{2,1,0:T(8,128)(2,1)S(1)}, u32[]{:S(2)}, u32[]{:S(2)}) %collective-permute-start.15) | collective-permute-done | bytes 1048608 | tf_op jit(solution)/shard_map/ppermute | solution.py:473
  79.3 4.3 %turn_rows.1 = bf16[8,512,512]{2,1,0:T(8,128)(2,1)} custom-call(s32[9]{0:T(128)} %get-tuple-element.39.order, bf16[8,512,512]{2,1,0:T(8,128)(2,1)} %all-to-all-done.1.rows), custom_call_target="tpu_custom_call" | custom-call | bytes 8388608 | tf_op jit(solution)/shard_map/turn_rows/pallas_call | solution.py:113
  83.6 9.5 %all-to-all-start.2 = ((bf16[64,64,512]{2,1,0:T(8,128)(2,1)}), bf16[64,64,512]{2,1,0:T(8,128)(2,1)}, u32[]{:S(2)}, u32[]{:S(2)}) async-start(bf16[64,64,512]{2,1,0:T(8,128)(2,1)} %bitcast.29), calls=%async_computation.2 | async-start | bytes 8388608 | tf_op jit(solution)/shard_map/all_to_all | solution.py:526
  93.1 7.8 %values.1 = bf16[8,32,512]{2,1,0:T(8,128)(2,1)} custom-call(s32[5]{0:T(128)} %stack.88.me.where, bf16[8,4,2,2,32,512]{5,4,3,2,1,0:T(8,128)(2,1)} %bitcast.30, bf16[4,512,512]{2,1,0:T(8,128)(2,1)} %copy-done.3, bf16[4,512,512]{2,1,0:T(8,128)(2,1)} %copy-done.4, bf16[4,512,512]{2,1,0:T(8,128)(2,1)} %copy-done.5, ...), custom_call_target="tpu_custom_call" | custom-call | flops 1 | bytes 1 | tf_op jit(solution)/shard_map/values/pallas_call | solution.py:286
  101.8 3.3 %collective-permute-start.16 = (bf16[4,32,512]{2,1,0:T(8,128)(2,1)S(1)}, bf16[4,32,512]{2,1,0:T(8,128)(2,1)S(1)}, u32[]{:S(2)}, u32[]{:S(2)}) collective-permute-start(bf16[4,32,512]{2,1,0:T(8,128)(2,1)S(1)} %constant_dynamic-slice_fusion.8), channel_id=1, source_target_pairs={{0,64},{16,80},{32,96},{48,112},{64,0},{80,16},{96,32},{112,48},{1... | collective-permute-start | bytes 393224 | tf_op jit(solution)/shard_map/ppermute | solution.py:538
  105.2 10.1 %grad_rows.1 = bf16[256,8192]{1,0:T(8,128)(2,1)} custom-call(s32[5]{0:T(128)} %stack.88.me.where, bf16[256,512]{1,0:T(8,128)(2,1)} %get-tuple-element.63.dv, bf16[4,512,512]{2,1,0:T(8,128)(2,1)} %copy-done.3, bf16[4,512,512]{2,1,0:T(8,128)(2,1)} %copy-done.4, bf16[4,512,512]{2,1,0:T(8,128)(2,1)} %copy-done.5, ...), custom_call_target="tpu_custom_call" | custom-call | flops 1 | bytes 1 | tf_op jit(solution)/shard_map/grad_rows/pallas_call | solution.py:333
  115.3 32.7 %collective-permute-done.16 = bf16[4,32,512]{2,1,0:T(8,128)(2,1)S(1)} collective-permute-done((bf16[4,32,512]{2,1,0:T(8,128)(2,1)S(1)}, bf16[4,32,512]{2,1,0:T(8,128)(2,1)S(1)}, u32[]{:S(2)}, u32[]{:S(2)}) %collective-permute-start.16) | collective-permute-done | bytes 131104 | tf_op jit(solution)/shard_map/ppermute | solution.py:538
  148.0 3.5 %weight_product.2 = bf16[512,512]{1,0:T(8,128)(2,1)S(1)} custom-call(s32[5]{0:T(128)S(1)} %copy-done.1, bf16[8,4,2,2,32,512]{5,4,3,2,1,0:T(8,128)(2,1)} %bitcast.22.rows, bf16[4,512,256]{2,1,0:T(8,128)(2,1)S(1)} %pad_maximum_fusion.2.near, bf16[4,512,256]{2,1,0:T(8,128)(2,1)S(1)} %collective-permute-done.15.far), custom_call_target="tpu_custom_call" | custom-call | flops 1 | bytes 1 | tf_op jit(solution)/shard_map/weight_product/pallas_call | solution.py:430
  151.4 3.1 %collective-permute-start.17 = (bf16[512,512]{1,0:T(8,128)(2,1)S(1)}, bf16[512,512]{1,0:T(8,128)(2,1)S(1)}, u32[]{:S(2)}, u32[]{:S(2)}) collective-permute-start(bf16[512,512]{1,0:T(8,128)(2,1)S(1)} %weight_product.2), channel_id=1, source_target_pairs={{0,8},{1,9},{2,10},{3,11},{4,12},{5,13},{6,14},{7,15},{8,0},{9,1},... | collective-permute-start | bytes 1572872 | tf_op jit(solution)/shard_map/ppermute | solution.py:452
  154.6 3.8 %collective-permute-start.19 = (bf16[2,32,512]{2,1,0:T(8,128)(2,1)S(1)}, bf16[2,32,512]{2,1,0:T(8,128)(2,1)S(1)}, u32[]{:S(2)}, u32[]{:S(2)}) collective-permute-start(bf16[2,32,512]{2,1,0:T(8,128)(2,1)S(1)} %pad_maximum_fusion.6), channel_id=1, source_target_pairs={{0,32},{16,48},{32,0},{48,16},{64,96},{80,112},{96,64},{112,80},{1... | collective-permute-start | bytes 196616 | tf_op jit(solution)/shard_map/ppermute | solution.py:547
  158.4 2.7 %collective-permute-start.20 = (bf16[2,32,512]{2,1,0:T(8,128)(2,1)S(1)}, bf16[2,32,512]{2,1,0:T(8,128)(2,1)S(1)}, u32[]{:S(2)}, u32[]{:S(2)}) collective-permute-start(bf16[2,32,512]{2,1,0:T(8,128)(2,1)S(1)} %pad_maximum_fusion.7), channel_id=1, source_target_pairs={{0,48},{16,0},{32,16},{48,32},{64,112},{80,64},{96,80},{112,96},{1... | collective-permute-start | bytes 196616 | tf_op jit(solution)/shard_map/ppermute | solution.py:547
  161.1 3.6 %weight_product.3 = f32[512,512]{1,0:T(8,128)S(1)} custom-call(s32[5]{0:T(128)S(1)} %copy-done.1, bf16[8,4,2,2,32,512]{5,4,3,2,1,0:T(8,128)(2,1)} %bitcast.22.rows, bf16[4,512,256]{2,1,0:T(8,128)(2,1)S(1)} %pad_maximum_fusion.2.near, bf16[4,512,256]{2,1,0:T(8,128)(2,1)S(1)} %collective-permute-done.15.far), custom_call_target="tpu_custom_call" | custom-call | flops 1 | bytes 1 | tf_op jit(solution)/shard_map/weight_product/pallas_call | solution.py:430
  164.7 3.1 %attend.1 = bf16[256,4096]{1,0:T(8,128)(2,1)} custom-call(s32[8]{0:T(128)S(1)} %copy-done.2, s32[5]{0:T(128)S(1)} %copy-done.1, bf16[8,256,128]{2,1,0:T(8,128)(2,1)S(1)} %copy-done, bf16[2,32,512]{2,1,0:T(8,128)(2,1)S(1)} %pad_maximum_fusion.4.rest_0_, bf16[2,32,512]{2,1,0:T(8,128)(2,1)S(1)} %collective-permute-done.18.rest_1_, ...), custom_call_target="tpu_custom_call" | custom-call | flops 1 | bytes 1 | tf_op jit(solution)/shard_map/attend/pallas_call | solution.py:394
  (67 shorter events, 11.7 us)
Async XLA Ops:
  0.6 24.3 %collective-permute-start.1 = (bf16[512,512]{1,0:T(8,128)(2,1)}, bf16[512,512]{1,0:T(8,128)(2,1)S(1)}, u32[]{:S(2)}, u32[]{:S(2)}) collective-permute-start(bf16[512,512]{1,0:T(8,128)(2,1)} %param.17), channel_id=1, source_target_pairs={{0,2},{1,3},{2,4},{3,5},{4,6},{5,7},{6,0},{7,1},{8,10},{9,11},{10,... | collective-permute-start | bytes 1572872 | tf_op jit(solution)/shard_map/ppermute | solution.py:458
  2.2 22.7 %collective-permute-start = (bf16[512,512]{1,0:T(8,128)(2,1)}, bf16[512,512]{1,0:T(8,128)(2,1)S(1)}, u32[]{:S(2)}, u32[]{:S(2)}) collective-permute-start(bf16[512,512]{1,0:T(8,128)(2,1)} %param.17), channel_id=1, source_target_pairs={{0,8},{1,9},{2,10},{3,11},{4,12},{5,13},{6,14},{7,15},{8,0},{9,1},... | collective-permute-start | bytes 1572872 | tf_op jit(solution)/shard_map/ppermute | solution.py:452
  3.8 21.1 %collective-permute-start.2 = (bf16[512,512]{1,0:T(8,128)(2,1)}, bf16[512,512]{1,0:T(8,128)(2,1)S(1)}, u32[]{:S(2)}, u32[]{:S(2)}) collective-permute-start(bf16[512,512]{1,0:T(8,128)(2,1)} %param.17), channel_id=1, source_target_pairs={{0,6},{1,7},{2,0},{3,1},{4,2},{5,3},{6,4},{7,5},{8,14},{9,15},{10,... | collective-permute-start | bytes 1572872 | tf_op jit(solution)/shard_map/ppermute | solution.py:458
  5.7 19.2 %all-to-all-start = ((f32[128,1,32]{2,1,0:T(1,128)}), f32[128,1,32]{2,1,0:T(1,128)S(1)}, u32[]{:S(2)}, u32[]{:S(2)}) async-start(f32[128,1,32]{2,1,0:T(1,128)} %bitcast.43), calls=%async_computation | async-start | bytes 131072 | tf_op jit(solution)/shard_map/all_to_all | solution.py:490
  25.5 53.8 %all-to-all-start.1 = ((bf16[8,512,512]{2,1,0:T(8,128)(2,1)}), bf16[8,512,512]{2,1,0:T(8,128)(2,1)}, u32[]{:S(2)}, u32[]{:S(2)}) async-start(bf16[8,512,512]{2,1,0:T(8,128)(2,1)} %bitcast.31), calls=%async_computation.1 | async-start | bytes 8388608 | tf_op jit(solution)/shard_map/all_to_all | solution.py:497
  30.1 17.1 %collective-permute-start.7 = (bf16[512,512]{1,0:T(8,128)(2,1)S(1)}, bf16[512,512]{1,0:T(8,128)(2,1)S(1)}, u32[]{:S(2)}, u32[]{:S(2)}) collective-permute-start(bf16[512,512]{1,0:T(8,128)(2,1)S(1)} %collective-permute-done), channel_id=1, source_target_pairs={{0,6},{1,7},{2,0},{3,1},{4,2},{5,3},{6,4},{7,5},{8,14},{9,15},{10,... | collective-permute-start | bytes 1572872 | tf_op jit(solution)/shard_map/ppermute | solution.py:458
  31.6 17.2 %collective-permute-start.5 = (bf16[512,512]{1,0:T(8,128)(2,1)S(1)}, bf16[512,512]{1,0:T(8,128)(2,1)S(1)}, u32[]{:S(2)}, u32[]{:S(2)}) collective-permute-start(bf16[512,512]{1,0:T(8,128)(2,1)S(1)} %collective-permute-done), channel_id=1, source_target_pairs={{0,2},{1,3},{2,4},{3,5},{4,6},{5,7},{6,0},{7,1},{8,10},{9,11},{10,... | collective-permute-start | bytes 1572872 | tf_op jit(solution)/shard_map/ppermute | solution.py:458
  32.2 18.1 %collective-permute-start.4 = (bf16[256,512]{1,0:T(8,128)(2,1)S(1)}, bf16[256,512]{1,0:T(8,128)(2,1)S(1)}, u32[]{:S(2)}, u32[]{:S(2)}) collective-permute-start(bf16[256,512]{1,0:T(8,128)(2,1)S(1)} %slice.19), channel_id=1, source_target_pairs={{0,6},{1,7},{2,0},{3,1},{4,2},{5,3},{6,4},{7,5},{8,14},{9,15},{10,... | collective-permute-start | bytes 786440 | tf_op jit(solution)/shard_map/ppermute | solution.py:458
  33.7 17.0 %collective-permute-start.3 = (bf16[256,512]{1,0:T(8,128)(2,1)S(1)}, bf16[256,512]{1,0:T(8,128)(2,1)}, u32[]{:S(2)}, u32[]{:S(2)}) collective-permute-start(bf16[256,512]{1,0:T(8,128)(2,1)S(1)} %slice.18), channel_id=1, source_target_pairs={{0,2},{1,3},{2,4},{3,5},{4,6},{5,7},{6,0},{7,1},{8,10},{9,11},{10,... | collective-permute-start | bytes 786440 | tf_op jit(solution)/shard_map/ppermute | solution.py:458
  47.1 4.6 %copy-start.7 = (bf16[512,512]{1,0:T(8,128)(2,1)S(1)}, bf16[512,512]{1,0:T(8,128)(2,1)}, u32[]{:S(2)}) copy-start(bf16[512,512]{1,0:T(8,128)(2,1)} %param.17) | copy-start | bytes 1572868
  47.2 7.9 %collective-permute-start.8 = (bf16[256,512]{1,0:T(8,128)(2,1)S(1)}, bf16[256,512]{1,0:T(8,128)(2,1)S(1)}, u32[]{:S(2)}, u32[]{:S(2)}) collective-permute-start(bf16[256,512]{1,0:T(8,128)(2,1)S(1)} %slice.25), channel_id=1, source_target_pairs={{0,6},{1,7},{2,0},{3,1},{4,2},{5,3},{6,4},{7,5},{8,14},{9,15},{10,... | collective-permute-start | bytes 786440 | tf_op jit(solution)/shard_map/ppermute | solution.py:458
  48.8 8.3 %collective-permute-start.6 = (bf16[256,512]{1,0:T(8,128)(2,1)S(1)}, bf16[256,512]{1,0:T(8,128)(2,1)S(1)}, u32[]{:S(2)}, u32[]{:S(2)}) collective-permute-start(bf16[256,512]{1,0:T(8,128)(2,1)S(1)} %slice.24), channel_id=1, source_target_pairs={{0,2},{1,3},{2,4},{3,5},{4,6},{5,7},{6,0},{7,1},{8,10},{9,11},{10,... | collective-permute-start | bytes 786440 | tf_op jit(solution)/shard_map/ppermute | solution.py:458
  52.0 5.4 %copy-start.3 = (bf16[4,512,512]{2,1,0:T(8,128)(2,1)}, bf16[4,512,512]{2,1,0:T(8,128)(2,1)S(1)}, u32[]{:S(2)}) copy-start(bf16[4,512,512]{2,1,0:T(8,128)(2,1)S(1)} %pad_maximum_fusion.rest_0_) | copy-start | bytes 6291460
  52.0 25.2 %collective-permute-start.9 = (bf16[4,512,512]{2,1,0:T(8,128)(2,1)S(1)}, bf16[4,512,512]{2,1,0:T(8,128)(2,1)S(1)}, u32[]{:S(2)}, u32[]{:S(2)}) collective-permute-start(bf16[4,512,512]{2,1,0:T(8,128)(2,1)S(1)} %pad_maximum_fusion.rest_0_), channel_id=1, source_target_pairs={{0,1},{1,0},{2,3},{3,2},{4,5},{5,4},{6,7},{7,6},{8,9},{9,8},{10,11... | collective-permute-start | bytes 6291464 | tf_op jit(solution)/shard_map/ppermute | solution.py:473
  57.4 19.8 %copy-start.4 = (bf16[4,512,512]{2,1,0:T(8,128)(2,1)}, bf16[4,512,512]{2,1,0:T(8,128)(2,1)S(1)}, u32[]{:S(2)}) copy-start(bf16[4,512,512]{2,1,0:T(8,128)(2,1)S(1)} %pad_maximum_fusion.1.rest_1_) | copy-start | bytes 6291460
  57.4 21.1 %collective-permute-start.10 = (bf16[4,512,512]{2,1,0:T(8,128)(2,1)S(1)}, bf16[4,512,512]{2,1,0:T(8,128)(2,1)}, u32[]{:S(2)}, u32[]{:S(2)}) collective-permute-start(bf16[4,512,512]{2,1,0:T(8,128)(2,1)S(1)} %pad_maximum_fusion.1.rest_1_), channel_id=1, source_target_pairs={{0,1},{1,0},{2,3},{3,2},{4,5},{5,4},{6,7},{7,6},{8,9},{9,8},{10,11... | collective-permute-start | bytes 6291464 | tf_op jit(solution)/shard_map/ppermute | solution.py:473
  58.1 8.6 %collective-permute-start.13 = (bf16[512,256]{1,0:T(8,128)(2,1)S(1)}, bf16[512,256]{1,0:T(8,128)(2,1)S(1)}, u32[]{:S(2)}, u32[]{:S(2)}) collective-permute-start(bf16[512,256]{1,0:T(8,128)(2,1)S(1)} %copy-done.9), channel_id=1, source_target_pairs={{0,6},{1,7},{2,0},{3,1},{4,2},{5,3},{6,4},{7,5},{8,14},{9,15},{10,... | collective-permute-start | bytes 786440 | tf_op jit(solution)/shard_map/ppermute | solution.py:458
  61.0 8.2 %collective-permute-start.11 = (bf16[512,256]{1,0:T(8,128)(2,1)S(1)}, bf16[512,256]{1,0:T(8,128)(2,1)S(1)}, u32[]{:S(2)}, u32[]{:S(2)}) collective-permute-start(bf16[512,256]{1,0:T(8,128)(2,1)S(1)} %copy-done.9), channel_id=1, source_target_pairs={{0,2},{1,3},{2,4},{3,5},{4,6},{5,7},{6,0},{7,1},{8,10},{9,11},{10,... | collective-permute-start | bytes 786440 | tf_op jit(solution)/shard_map/ppermute | solution.py:458
  66.7 5.1 %collective-permute-start.14 = (bf16[256,256]{1,0:T(8,128)(2,1)S(1)}, bf16[256,256]{1,0:T(8,128)(2,1)S(1)}, u32[]{:S(2)}, u32[]{:S(2)}) collective-permute-start(bf16[256,256]{1,0:T(8,128)(2,1)S(1)} %slice.27), channel_id=1, source_target_pairs={{0,6},{1,7},{2,0},{3,1},{4,2},{5,3},{6,4},{7,5},{8,14},{9,15},{10,... | collective-permute-start | bytes 393224 | tf_op jit(solution)/shard_map/ppermute | solution.py:458
  69.3 5.0 %collective-permute-start.12 = (bf16[256,256]{1,0:T(8,128)(2,1)S(1)}, bf16[256,256]{1,0:T(8,128)(2,1)S(1)}, u32[]{:S(2)}, u32[]{:S(2)}) collective-permute-start(bf16[256,256]{1,0:T(8,128)(2,1)S(1)} %slice.26), channel_id=1, source_target_pairs={{0,2},{1,3},{2,4},{3,5},{4,6},{5,7},{6,0},{7,1},{8,10},{9,11},{10,... | collective-permute-start | bytes 393224 | tf_op jit(solution)/shard_map/ppermute | solution.py:458
  74.5 2.7 %collective-permute-start.15 = (bf16[4,512,256]{2,1,0:T(8,128)(2,1)S(1)}, bf16[4,512,256]{2,1,0:T(8,128)(2,1)S(1)}, u32[]{:S(2)}, u32[]{:S(2)}) collective-permute-start(bf16[4,512,256]{2,1,0:T(8,128)(2,1)S(1)} %pad_maximum_fusion.2.near), channel_id=1, source_target_pairs={{0,1},{1,0},{2,3},{3,2},{4,5},{5,4},{6,7},{7,6},{8,9},{9,8},{10,11... | collective-permute-start | bytes 3145736 | tf_op jit(solution)/shard_map/ppermute | solution.py:473
  77.2 1.3 copy-start.5
  83.6 64.4 %all-to-all-start.2 = ((bf16[64,64,512]{2,1,0:T(8,128)(2,1)}), bf16[64,64,512]{2,1,0:T(8,128)(2,1)}, u32[]{:S(2)}, u32[]{:S(2)}) async-start(bf16[64,64,512]{2,1,0:T(8,128)(2,1)} %bitcast.29), calls=%async_computation.2 | async-start | bytes 8388608 | tf_op jit(solution)/shard_map/all_to_all | solution.py:526
  101.8 46.1 %collective-permute-start.16 = (bf16[4,32,512]{2,1,0:T(8,128)(2,1)S(1)}, bf16[4,32,512]{2,1,0:T(8,128)(2,1)S(1)}, u32[]{:S(2)}, u32[]{:S(2)}) collective-permute-start(bf16[4,32,512]{2,1,0:T(8,128)(2,1)S(1)} %constant_dynamic-slice_fusion.8), channel_id=1, source_target_pairs={{0,64},{16,80},{32,96},{48,112},{64,0},{80,16},{96,32},{112,48},{1... | collective-permute-start | bytes 393224 | tf_op jit(solution)/shard_map/ppermute | solution.py:538
  105.1 10.1 %copy-start.6 = (bf16[8,32,512]{2,1,0:T(8,128)(2,1)S(1)}, bf16[8,32,512]{2,1,0:T(8,128)(2,1)}, u32[]{:S(2)}) copy-start(bf16[8,32,512]{2,1,0:T(8,128)(2,1)} %values.1) | copy-start | bytes 786436
  105.1 42.8 %copy-start.1 = (s32[5]{0:T(128)S(1)}, s32[5]{0:T(128)}, u32[]{:S(2)}) copy-start(s32[5]{0:T(128)} %stack.88.me.where) | copy-start | bytes 64
  151.4 16.4 %collective-permute-start.17 = (bf16[512,512]{1,0:T(8,128)(2,1)S(1)}, bf16[512,512]{1,0:T(8,128)(2,1)S(1)}, u32[]{:S(2)}, u32[]{:S(2)}) collective-permute-start(bf16[512,512]{1,0:T(8,128)(2,1)S(1)} %weight_product.2), channel_id=1, source_target_pairs={{0,8},{1,9},{2,10},{3,11},{4,12},{5,13},{6,14},{7,15},{8,0},{9,1},... | collective-permute-start | bytes 1572872 | tf_op jit(solution)/shard_map/ppermute | solution.py:452
  154.5 10.2 %collective-permute-start.18 = (bf16[2,32,512]{2,1,0:T(8,128)(2,1)S(1)}, bf16[2,32,512]{2,1,0:T(8,128)(2,1)S(1)}, u32[]{:S(2)}, u32[]{:S(2)}) collective-permute-start(bf16[2,32,512]{2,1,0:T(8,128)(2,1)S(1)} %pad_maximum_fusion.5), channel_id=1, source_target_pairs={{0,16},{16,32},{32,48},{48,0},{64,80},{80,96},{96,112},{112,64},{1... | collective-permute-start | bytes 196616 | tf_op jit(solution)/shard_map/ppermute | solution.py:547
  154.6 10.1 %collective-permute-start.19 = (bf16[2,32,512]{2,1,0:T(8,128)(2,1)S(1)}, bf16[2,32,512]{2,1,0:T(8,128)(2,1)S(1)}, u32[]{:S(2)}, u32[]{:S(2)}) collective-permute-start(bf16[2,32,512]{2,1,0:T(8,128)(2,1)S(1)} %pad_maximum_fusion.6), channel_id=1, source_target_pairs={{0,32},{16,48},{32,0},{48,16},{64,96},{80,112},{96,64},{112,80},{1... | collective-permute-start | bytes 196616 | tf_op jit(solution)/shard_map/ppermute | solution.py:547
  158.4 6.3 %copy-start = (bf16[8,256,128]{2,1,0:T(8,128)(2,1)S(1)}, bf16[8,256,128]{2,1,0:T(8,128)(2,1)}, u32[]{:S(2)}) copy-start(bf16[8,256,128]{2,1,0:T(8,128)(2,1)} %get-tuple-element.69.probs) | copy-start | bytes 1572868
  158.4 6.3 %copy-start.2 = (s32[8]{0:T(128)S(1)}, s32[8]{0:T(128)}, u32[]{:S(2)}) copy-start(s32[8]{0:T(128)} %get-tuple-element.46.colours) | copy-start | bytes 100
  158.4 6.3 %collective-permute-start.20 = (bf16[2,32,512]{2,1,0:T(8,128)(2,1)S(1)}, bf16[2,32,512]{2,1,0:T(8,128)(2,1)S(1)}, u32[]{:S(2)}, u32[]{:S(2)}) collective-permute-start(bf16[2,32,512]{2,1,0:T(8,128)(2,1)S(1)} %pad_maximum_fusion.7), channel_id=1, source_target_pairs={{0,48},{16,0},{32,16},{48,32},{64,112},{80,64},{96,80},{112,96},{1... | collective-permute-start | bytes 196616 | tf_op jit(solution)/shard_map/ppermute | solution.py:547
  (2 other events, 1.6 us)

commit v5 on v4

--- a/solution.py
+++ b/solution.py
@@ -390,7 +390,7 @@
     group = span // seq
     width = kv * group * HD
     levels = len(values)
-    each = 2
+    each = 4
     return pl.pallas_call(
         functools.partial(attend_body, kv, group, levels, each),
         grid_spec=pltpu.PrefetchScalarGridSpec(

time: 170 us -> 169 us (level)
  no operation moved by 1% of the time
where the time goes in v5:
time: 169 us; the launch traced here: 168 us
  waiting for transfers between devices  57.9 us (34%)
  starting transfers between devices  53 us (31%)
  Pallas kernels  49.5 us (29%)
  local copies, waits for them, and re-layouts  4.16 us (2%)
  other arithmetic  2.69 us (2%)
    ppermute x1, waiting for transfers between devices, shards(): got = lax.ppermute(give, 'dp', [(i, (i + 4) % dp) for i in range(dp)])  32.7 us
    ppermute x12, waiting for transfers between devices, step_along(): return lax.ppermute(x, 'fsdp', to)  17 us
    ppermute x12, starting transfers between devices, step_along(): return lax.ppermute(x, 'fsdp', to)  14 us
    pallas_call x1, Pallas kernels, probs_and_dvalues(): pl.pallas_call(functools.partial(probs_body, kv, group, slots), grid_spec...  10.4 us
    all_to_all x1, starting transfers between devices, shards(): lax.all_to_all(info, ('dp', 'fsdp'), split_axis=0, concat_axis=0, tiled=T...  10.2 us
    pallas_call x1, Pallas kernels, grad_rows_of(): pl.pallas_call(grad_rows_body, grid_spec=pltpu.PrefetchScalarGridSpec(num...  10.1 us
    all_to_all x1, starting transfers between devices, shards(): lax.all_to_all(rows.reshape(dp * half, 2 * seq, part), ('dp', 'fsdp'), sp...  9.42 us
    pallas_call x1, Pallas kernels, values_of(): pl.pallas_call(functools.partial(values_body, around), grid_spec=pltpu.Pr...  7.79 us
  transfers between devices with their start and end apart: 24, of which 11 were waited for; matrix products, arithmetic and copies ran while one was open for 2% of the time, Pallas kernels for 25%

profile of v5, /device:TPU:2, one launch (start us, length us, event | category | flops | bytes accessed | tf_op | source)
XLA Modules:
  0.0 168.2 jit_solution(12370545166026157077)
XLA Ops:
  0.6 1.6 collective-permute-start.1
  2.2 1.6 collective-permute-start
  4.3 1.4 prepare.1
  5.7 10.2 %all-to-all-start = ((f32[128,1,32]{2,1,0:T(1,128)}), f32[128,1,32]{2,1,0:T(1,128)S(1)}, u32[]{:S(2)}, u32[]{:S(2)}) async-start(f32[128,1,32]{2,1,0:T(1,128)} %bitcast.43), calls=%async_computation | async-start | bytes 131072 | tf_op jit(solution)/shard_map/all_to_all | solution.py:490
  15.9 4.2 %pack_rows.1 = bf16[8,16,32,512]{3,2,1,0:T(8,128)(2,1)} custom-call(s32[9]{0:T(128)} %get-tuple-element.39.order, bf16[8,32,8192]{2,1,0:T(8,128)(2,1)} %rows.1), custom_call_target="tpu_custom_call" | custom-call | bytes 8388608 | tf_op jit(solution)/shard_map/pack_rows/pallas_call | solution.py:77
  20.1 4.8 %all-to-all-done = f32[128,1,32]{2,1,0:T(1,128)S(1)} async-done(((f32[128,1,32]{2,1,0:T(1,128)}), f32[128,1,32]{2,1,0:T(1,128)S(1)}, u32[]{:S(2)}, u32[]{:S(2)}) %all-to-all-start) | async-done | bytes 16416 | tf_op jit(solution)/shard_map/all_to_all | solution.py:490
  25.5 4.5 %all-to-all-start.1 = ((bf16[8,512,512]{2,1,0:T(8,128)(2,1)}), bf16[8,512,512]{2,1,0:T(8,128)(2,1)}, u32[]{:S(2)}, u32[]{:S(2)}) async-start(bf16[8,512,512]{2,1,0:T(8,128)(2,1)} %bitcast.31), calls=%async_computation.1 | async-start | bytes 8388608 | tf_op jit(solution)/shard_map/all_to_all | solution.py:497
  30.1 1.5 collective-permute-start.7
  32.2 1.5 collective-permute-start.4
  34.9 1.7 %plan_slots.1 = (s32[8]{0:T(128)}, s32[8]{0:T(128)}, f32[8,128]{1,0:T(8,128)}) custom-call(s32[5]{0:T(128)} %stack.88.me.where, f32[128,32]{1,0:T(8,128)} %bitcast.41), custom_call_target="tpu_custom_call" | custom-call | flops 1 | bytes 1 | tf_op jit(solution)/shard_map/plan_slots/pallas_call | solution.py:167
  36.7 10.4 %probs_dvalues.1 = (bf16[256,512]{1,0:T(8,128)(2,1)}, bf16[512,256]{1,0:T(8,128)(2,1)}, bf16[8,256,128]{2,1,0:T(8,128)(2,1)}) custom-call(s32[8]{0:T(128)} %get-tuple-element.45.length, s32[8]{0:T(128)} %get-tuple-element.46.colours, f32[8,128]{1,0:T(8,128)} %get-tuple-element.47.factor, bf16[256,4096]{1,0:T(8,128)(2,1)} %q.1, bf16[256,512]{1,0:T(8,128)(2,1)} %k.1, ...), custom_call_target="tpu_custom_call" | custom-call | flops 1 | bytes 1 | tf_op jit(solution)/shard_map/probs_dvalues/pallas_call | solution.py:226
  47.2 1.6 collective-permute-start.8
  52.1 3.0 %collective-permute-done.8 = bf16[256,512]{1,0:T(8,128)(2,1)S(1)} collective-permute-done((bf16[256,512]{1,0:T(8,128)(2,1)S(1)}, bf16[256,512]{1,0:T(8,128)(2,1)S(1)}, u32[]{:S(2)}, u32[]{:S(2)}) %collective-permute-start.8) | collective-permute-done | bytes 262176 | tf_op jit(solution)/shard_map/ppermute | solution.py:458
  55.1 2.0 %collective-permute-done.6 = bf16[256,512]{1,0:T(8,128)(2,1)S(1)} collective-permute-done((bf16[256,512]{1,0:T(8,128)(2,1)S(1)}, bf16[256,512]{1,0:T(8,128)(2,1)S(1)}, u32[]{:S(2)}, u32[]{:S(2)}) %collective-permute-start.6) | collective-permute-done | bytes 262176 | tf_op jit(solution)/shard_map/ppermute | solution.py:458
  58.1 3.0 %collective-permute-start.13 = (bf16[512,256]{1,0:T(8,128)(2,1)S(1)}, bf16[512,256]{1,0:T(8,128)(2,1)S(1)}, u32[]{:S(2)}, u32[]{:S(2)}) collective-permute-start(bf16[512,256]{1,0:T(8,128)(2,1)S(1)} %copy-done.9), channel_id=1, source_target_pairs={{0,6},{1,7},{2,0},{3,1},{4,2},{5,3},{6,4},{7,5},{8,14},{9,15},{10,... | collective-permute-start | bytes 786440 | tf_op jit(solution)/shard_map/ppermute | solution.py:458
  61.0 5.7 %collective-permute-done.13 = bf16[512,256]{1,0:T(8,128)(2,1)S(1)} collective-permute-done((bf16[512,256]{1,0:T(8,128)(2,1)S(1)}, bf16[512,256]{1,0:T(8,128)(2,1)S(1)}, u32[]{:S(2)}, u32[]{:S(2)}) %collective-permute-start.13) | collective-permute-done | bytes 262176 | tf_op jit(solution)/shard_map/ppermute | solution.py:458
  66.7 2.6 %collective-permute-start.14 = (bf16[256,256]{1,0:T(8,128)(2,1)S(1)}, bf16[256,256]{1,0:T(8,128)(2,1)S(1)}, u32[]{:S(2)}, u32[]{:S(2)}) collective-permute-start(bf16[256,256]{1,0:T(8,128)(2,1)S(1)} %slice.27), channel_id=1, source_target_pairs={{0,6},{1,7},{2,0},{3,1},{4,2},{5,3},{6,4},{7,5},{8,14},{9,15},{10,... | collective-permute-start | bytes 393224 | tf_op jit(solution)/shard_map/ppermute | solution.py:458
  69.4 2.4 %collective-permute-done.14 = bf16[256,256]{1,0:T(8,128)(2,1)S(1)} collective-permute-done((bf16[256,256]{1,0:T(8,128)(2,1)S(1)}, bf16[256,256]{1,0:T(8,128)(2,1)S(1)}, u32[]{:S(2)}, u32[]{:S(2)}) %collective-permute-start.14) | collective-permute-done | bytes 131104 | tf_op jit(solution)/shard_map/ppermute | solution.py:458
  71.8 2.5 %collective-permute-done.12 = bf16[256,256]{1,0:T(8,128)(2,1)S(1)} collective-permute-done((bf16[256,256]{1,0:T(8,128)(2,1)S(1)}, bf16[256,256]{1,0:T(8,128)(2,1)S(1)}, u32[]{:S(2)}, u32[]{:S(2)}) %collective-permute-start.12) | collective-permute-done | bytes 131104 | tf_op jit(solution)/shard_map/ppermute | solution.py:458
  74.6 2.6 %collective-permute-done.15.far = bf16[4,512,256]{2,1,0:T(8,128)(2,1)S(1)} collective-permute-done((bf16[4,512,256]{2,1,0:T(8,128)(2,1)S(1)}, bf16[4,512,256]{2,1,0:T(8,128)(2,1)S(1)}, u32[]{:S(2)}, u32[]{:S(2)}) %collective-permute-start.15) | collective-permute-done | bytes 1048608 | tf_op jit(solution)/shard_map/ppermute | solution.py:473
  79.3 4.3 %turn_rows.1 = bf16[8,512,512]{2,1,0:T(8,128)(2,1)} custom-call(s32[9]{0:T(128)} %get-tuple-element.39.order, bf16[8,512,512]{2,1,0:T(8,128)(2,1)} %all-to-all-done.1.rows), custom_call_target="tpu_custom_call" | custom-call | bytes 8388608 | tf_op jit(solution)/shard_map/turn_rows/pallas_call | solution.py:113
  83.6 9.4 %all-to-all-start.2 = ((bf16[64,64,512]{2,1,0:T(8,128)(2,1)}), bf16[64,64,512]{2,1,0:T(8,128)(2,1)}, u32[]{:S(2)}, u32[]{:S(2)}) async-start(bf16[64,64,512]{2,1,0:T(8,128)(2,1)} %bitcast.29), calls=%async_computation.2 | async-start | bytes 8388608 | tf_op jit(solution)/shard_map/all_to_all | solution.py:526
  93.0 7.8 %values.1 = bf16[8,32,512]{2,1,0:T(8,128)(2,1)} custom-call(s32[5]{0:T(128)} %stack.88.me.where, bf16[8,4,2,2,32,512]{5,4,3,2,1,0:T(8,128)(2,1)} %bitcast.30, bf16[4,512,512]{2,1,0:T(8,128)(2,1)} %copy-done.3, bf16[4,512,512]{2,1,0:T(8,128)(2,1)} %copy-done.4, bf16[4,512,512]{2,1,0:T(8,128)(2,1)} %copy-done.5, ...), custom_call_target="tpu_custom_call" | custom-call | flops 1 | bytes 1 | tf_op jit(solution)/shard_map/values/pallas_call | solution.py:286
  101.8 3.3 %collective-permute-start.16 = (bf16[4,32,512]{2,1,0:T(8,128)(2,1)S(1)}, bf16[4,32,512]{2,1,0:T(8,128)(2,1)S(1)}, u32[]{:S(2)}, u32[]{:S(2)}) collective-permute-start(bf16[4,32,512]{2,1,0:T(8,128)(2,1)S(1)} %constant_dynamic-slice_fusion.8), channel_id=1, source_target_pairs={{0,64},{16,80},{32,96},{48,112},{64,0},{80,16},{96,32},{112,48},{1... | collective-permute-start | bytes 393224 | tf_op jit(solution)/shard_map/ppermute | solution.py:538
  105.1 10.1 %grad_rows.1 = bf16[256,8192]{1,0:T(8,128)(2,1)} custom-call(s32[5]{0:T(128)} %stack.88.me.where, bf16[256,512]{1,0:T(8,128)(2,1)} %get-tuple-element.63.dv, bf16[4,512,512]{2,1,0:T(8,128)(2,1)} %copy-done.3, bf16[4,512,512]{2,1,0:T(8,128)(2,1)} %copy-done.4, bf16[4,512,512]{2,1,0:T(8,128)(2,1)} %copy-done.5, ...), custom_call_target="tpu_custom_call" | custom-call | flops 1 | bytes 1 | tf_op jit(solution)/shard_map/grad_rows/pallas_call | solution.py:333
  115.2 32.7 %collective-permute-done.16 = bf16[4,32,512]{2,1,0:T(8,128)(2,1)S(1)} collective-permute-done((bf16[4,32,512]{2,1,0:T(8,128)(2,1)S(1)}, bf16[4,32,512]{2,1,0:T(8,128)(2,1)S(1)}, u32[]{:S(2)}, u32[]{:S(2)}) %collective-permute-start.16) | collective-permute-done | bytes 131104 | tf_op jit(solution)/shard_map/ppermute | solution.py:538
  147.9 3.5 %weight_product.2 = bf16[512,512]{1,0:T(8,128)(2,1)S(1)} custom-call(s32[5]{0:T(128)S(1)} %copy-done.1, bf16[8,4,2,2,32,512]{5,4,3,2,1,0:T(8,128)(2,1)} %bitcast.22.rows, bf16[4,512,256]{2,1,0:T(8,128)(2,1)S(1)} %pad_maximum_fusion.2.near, bf16[4,512,256]{2,1,0:T(8,128)(2,1)S(1)} %collective-permute-done.15.far), custom_call_target="tpu_custom_call" | custom-call | flops 1 | bytes 1 | tf_op jit(solution)/shard_map/weight_product/pallas_call | solution.py:430
  151.4 3.1 %collective-permute-start.17 = (bf16[512,512]{1,0:T(8,128)(2,1)S(1)}, bf16[512,512]{1,0:T(8,128)(2,1)S(1)}, u32[]{:S(2)}, u32[]{:S(2)}) collective-permute-start(bf16[512,512]{1,0:T(8,128)(2,1)S(1)} %weight_product.2), channel_id=1, source_target_pairs={{0,8},{1,9},{2,10},{3,11},{4,12},{5,13},{6,14},{7,15},{8,0},{9,1},... | collective-permute-start | bytes 1572872 | tf_op jit(solution)/shard_map/ppermute | solution.py:452
  154.6 3.8 %collective-permute-start.19 = (bf16[2,32,512]{2,1,0:T(8,128)(2,1)S(1)}, bf16[2,32,512]{2,1,0:T(8,128)(2,1)S(1)}, u32[]{:S(2)}, u32[]{:S(2)}) collective-permute-start(bf16[2,32,512]{2,1,0:T(8,128)(2,1)S(1)} %pad_maximum_fusion.6), channel_id=1, source_target_pairs={{0,32},{16,48},{32,0},{48,16},{64,96},{80,112},{96,64},{112,80},{1... | collective-permute-start | bytes 196616 | tf_op jit(solution)/shard_map/ppermute | solution.py:547
  158.4 2.7 %collective-permute-start.20 = (bf16[2,32,512]{2,1,0:T(8,128)(2,1)S(1)}, bf16[2,32,512]{2,1,0:T(8,128)(2,1)S(1)}, u32[]{:S(2)}, u32[]{:S(2)}) collective-permute-start(bf16[2,32,512]{2,1,0:T(8,128)(2,1)S(1)} %pad_maximum_fusion.7), channel_id=1, source_target_pairs={{0,48},{16,0},{32,16},{48,32},{64,112},{80,64},{96,80},{112,96},{1... | collective-permute-start | bytes 196616 | tf_op jit(solution)/shard_map/ppermute | solution.py:547
  161.0 3.6 %weight_product.3 = f32[512,512]{1,0:T(8,128)S(1)} custom-call(s32[5]{0:T(128)S(1)} %copy-done.1, bf16[8,4,2,2,32,512]{5,4,3,2,1,0:T(8,128)(2,1)} %bitcast.22.rows, bf16[4,512,256]{2,1,0:T(8,128)(2,1)S(1)} %pad_maximum_fusion.2.near, bf16[4,512,256]{2,1,0:T(8,128)(2,1)S(1)} %collective-permute-done.15.far), custom_call_target="tpu_custom_call" | custom-call | flops 1 | bytes 1 | tf_op jit(solution)/shard_map/weight_product/pallas_call | solution.py:430
  164.7 2.5 %attend.1 = bf16[256,4096]{1,0:T(8,128)(2,1)} custom-call(s32[8]{0:T(128)S(1)} %copy-done.2, s32[5]{0:T(128)S(1)} %copy-done.1, bf16[8,256,128]{2,1,0:T(8,128)(2,1)S(1)} %copy-done, bf16[2,32,512]{2,1,0:T(8,128)(2,1)S(1)} %pad_maximum_fusion.4.rest_0_, bf16[2,32,512]{2,1,0:T(8,128)(2,1)S(1)} %collective-permute-done.18.rest_1_, ...), custom_call_target="tpu_custom_call" | custom-call | flops 1 | bytes 1 | tf_op jit(solution)/shard_map/attend/pallas_call | solution.py:394
  (67 shorter events, 11.7 us)
Async XLA Ops:
  0.6 24.3 %collective-permute-start.1 = (bf16[512,512]{1,0:T(8,128)(2,1)}, bf16[512,512]{1,0:T(8,128)(2,1)S(1)}, u32[]{:S(2)}, u32[]{:S(2)}) collective-permute-start(bf16[512,512]{1,0:T(8,128)(2,1)} %param.17), channel_id=1, source_target_pairs={{0,2},{1,3},{2,4},{3,5},{4,6},{5,7},{6,0},{7,1},{8,10},{9,11},{10,... | collective-permute-start | bytes 1572872 | tf_op jit(solution)/shard_map/ppermute | solution.py:458
  2.2 22.7 %collective-permute-start = (bf16[512,512]{1,0:T(8,128)(2,1)}, bf16[512,512]{1,0:T(8,128)(2,1)S(1)}, u32[]{:S(2)}, u32[]{:S(2)}) collective-permute-start(bf16[512,512]{1,0:T(8,128)(2,1)} %param.17), channel_id=1, source_target_pairs={{0,8},{1,9},{2,10},{3,11},{4,12},{5,13},{6,14},{7,15},{8,0},{9,1},... | collective-permute-start | bytes 1572872 | tf_op jit(solution)/shard_map/ppermute | solution.py:452
  3.8 21.1 %collective-permute-start.2 = (bf16[512,512]{1,0:T(8,128)(2,1)}, bf16[512,512]{1,0:T(8,128)(2,1)S(1)}, u32[]{:S(2)}, u32[]{:S(2)}) collective-permute-start(bf16[512,512]{1,0:T(8,128)(2,1)} %param.17), channel_id=1, source_target_pairs={{0,6},{1,7},{2,0},{3,1},{4,2},{5,3},{6,4},{7,5},{8,14},{9,15},{10,... | collective-permute-start | bytes 1572872 | tf_op jit(solution)/shard_map/ppermute | solution.py:458
  5.7 19.2 %all-to-all-start = ((f32[128,1,32]{2,1,0:T(1,128)}), f32[128,1,32]{2,1,0:T(1,128)S(1)}, u32[]{:S(2)}, u32[]{:S(2)}) async-start(f32[128,1,32]{2,1,0:T(1,128)} %bitcast.43), calls=%async_computation | async-start | bytes 131072 | tf_op jit(solution)/shard_map/all_to_all | solution.py:490
  25.5 53.8 %all-to-all-start.1 = ((bf16[8,512,512]{2,1,0:T(8,128)(2,1)}), bf16[8,512,512]{2,1,0:T(8,128)(2,1)}, u32[]{:S(2)}, u32[]{:S(2)}) async-start(bf16[8,512,512]{2,1,0:T(8,128)(2,1)} %bitcast.31), calls=%async_computation.1 | async-start | bytes 8388608 | tf_op jit(solution)/shard_map/all_to_all | solution.py:497
  30.1 17.1 %collective-permute-start.7 = (bf16[512,512]{1,0:T(8,128)(2,1)S(1)}, bf16[512,512]{1,0:T(8,128)(2,1)S(1)}, u32[]{:S(2)}, u32[]{:S(2)}) collective-permute-start(bf16[512,512]{1,0:T(8,128)(2,1)S(1)} %collective-permute-done), channel_id=1, source_target_pairs={{0,6},{1,7},{2,0},{3,1},{4,2},{5,3},{6,4},{7,5},{8,14},{9,15},{10,... | collective-permute-start | bytes 1572872 | tf_op jit(solution)/shard_map/ppermute | solution.py:458
  31.6 17.2 %collective-permute-start.5 = (bf16[512,512]{1,0:T(8,128)(2,1)S(1)}, bf16[512,512]{1,0:T(8,128)(2,1)S(1)}, u32[]{:S(2)}, u32[]{:S(2)}) collective-permute-start(bf16[512,512]{1,0:T(8,128)(2,1)S(1)} %collective-permute-done), channel_id=1, source_target_pairs={{0,2},{1,3},{2,4},{3,5},{4,6},{5,7},{6,0},{7,1},{8,10},{9,11},{10,... | collective-permute-start | bytes 1572872 | tf_op jit(solution)/shard_map/ppermute | solution.py:458
  32.2 18.1 %collective-permute-start.4 = (bf16[256,512]{1,0:T(8,128)(2,1)S(1)}, bf16[256,512]{1,0:T(8,128)(2,1)S(1)}, u32[]{:S(2)}, u32[]{:S(2)}) collective-permute-start(bf16[256,512]{1,0:T(8,128)(2,1)S(1)} %slice.19), channel_id=1, source_target_pairs={{0,6},{1,7},{2,0},{3,1},{4,2},{5,3},{6,4},{7,5},{8,14},{9,15},{10,... | collective-permute-start | bytes 786440 | tf_op jit(solution)/shard_map/ppermute | solution.py:458
  33.7 17.0 %collective-permute-start.3 = (bf16[256,512]{1,0:T(8,128)(2,1)S(1)}, bf16[256,512]{1,0:T(8,128)(2,1)}, u32[]{:S(2)}, u32[]{:S(2)}) collective-permute-start(bf16[256,512]{1,0:T(8,128)(2,1)S(1)} %slice.18), channel_id=1, source_target_pairs={{0,2},{1,3},{2,4},{3,5},{4,6},{5,7},{6,0},{7,1},{8,10},{9,11},{10,... | collective-permute-start | bytes 786440 | tf_op jit(solution)/shard_map/ppermute | solution.py:458
  47.1 4.6 %copy-start.7 = (bf16[512,512]{1,0:T(8,128)(2,1)S(1)}, bf16[512,512]{1,0:T(8,128)(2,1)}, u32[]{:S(2)}) copy-start(bf16[512,512]{1,0:T(8,128)(2,1)} %param.17) | copy-start | bytes 1572868
  47.2 7.9 %collective-permute-start.8 = (bf16[256,512]{1,0:T(8,128)(2,1)S(1)}, bf16[256,512]{1,0:T(8,128)(2,1)S(1)}, u32[]{:S(2)}, u32[]{:S(2)}) collective-permute-start(bf16[256,512]{1,0:T(8,128)(2,1)S(1)} %slice.25), channel_id=1, source_target_pairs={{0,6},{1,7},{2,0},{3,1},{4,2},{5,3},{6,4},{7,5},{8,14},{9,15},{10,... | collective-permute-start | bytes 786440 | tf_op jit(solution)/shard_map/ppermute | solution.py:458
  48.8 8.3 %collective-permute-start.6 = (bf16[256,512]{1,0:T(8,128)(2,1)S(1)}, bf16[256,512]{1,0:T(8,128)(2,1)S(1)}, u32[]{:S(2)}, u32[]{:S(2)}) collective-permute-start(bf16[256,512]{1,0:T(8,128)(2,1)S(1)} %slice.24), channel_id=1, source_target_pairs={{0,2},{1,3},{2,4},{3,5},{4,6},{5,7},{6,0},{7,1},{8,10},{9,11},{10,... | collective-permute-start | bytes 786440 | tf_op jit(solution)/shard_map/ppermute | solution.py:458
  52.0 5.4 %copy-start.3 = (bf16[4,512,512]{2,1,0:T(8,128)(2,1)}, bf16[4,512,512]{2,1,0:T(8,128)(2,1)S(1)}, u32[]{:S(2)}) copy-start(bf16[4,512,512]{2,1,0:T(8,128)(2,1)S(1)} %pad_maximum_fusion.rest_0_) | copy-start | bytes 6291460
  52.0 25.2 %collective-permute-start.9 = (bf16[4,512,512]{2,1,0:T(8,128)(2,1)S(1)}, bf16[4,512,512]{2,1,0:T(8,128)(2,1)S(1)}, u32[]{:S(2)}, u32[]{:S(2)}) collective-permute-start(bf16[4,512,512]{2,1,0:T(8,128)(2,1)S(1)} %pad_maximum_fusion.rest_0_), channel_id=1, source_target_pairs={{0,1},{1,0},{2,3},{3,2},{4,5},{5,4},{6,7},{7,6},{8,9},{9,8},{10,11... | collective-permute-start | bytes 6291464 | tf_op jit(solution)/shard_map/ppermute | solution.py:473
  57.4 19.8 %copy-start.4 = (bf16[4,512,512]{2,1,0:T(8,128)(2,1)}, bf16[4,512,512]{2,1,0:T(8,128)(2,1)S(1)}, u32[]{:S(2)}) copy-start(bf16[4,512,512]{2,1,0:T(8,128)(2,1)S(1)} %pad_maximum_fusion.1.rest_1_) | copy-start | bytes 6291460
  57.4 21.1 %collective-permute-start.10 = (bf16[4,512,512]{2,1,0:T(8,128)(2,1)S(1)}, bf16[4,512,512]{2,1,0:T(8,128)(2,1)}, u32[]{:S(2)}, u32[]{:S(2)}) collective-permute-start(bf16[4,512,512]{2,1,0:T(8,128)(2,1)S(1)} %pad_maximum_fusion.1.rest_1_), channel_id=1, source_target_pairs={{0,1},{1,0},{2,3},{3,2},{4,5},{5,4},{6,7},{7,6},{8,9},{9,8},{10,11... | collective-permute-start | bytes 6291464 | tf_op jit(solution)/shard_map/ppermute | solution.py:473
  58.1 8.6 %collective-permute-start.13 = (bf16[512,256]{1,0:T(8,128)(2,1)S(1)}, bf16[512,256]{1,0:T(8,128)(2,1)S(1)}, u32[]{:S(2)}, u32[]{:S(2)}) collective-permute-start(bf16[512,256]{1,0:T(8,128)(2,1)S(1)} %copy-done.9), channel_id=1, source_target_pairs={{0,6},{1,7},{2,0},{3,1},{4,2},{5,3},{6,4},{7,5},{8,14},{9,15},{10,... | collective-permute-start | bytes 786440 | tf_op jit(solution)/shard_map/ppermute | solution.py:458
  61.0 8.2 %collective-permute-start.11 = (bf16[512,256]{1,0:T(8,128)(2,1)S(1)}, bf16[512,256]{1,0:T(8,128)(2,1)S(1)}, u32[]{:S(2)}, u32[]{:S(2)}) collective-permute-start(bf16[512,256]{1,0:T(8,128)(2,1)S(1)} %copy-done.9), channel_id=1, source_target_pairs={{0,2},{1,3},{2,4},{3,5},{4,6},{5,7},{6,0},{7,1},{8,10},{9,11},{10,... | collective-permute-start | bytes 786440 | tf_op jit(solution)/shard_map/ppermute | solution.py:458
  66.7 5.1 %collective-permute-start.14 = (bf16[256,256]{1,0:T(8,128)(2,1)S(1)}, bf16[256,256]{1,0:T(8,128)(2,1)S(1)}, u32[]{:S(2)}, u32[]{:S(2)}) collective-permute-start(bf16[256,256]{1,0:T(8,128)(2,1)S(1)} %slice.27), channel_id=1, source_target_pairs={{0,6},{1,7},{2,0},{3,1},{4,2},{5,3},{6,4},{7,5},{8,14},{9,15},{10,... | collective-permute-start | bytes 393224 | tf_op jit(solution)/shard_map/ppermute | solution.py:458
  69.3 5.0 %collective-permute-start.12 = (bf16[256,256]{1,0:T(8,128)(2,1)S(1)}, bf16[256,256]{1,0:T(8,128)(2,1)S(1)}, u32[]{:S(2)}, u32[]{:S(2)}) collective-permute-start(bf16[256,256]{1,0:T(8,128)(2,1)S(1)} %slice.26), channel_id=1, source_target_pairs={{0,2},{1,3},{2,4},{3,5},{4,6},{5,7},{6,0},{7,1},{8,10},{9,11},{10,... | collective-permute-start | bytes 393224 | tf_op jit(solution)/shard_map/ppermute | solution.py:458
  74.5 2.7 %collective-permute-start.15 = (bf16[4,512,256]{2,1,0:T(8,128)(2,1)S(1)}, bf16[4,512,256]{2,1,0:T(8,128)(2,1)S(1)}, u32[]{:S(2)}, u32[]{:S(2)}) collective-permute-start(bf16[4,512,256]{2,1,0:T(8,128)(2,1)S(1)} %pad_maximum_fusion.2.near), channel_id=1, source_target_pairs={{0,1},{1,0},{2,3},{3,2},{4,5},{5,4},{6,7},{7,6},{8,9},{9,8},{10,11... | collective-permute-start | bytes 3145736 | tf_op jit(solution)/shard_map/ppermute | solution.py:473
  77.2 1.3 copy-start.5
  83.6 64.3 %all-to-all-start.2 = ((bf16[64,64,512]{2,1,0:T(8,128)(2,1)}), bf16[64,64,512]{2,1,0:T(8,128)(2,1)}, u32[]{:S(2)}, u32[]{:S(2)}) async-start(bf16[64,64,512]{2,1,0:T(8,128)(2,1)} %bitcast.29), calls=%async_computation.2 | async-start | bytes 8388608 | tf_op jit(solution)/shard_map/all_to_all | solution.py:526
  101.8 46.1 %collective-permute-start.16 = (bf16[4,32,512]{2,1,0:T(8,128)(2,1)S(1)}, bf16[4,32,512]{2,1,0:T(8,128)(2,1)S(1)}, u32[]{:S(2)}, u32[]{:S(2)}) collective-permute-start(bf16[4,32,512]{2,1,0:T(8,128)(2,1)S(1)} %constant_dynamic-slice_fusion.8), channel_id=1, source_target_pairs={{0,64},{16,80},{32,96},{48,112},{64,0},{80,16},{96,32},{112,48},{1... | collective-permute-start | bytes 393224 | tf_op jit(solution)/shard_map/ppermute | solution.py:538
  105.1 10.1 %copy-start.6 = (bf16[8,32,512]{2,1,0:T(8,128)(2,1)S(1)}, bf16[8,32,512]{2,1,0:T(8,128)(2,1)}, u32[]{:S(2)}) copy-start(bf16[8,32,512]{2,1,0:T(8,128)(2,1)} %values.1) | copy-start | bytes 786436
  105.1 42.8 %copy-start.1 = (s32[5]{0:T(128)S(1)}, s32[5]{0:T(128)}, u32[]{:S(2)}) copy-start(s32[5]{0:T(128)} %stack.88.me.where) | copy-start | bytes 64
  151.4 15.8 %collective-permute-start.17 = (bf16[512,512]{1,0:T(8,128)(2,1)S(1)}, bf16[512,512]{1,0:T(8,128)(2,1)S(1)}, u32[]{:S(2)}, u32[]{:S(2)}) collective-permute-start(bf16[512,512]{1,0:T(8,128)(2,1)S(1)} %weight_product.2), channel_id=1, source_target_pairs={{0,8},{1,9},{2,10},{3,11},{4,12},{5,13},{6,14},{7,15},{8,0},{9,1},... | collective-permute-start | bytes 1572872 | tf_op jit(solution)/shard_map/ppermute | solution.py:452
  154.5 10.2 %collective-permute-start.18 = (bf16[2,32,512]{2,1,0:T(8,128)(2,1)S(1)}, bf16[2,32,512]{2,1,0:T(8,128)(2,1)S(1)}, u32[]{:S(2)}, u32[]{:S(2)}) collective-permute-start(bf16[2,32,512]{2,1,0:T(8,128)(2,1)S(1)} %pad_maximum_fusion.5), channel_id=1, source_target_pairs={{0,16},{16,32},{32,48},{48,0},{64,80},{80,96},{96,112},{112,64},{1... | collective-permute-start | bytes 196616 | tf_op jit(solution)/shard_map/ppermute | solution.py:547
  154.6 10.1 %collective-permute-start.19 = (bf16[2,32,512]{2,1,0:T(8,128)(2,1)S(1)}, bf16[2,32,512]{2,1,0:T(8,128)(2,1)S(1)}, u32[]{:S(2)}, u32[]{:S(2)}) collective-permute-start(bf16[2,32,512]{2,1,0:T(8,128)(2,1)S(1)} %pad_maximum_fusion.6), channel_id=1, source_target_pairs={{0,32},{16,48},{32,0},{48,16},{64,96},{80,112},{96,64},{112,80},{1... | collective-permute-start | bytes 196616 | tf_op jit(solution)/shard_map/ppermute | solution.py:547
  158.3 6.3 %copy-start = (bf16[8,256,128]{2,1,0:T(8,128)(2,1)S(1)}, bf16[8,256,128]{2,1,0:T(8,128)(2,1)}, u32[]{:S(2)}) copy-start(bf16[8,256,128]{2,1,0:T(8,128)(2,1)} %get-tuple-element.69.probs) | copy-start | bytes 1572868
  158.3 6.3 %copy-start.2 = (s32[8]{0:T(128)S(1)}, s32[8]{0:T(128)}, u32[]{:S(2)}) copy-start(s32[8]{0:T(128)} %get-tuple-element.46.colours) | copy-start | bytes 100
  158.4 6.3 %collective-permute-start.20 = (bf16[2,32,512]{2,1,0:T(8,128)(2,1)S(1)}, bf16[2,32,512]{2,1,0:T(8,128)(2,1)S(1)}, u32[]{:S(2)}, u32[]{:S(2)}) collective-permute-start(bf16[2,32,512]{2,1,0:T(8,128)(2,1)S(1)} %pad_maximum_fusion.7), channel_id=1, source_target_pairs={{0,48},{16,0},{32,16},{48,32},{64,112},{80,64},{96,80},{112,96},{1... | collective-permute-start | bytes 196616 | tf_op jit(solution)/shard_map/ppermute | solution.py:547
  (2 other events, 1.6 us)
